TPU v7x, 512 devices: a whole 4x8x8 slice. The times are simulated.
512 devices in a mesh: ctx: 64 (over x, y, core), tp: 8 (over z).
Axes of the slice: x: 4, y: 8, z: 8, core: 2. Of those that a mesh axis runs over, the one named last changes fastest.
Arguments:
- queries: bfloat16 [8, 64, 8192], P(None, 'ctx', 'tp'), may hold values from -16 to 16
- node_kv: bfloat16 [8, 64, 2048], P(None, 'ctx', 'tp'), may hold values from -6 to 6
- key_value_pool: bfloat16 [4608, 64, 2048], P('ctx', None, 'tp'), may hold values from -6 to 6
- out_weight: bfloat16 [8192, 8192], P('tp', 'ctx'), may hold values from -0.0625 to 0.0625
- parents: int32 [8, 64], replicated, may hold values from -1 to 62, as said below
- accepted_path: int32 [8, 8], replicated, may hold values from 0 to 62, as said below
- accept_count: int32 [8], replicated, may hold values from 1 to 8
- lengths: int32 [8], replicated, may hold values from 4096 to 32760, as said below
- page_table: int32 [8, 512], P(None, 'ctx'), may hold values from 0 to 71, as said below
- free_slot: int32 [8, 64], P(None, 'ctx'), may hold values from 0 to 71, as said below
Outputs:
- projected: float32 [8, 64, 8192], P(None, 'tp', 'ctx')
- updated_pool: bfloat16 [4608, 64, 2048], P('ctx', None, 'tp')
- new_page_table: int32 [8, 512], P(None, 'ctx')
Inputs may be any that keep to these rules, and one draw needn't show every extreme that they name: parents[r, 0] = -1, and every other node's parent has a smaller index than the node. accepted_path[r, 0] = 0 and accepted_path[r, j] is the parent of accepted_path[r, j + 1]. Requests 2k and 2k + 1 that share pages have equal lengths. page_table[r, p] is a slot of the pool of ctx index p div 8. Entries are distinct except that request 2k + 1 may share its pages 0 to lengths[2k] div 64 with request 2k; no page after a request's tail page is shared. free_slot[r, c] is a slot of ctx index c that no entry of page_table names; distinct over r.
All inputs are finite; a program needn't handle non-finite values.
Results may differ from a plain program's by a relative error of at most 0.0027.
Values may be sent and summed in bfloat16 or wider, within the bound.
No kernel may reach another device: no remote copies, remote signals or barrier semaphores. Data moves between devices by JAX's collectives and lax.ppermute only.
A program may use at most 64 MiB of HBM per device.

v0:
```python
import jax
import jax.numpy as jnp
from jax import lax
from jax.sharding import PartitionSpec as P

HEAD_WIDTH = 128
PATH_ROWS = 8


masked_score = -1e30


def ancestry(parents):
    node_count = parents.shape[-1]
    node_ids = jnp.arange(node_count, dtype=jnp.int32)
    reached = (parents[:, :, None] == node_ids[None, None, :]).astype(jnp.float32)
    reached = reached + jnp.eye(node_count, dtype=jnp.float32)[None]
    for squaring in range(max(1, (node_count - 1).bit_length())):
        reached = jnp.minimum(
            jnp.einsum("rij,rjk->rik", reached, reached, precision=lax.Precision.HIGHEST), 1.0
        )
    return reached


def soft_partial(scores, live_mask, value_rows):
    row_max = jnp.max(jnp.where(live_mask, scores, masked_score), axis=-1)
    shifted = jnp.where(live_mask, scores, row_max[..., None]) - row_max[..., None]
    weights = jnp.where(live_mask, jnp.exp(shifted), 0.0)
    row_sum = jnp.sum(weights, axis=-1)
    weighted = jnp.einsum(
        "nkgt,tkd->nkgd", weights, value_rows.astype(jnp.float32), precision=lax.Precision.HIGHEST
    )
    return (row_max, row_sum, weighted)


def join_partials(earlier, later):
    row_max = jnp.maximum(earlier[0], later[0])
    scale_early = jnp.exp(earlier[0] - row_max)
    scale_late = jnp.exp(later[0] - row_max)
    return (
        row_max,
        scale_early * earlier[1] + scale_late * later[1],
        scale_early[..., None] * earlier[2] + scale_late[..., None] * later[2],
    )


def on_device(
    queries,
    node_kv,
    key_value_pool,
    out_weight,
    parents,
    accepted_path,
    accept_count,
    lengths,
    page_table,
    free_slot,
):
    ctx_index = lax.axis_index("ctx")
    requests, node_local, width_q = queries.shape
    kv_width = node_kv.shape[2]
    kv_local = kv_width // (2 * HEAD_WIDTH)
    query_group_width = width_q // (kv_local * HEAD_WIDTH)
    head_local = kv_local * query_group_width
    pool_local = key_value_pool.shape[0]
    page_rows = key_value_pool.shape[1]
    pages_local = page_table.shape[1]
    span_rows = pages_local * page_rows
    score_scale = HEAD_WIDTH ** (-0.5)
    first_node = ctx_index * node_local
    start_pos = ctx_index * span_rows
    tree_mask = ancestry(parents)
    local_mask = lax.dynamic_slice_in_dim(tree_mask, first_node, node_local, 2)
    every_query = lax.all_gather(queries, "ctx", axis=1, tiled=True)
    node_count = every_query.shape[1]
    query_heads = every_query.reshape(requests, node_count, kv_local, query_group_width, HEAD_WIDTH)
    cache_rows = key_value_pool[page_table].reshape(requests, span_rows, kv_local, 2, HEAD_WIDTH)
    tree_rows = node_kv.reshape(requests, node_local, kv_local, 2, HEAD_WIDTH)
    cache_live = (start_pos + jnp.arange(span_rows, dtype=jnp.int32))[None, :] < lengths[:, None]

    def cache_part(query_per_request, cache_per_request, live_r):
        scores = (
            jnp.einsum(
                "nkgd,tkd->nkgt",
                query_per_request,
                cache_per_request[:, :, 0],
                preferred_element_type=jnp.float32,
            )
            * score_scale
        )
        return soft_partial(scores, live_r[None, None, None, :], cache_per_request[:, :, 1])

    def attend(per_request):
        query_per_request, cache_per_request, tree_r, live_r, mask_r, length_r = per_request
        tree_scores = (
            jnp.einsum(
                "nkgd,jkd->nkgj",
                query_per_request,
                tree_r[:, :, 0],
                preferred_element_type=jnp.float32,
            )
            * score_scale
        )
        tree_partial = soft_partial(tree_scores, (mask_r > 0.5)[:, None, None, :], tree_r[:, :, 1])
        cache_partial = cache_part(query_per_request, cache_per_request, live_r)
        return join_partials(cache_partial, tree_partial)

    row_max, row_sum, weighted = lax.map(
        attend, (query_heads, cache_rows, tree_rows, cache_live, local_mask, lengths)
    )
    row_max = row_max.reshape(requests, node_count, head_local)
    row_sum = row_sum.reshape(requests, node_count, head_local)
    weighted = weighted.reshape(requests, node_count, head_local, HEAD_WIDTH)
    peak = lax.pmax(row_max, "ctx")
    factor = jnp.exp(row_max - peak)
    totals = lax.psum((factor * row_sum, factor[..., None] * weighted), "ctx")
    attention = (totals[1] / totals[0][..., None]).astype(jnp.bfloat16)
    partial_out = jnp.einsum(
        "rnf,fe->rne",
        attention.reshape(requests, node_count, head_local * HEAD_WIDTH),
        out_weight,
        preferred_element_type=jnp.float32,
    )
    projected = lax.psum_scatter(partial_out, "tp", scatter_dimension=1, tiled=True)
    every_node = lax.all_gather(node_kv, "ctx", axis=1, tiled=True)
    written_pool = jnp.take_along_axis(every_node, accepted_path[:, :, None], axis=1)
    slot_ids = jnp.arange(pool_local, dtype=jnp.int32)
    ref_count = jnp.sum(
        (page_table.reshape(-1)[:, None] == slot_ids[None, :]).astype(jnp.int32), axis=0
    )
    tail_local = lengths - start_pos
    tail_here = (tail_local >= 0) & (tail_local < span_rows)
    tail_page = jnp.clip(tail_local // page_rows, 0, pages_local - 1)
    tail_slot = jnp.take_along_axis(page_table, tail_page[:, None], axis=1)[:, 0]
    shared = tail_here & (ref_count[tail_slot] > 1)
    spare_slot = free_slot[:, 0]
    copy_target = jnp.where(shared, spare_slot, pool_local)
    updated_pool = key_value_pool.at[copy_target].set(key_value_pool[tail_slot], mode="drop")
    page_hot = jnp.arange(pages_local, dtype=jnp.int32)[None, :] == tail_page[:, None]
    new_table = jnp.where(shared[:, None] & page_hot, spare_slot[:, None], page_table)
    offsets = jnp.arange(PATH_ROWS, dtype=jnp.int32)
    row_pos = lengths[:, None] + offsets[None, :] - start_pos
    row_here = (offsets[None, :] < accept_count[:, None]) & (row_pos >= 0) & (row_pos < span_rows)
    row_page = jnp.clip(row_pos // page_rows, 0, pages_local - 1)
    row_pool_slot = jnp.where(
        row_here, jnp.take_along_axis(new_table, row_page, axis=1), pool_local
    )
    row_within_page = row_pos % page_rows
    updated_pool = updated_pool.at[row_pool_slot.reshape(-1), row_within_page.reshape(-1)].set(
        written_pool.reshape(-1, kv_width), mode="drop"
    )
    return (projected, updated_pool, new_table)


def solution(mesh):
    placed = (
        P(None, "ctx", "tp"),
        P(None, "ctx", "tp"),
        P("ctx", None, "tp"),
        P("tp", "ctx"),
        P(),
        P(),
        P(),
        P(),
        P(None, "ctx"),
        P(None, "ctx"),
    )
    return jax.shard_map(
        on_device,
        mesh=mesh,
        in_specs=placed,
        out_specs=(P(None, "tp", "ctx"), P("ctx", None, "tp"), P(None, "ctx")),
        check_vma=False,
    )
```

profile of v0, /device:TPU:1, one launch (start us, length us, event | category | flops | bytes accessed | tf_op | source)
XLA Modules:
  0.0 694.1 jit_solution(2269102967953059014)
XLA Ops:
  7.3 1.7 copy.85
  13.6 2.0 gather_fusion
  15.6 4.0 reshape.531
  19.7 79.2 %all-gather.2.cloned.1.call-done = bf16[8,64,1024]{2,0,1:T(8,128)(2,1)} async-done(((bf16[8,1,1024]{2,0,1:T(8,128)(2,1)}), bf16[8,64,1024]{2,0,1:T(8,128)(2,1)}) %all-gather.2.cloned.1.call-update) | async-done | bytes 1048592 | tf_op jit(solution)/shard_map/all_gather | solution.py:74
  98.9 2.5 copy.58
  101.4 37.6 %while.14 = (s32[]{:T(128)}, f32[8,64,1,8]{1,3,2,0:T(8,128)S(1)}, f32[8,64,1,8]{1,3,2,0:T(8,128)S(1)}, f32[8,64,1,8,128]{4,1,3,2,0:T(8,128)}, pred[8,512]{1,0:T(...) while((s32[]{:T(128)}, f32[8,64,1,8]{1,3,2,0:T(8,128)S(1)}, ...), condition=%wide.region_3.4_spmd, body=%wide.region_0.3_spmd.sunk | while | flops 472781504 | bytes 5306569 | solution.py:108
  102.6 1.2 constant_dynamic-slice_fusion.7
  104.5 1.5 fusion.66
  107.3 1.2 constant_dynamic-slice_fusion.7
  109.2 1.5 fusion.66
  113.9 1.5 fusion.66
  118.6 1.5 fusion.66
  123.3 1.5 fusion.66
  128.0 1.5 fusion.66
  130.7 1.2 constant_dynamic-slice_fusion.7
  132.7 1.5 fusion.66
  137.4 1.5 fusion.66
  139.0 243.2 %pmax.7 = f32[8,64,8]{1,2,0:T(8,128)S(1)} all-reduce(f32[8,64,8]{1,2,0:T(8,128)S(1)} %bitcast.170), channel_id=1, replica_groups=mesh['ctx'=64,'tp'=8] {'ctx'}, use_global_device_ids=true, to_apply=%region_4.5 | all-reduce | flops 4096 | bytes 32768 | tf_op jit(solution)/shard_map/pmax | solution.py:114
  382.2 3.5 bitcast_multiply_fusion.1
  386.4 246.2 %psum.15 = f32[8,64,8]{1,2,0:T(8,128)S(1)} all-reduce(f32[8,64,8]{1,2,0:T(8,128)S(1)} %get-tuple-element.108), channel_id=1, replica_groups=mesh['ctx'=64,'tp'=8] {'ctx'}, use_global_device_ids=true, to_apply=%region_6.7 | all-reduce | flops 4096 | bytes 32768 | tf_op jit(solution)/shard_map/psum | solution.py:116
  632.6 3.1 fusion.17
  637.1 42.5 %all_gather.7 = bf16[8,64,256]{2,0,1:T(8,128)(2,1)S(1)} all-gather(bf16[8,1,256]{2,0,1:T(8,128)(2,1)S(1)} %copy-done.4), channel_id=1, replica_groups=mesh['ctx'=64,'tp'=8] {'ctx'}, dimensions={1}, use_global_device_ids=true | all-gather | bytes 266240 | tf_op jit(solution)/shard_map/all_gather | solution.py:125
  682.1 4.0 scatter_fusion.1
  686.2 1.4 copy-done.3
  (163 shorter events, 30.5 us)
Async XLA Ops:
  7.2 625.5 %copy-start = (bf16[1024,128]{1,0:T(8,128)(2,1)S(1)}, bf16[1024,128]{1,0:T(8,128)(2,1)}, u32[]{:S(2)}) copy-start(bf16[1024,128]{1,0:T(8,128)(2,1)} %param.15) | copy-start | bytes 786436
  7.2 3.6 copy-start.4
  7.2 3.7 copy-start.7
  7.2 2.0 copy-start.6
  7.2 1.8 copy-start.2
  7.2 3.4 copy-start.8
  7.2 91.7 %all-gather.2.cloned.1.call-start = ((), (), s32[]{:S(2)}) async-start(), calls=%async_computation.1 | async-start | bytes 1064960 | tf_op jit(solution)/shard_map/all_gather | solution.py:74
  9.0 623.6 %all-reduce.2.cloned.1.call-start = ((), (), s32[]{:S(2)}) async-start(), calls=%async_computation.2 | async-start | bytes 4194304 | tf_op jit(solution)/shard_map/psum | solution.py:116
  10.7 668.9 %copy-start.1 = (s32[8,8]{1,0:T(8,128)}, s32[8,8]{1,0:T(8,128)S(1)}, u32[]{:S(2)}) copy-start(s32[8,8]{1,0:T(8,128)S(1)} %get-tuple-element.113) | copy-start | bytes 772
  385.7 0.7 copy-start.5
  385.7 300.4 %reduce-scatter.2.cloned.1.call-start = ((), (), s32[]{:S(2)}) async-start(), calls=%async_computation.3 | async-start | bytes 294912 | tf_op jit(solution)/shard_map/reduce_scatter | solution.py:124
  632.6 3.9 copy-start.9
  686.1 1.4 copy-start.3
Sparse Core Ops, SparseCore 0:
  11.4 87.4 all-gather.1
  385.8 197.6 all-reduce.1
  635.8 33.7 reduce-scatter.1
where the time goes:
time: 695 us; the launch traced here: 694 us
  blocking collectives  532 us (77%)
  waiting for transfers between devices  79.3 us (11%)
  local copies, waits for them, and re-layouts  38.6 us (6%)
  matrix products  22.3 us (3%)
  between operations  14 us (2%)
  other arithmetic  7.36 us (1%)
    psum x1, blocking collectives, on_device(): totals = lax.psum((factor * row_sum, factor[..., None] * weighted), 'ctx')  246 us
    pmax x1, blocking collectives, on_device(): peak = lax.pmax(row_max, 'ctx')  243 us
    all_gather x1, waiting for transfers between devices, on_device(): every_query = lax.all_gather(queries, 'ctx', axis=1, tiled=True)  79.2 us
    all_gather x1, blocking collectives, on_device(): every_node = lax.all_gather(node_kv, 'ctx', axis=1, tiled=True)  42.5 us
    dynamic_slice x32, local copies, waits for them, and re-layouts, on_device(): lax.map(attend, (query_heads, cache_rows, tree_rows, cache_live, local_ma...  17.2 us
  transfers between devices with their start and end apart: 3, of which 1 were waited for; matrix products, arithmetic and copies ran while one was open for 3% of the time, Pallas kernels for 0%

commit v1 on v0

v1 whole, which is shorter than its diff:
```python
import jax
import jax.numpy as jnp
from jax import lax
from jax.experimental import pallas as pl
from jax.experimental.pallas import tpu as pltpu
from jax.sharding import Mesh, PartitionSpec as P

F32 = jnp.float32
BF16 = jnp.bfloat16

HEAD = 128
PATH_ROWS = 8
PAGE = 64
REQUESTS = 8
HALF = 4
NODES = 64
PAGES_LOCAL = 8
SPAN = PAGE * PAGES_LOCAL
LANES = 8 * NODES
CHIPS = 32
TAIL = 8
BLOCK = 64 + TAIL
DEAD = -1e30
FLOOR = -1e28
LOG2E = 1.4426950408889634
SCALE2 = HEAD ** (-0.5) * LOG2E

W_ROWS = 512
PAGE_ROWS0 = W_ROWS
NODE_ROWS0 = W_ROWS + HALF * SPAN
SEND_ROWS = NODE_ROWS0 + 16

VMEM = pltpu.VMEM
SMEM = pltpu.SMEM
LIMIT = 40 * 1024 * 1024


def iota(shape, dim):
    return lax.broadcasted_iota(jnp.int32, shape, dim)


def dot(a, b, ca=1, cb=0):
    return lax.dot_general(a, b, (((ca,), (cb,)), ((), ())), preferred_element_type=F32)


def ctx_index():
    return (lax.axis_index("x") * 8 + lax.axis_index("y")) * 2 + lax.axis_index("core")


def pack_kernel(where, table, pool, weight, node, parents, send, mask, node_pad, sems):
    core = where[0]
    ctx = where[1]
    other = HALF * (1 - core)
    copies = []
    for r in range(HALF):
        for p in range(PAGES_LOCAL):
            n = r * PAGES_LOCAL + p
            copies.append(
                pltpu.make_async_copy(
                    pool.at[table[other + r, p]],
                    send.at[pl.ds(PAGE_ROWS0 + n * PAGE, PAGE), :],
                    sems.at[n],
                )
            )
    for half in range(2):
        copies.append(
            pltpu.make_async_copy(
                weight.at[pl.ds(half * W_ROWS, W_ROWS), :],
                send.at[pl.ds(0, W_ROWS), pl.ds(half * HEAD, HEAD)],
                sems.at[32 + half],
            )
        )
    for c in copies:
        c.start()
    rows = node[...].astype(F32)
    node_pad[...] = jnp.concatenate([rows, jnp.zeros_like(rows)], axis=0).astype(BF16)
    last = pltpu.make_async_copy(node_pad, send.at[pl.ds(NODE_ROWS0, 16), :], sems.at[34])
    last.start()
    up = iota((NODES, NODES), 0)
    down = iota((NODES, NODES), 1)
    twice = (iota((NODES, 2 * NODES), 0) == iota((NODES, 2 * NODES), 1) % NODES).astype(F32).astype(BF16)
    pick_row = iota((16, NODES), 0)
    pick_node = iota((16, NODES), 1)
    for r in range(HALF):
        mine = HALF * core + r
        link = parents[pl.ds(mine, 1), :]
        reach = ((up == link) | (up == down)).astype(F32).astype(BF16)
        for _ in range(6):
            reach = jnp.minimum(dot(reach, reach), 1.0).astype(BF16)
        pick = ((pick_row == mine) & (pick_node == ctx)) | (
            (pick_row == REQUESTS + mine) & (pick_node == ctx + 1 - 2 * core)
        )
        seen = dot(pick.astype(F32).astype(BF16), reach).astype(BF16)
        mask[r] = dot(seen, twice)
    for c in copies:
        c.wait()
    last.wait()


def attend_kernel(where, table, lengths, pool, queries, peer, node, mask, out, own, sems):
    core = where[0]
    ctx = where[1]
    mine = HALF * core
    copies = []
    for r in range(HALF):
        for p in range(PAGES_LOCAL):
            n = r * PAGES_LOCAL + p
            copies.append(
                pltpu.make_async_copy(
                    pool.at[table[mine + r, p]],
                    own.at[pl.ds(n * PAGE, PAGE), :],
                    sems.at[n],
                )
            )
    for c in copies:
        c.start()
    lane = iota((LANES, LANES), 1)
    order = (iota((LANES, LANES), 0) == (lane % NODES) * 8 + lane // NODES).astype(F32).astype(BF16)
    peer_node = peer[pl.ds(NODE_ROWS0, 16), :].astype(F32)[:REQUESTS]
    own_node = node[...].astype(F32)
    nodes = jnp.concatenate([own_node, peer_node], axis=0).astype(BF16)
    ones = jnp.ones((16, SPAN), BF16)
    ones_tree = jnp.ones((16, 16), BF16)
    row = iota((SPAN, LANES), 0)
    tail_row = iota((TAIL, HEAD), 0)
    for c in copies:
        c.wait()
    for r in range(HALF):
        part = queries[:, pl.ds((r // 2) * 16, 16), :].astype(F32)[:, (r % 2) * 8 : (r % 2) * 8 + 8, :]
        part = part.reshape(LANES, HEAD).astype(BF16)
        query = dot(part, order, 0, 0).astype(BF16)
        length = lengths[mine + r]
        span_own = own[pl.ds(r * SPAN, SPAN), :]
        span_peer = peer[pl.ds(PAGE_ROWS0 + r * SPAN, SPAN), :]
        live_own = row < length - ctx * SPAN
        live_peer = row < length - (ctx + 1 - 2 * core) * SPAN
        seen = jnp.concatenate([mask[r]] * 4, axis=1)
        s_own = jnp.where(live_own, dot(span_own[:, :HEAD], query), DEAD)
        s_peer = jnp.where(live_peer, dot(span_peer[:, :HEAD], query), DEAD)
        s_tree = jnp.where(seen > 0.5, dot(nodes[:, :HEAD], query), DEAD)
        peak = jnp.maximum(
            jnp.maximum(jnp.max(s_own, axis=0, keepdims=True), jnp.max(s_peer, axis=0, keepdims=True)),
            jnp.max(s_tree, axis=0, keepdims=True),
        )
        peak = jnp.maximum(peak, FLOOR) * SCALE2
        total = None
        for s, v, one in (
            (s_own, span_own[:, HEAD:], ones),
            (s_peer, span_peer[:, HEAD:], ones),
            (s_tree, nodes[:, HEAD:], ones_tree),
        ):
            p = jnp.exp2(s * SCALE2 - peak).astype(BF16)
            lhs = jnp.concatenate([v.astype(F32).T.astype(BF16), one], axis=0)
            add = dot(lhs, p)
            total = add if total is None else total + add
        row_sum = total[HEAD : HEAD + 1]
        some = row_sum > 0.0
        mixed = total[:HEAD] * (1.0 / jnp.where(some, row_sum, 1.0))
        log_sum = jnp.where(some, peak + jnp.log2(jnp.where(some, row_sum, 1.0)), DEAD)
        first = log_sum.astype(BF16).astype(F32)
        rest = log_sum - first
        second = rest.astype(BF16).astype(F32)
        third = rest - second
        for pair in range(4):
            lanes = slice(pair * HEAD, (pair + 1) * HEAD)
            for half in range(2):
                e = r * 8 + pair * 2 + half
                q = e // 4
                terms = (
                    first[:, lanes],
                    second[:, lanes],
                    third[:, lanes],
                    own_node[q : q + 1, :HEAD],
                    own_node[q : q + 1, HEAD:],
                    peer_node[q : q + 1, :HEAD],
                    peer_node[q : q + 1, HEAD:],
                )
                tail = jnp.zeros((TAIL, HEAD), F32)
                for t, term in enumerate(terms):
                    tail = jnp.where(tail_row == t, term, tail)
                block = jnp.concatenate([mixed[half * 64 : half * 64 + 64, lanes], tail], axis=0)
                out[e] = block.astype(BF16)


def combine_kernel(where, path, got, out):
    core = where[0]
    chip = where[1] // 2
    logs = []
    for s in range(CHIPS):
        tail = got[s].astype(F32)[64:BLOCK]
        logs.append(tail[0:1] + tail[1:2] + tail[2:3])
    peak = logs[0]
    for s in range(1, CHIPS):
        peak = jnp.maximum(peak, logs[s])
    total = jnp.zeros((1, HEAD), F32)
    mixed = jnp.zeros((64, HEAD), F32)
    for s in range(CHIPS):
        share = jnp.exp2(logs[s] - peak)
        total = total + share
        mixed = mixed + share * got[s].astype(F32)[:64]
    mixed = mixed * (1.0 / total)
    tail_row = iota((TAIL, HEAD), 0)
    tail = jnp.zeros((TAIL, HEAD), F32)
    for j in range(2):
        node = path[chip // 4, 2 * (chip % 4) + j]
        held = got[node // 2].astype(F32)[64:BLOCK]
        is_own = node % 2 == core
        key = jnp.where(is_own, held[3:4], held[5:6])
        value = jnp.where(is_own, held[4:5], held[6:7])
        tail = jnp.where(tail_row == 2 * j, key, tail)
        tail = jnp.where(tail_row == 2 * j + 1, value, tail)
    block = jnp.concatenate([mixed, tail], axis=0).astype(BF16)
    for s in range(CHIPS):
        out[s] = block


def project_kernel(where, got, weight, peer, out):
    core = where[0]
    own_w = weight[...]
    peer_w = peer[...]
    sides = []
    for h in range(2):
        own_h = jnp.concatenate([own_w[(2 * p + h) * HEAD : (2 * p + h + 1) * HEAD] for p in range(4)], axis=0)
        peer_h = []
        for p in range(4):
            at = (2 * p + h) * HEAD
            cols = slice((at // W_ROWS) * HEAD, (at // W_ROWS) * HEAD + HEAD)
            peer_h.append(peer_w[at % W_ROWS : at % W_ROWS + HEAD, cols])
        sides.append(jnp.concatenate([own_h, jnp.concatenate(peer_h, axis=0)], axis=1))
    for r in range(HALF):
        a = got[pl.ds(r * 8, 8)][:, :64, :].reshape(W_ROWS, HEAD)
        even = dot(a, sides[0], 0, 0)
        odd = dot(a, sides[1], 0, 0)
        sums = even[:NODES] + odd[NODES:]
        for t in range(8):
            out[core * 8 + t, r] = sums[t * 8 : t * 8 + 8, :HEAD]
            out[(1 - core) * 8 + t, r] = sums[t * 8 : t * 8 + 8, HEAD:]


def write_kernel(where, table, lengths, counts, spare, table_v, got, pool_in, pool, new_table, pages, sems):
    ctx = where[1]
    for r in range(REQUESTS):
        for p in range(PAGES_LOCAL):
            new_table[r, p] = table[r, p]
    row = iota((PAGE, 2 * HEAD), 0)
    for r in range(REQUESTS):
        length = lengths[r]
        count = counts[r]
        tail_page = length // PAGE
        for step in range(2):
            page = tail_page + step
            local = page - ctx * PAGES_LOCAL
            first = length - page * PAGE
            here = (local >= 0) & (local < PAGES_LOCAL)
            if step == 1:
                here = here & (first + count > 0)

            @pl.when(here)
            def _():
                slot = table[r, local]
                target = slot
                if step == 0:
                    uses = jnp.sum((table_v[...] == slot).astype(jnp.int32))
                    target = jnp.where(uses > 1, spare[r, 0], slot)
                    new_table[r, local] = target
                fetch = pltpu.make_async_copy(pool_in.at[slot], pages.at[2 * r + step], sems.at[2 * r + step])
                fetch.start()
                fetch.wait()
                now = pages[2 * r + step].astype(F32)
                for j in range(PATH_ROWS):
                    held = got[r * 4 + j // 2].astype(F32)[64:BLOCK]
                    new = jnp.concatenate([held[2 * (j % 2) : 2 * (j % 2) + 1], held[2 * (j % 2) + 1 : 2 * (j % 2) + 2]], axis=1)
                    now = jnp.where((row == first + j) & (j < count), new, now)
                pages[2 * r + step] = now.astype(BF16)
                store = pltpu.make_async_copy(pages.at[2 * r + step], pool.at[target], sems.at[2 * r + step])
                store.start()
                store.wait()


def spec(space):
    return pl.BlockSpec(memory_space=space)


def on_device(queries, node_kv, pool, out_weight, parents, path, counts, lengths, table, free_slot):
    params = pltpu.CompilerParams(vmem_limit_bytes=LIMIT)
    any_ = spec(pl.ANY)
    core = lax.axis_index("core")
    where = jnp.stack([core, ctx_index()]).astype(jnp.int32)
    node = node_kv.reshape(REQUESTS, 2 * HEAD)

    send, mask = pl.pallas_call(
        pack_kernel,
        out_shape=(
            jax.ShapeDtypeStruct((SEND_ROWS, 2 * HEAD), BF16),
            jax.ShapeDtypeStruct((HALF, 16, 2 * NODES), F32),
        ),
        in_specs=[spec(SMEM), spec(SMEM), any_, any_, spec(VMEM), spec(VMEM)],
        out_specs=(any_, spec(VMEM)),
        scratch_shapes=[VMEM((16, 2 * HEAD), BF16), pltpu.SemaphoreType.DMA((35,))],
        compiler_params=params,
        name="pack",
    )(where, table, pool, out_weight, node, parents)
    peer = lax.ppermute(send, "core", [(0, 1), (1, 0)])

    by_core = queries.reshape(2, HALF * 8, HEAD)
    message = jnp.broadcast_to(by_core[None], (CHIPS, 2, HALF * 8, HEAD)).reshape(2 * CHIPS, HALF * 8, HEAD)
    every_query = lax.all_to_all(message, ("x", "y", "core"), 0, 0, tiled=True)

    partial = pl.pallas_call(
        attend_kernel,
        out_shape=jax.ShapeDtypeStruct((CHIPS, BLOCK, HEAD), BF16),
        in_specs=[spec(SMEM), spec(SMEM), spec(SMEM), any_, spec(VMEM), spec(VMEM), spec(VMEM), spec(VMEM)],
        out_specs=spec(VMEM),
        scratch_shapes=[VMEM((HALF * SPAN, 2 * HEAD), BF16), pltpu.SemaphoreType.DMA((32,))],
        compiler_params=params,
        name="attend",
    )(where, table, lengths, pool, every_query, peer, node, mask)

    parts = lax.all_to_all(partial, ("x", "y"), 0, 0, tiled=True)
    mixed = pl.pallas_call(
        combine_kernel,
        out_shape=jax.ShapeDtypeStruct((CHIPS, BLOCK, HEAD), BF16),
        in_specs=[spec(SMEM), spec(SMEM), spec(VMEM)],
        out_specs=spec(VMEM),
        compiler_params=params,
        name="combine",
    )(where, path, parts)
    attention = lax.all_to_all(mixed, ("x", "y"), 0, 0, tiled=True)

    sums = pl.pallas_call(
        project_kernel,
        grid=(1,),
        out_shape=jax.ShapeDtypeStruct((16, HALF, 8, HEAD), F32),
        in_specs=[
            spec(SMEM),
            pl.BlockSpec((CHIPS, BLOCK, HEAD), lambda i: (0, 0, 0)),
            pl.BlockSpec((8 * HEAD, HEAD), lambda i: (0, 0)),
            pl.BlockSpec((W_ROWS, 2 * HEAD), lambda i: (0, 0)),
        ],
        out_specs=pl.BlockSpec((16, HALF, 8, HEAD), lambda i: (0, 0, 0, 0)),
        compiler_params=params,
        name="project",
    )(where, attention, out_weight, peer)
    shares = lax.all_to_all(sums, ("core", "tp"), 0, 0, tiled=True)
    projected = jnp.sum(shares.reshape(2, 8, HALF, 8, HEAD), axis=1).reshape(REQUESTS, 8, HEAD)

    updated_pool, new_table = pl.pallas_call(
        write_kernel,
        out_shape=(
            jax.ShapeDtypeStruct(pool.shape, pool.dtype),
            jax.ShapeDtypeStruct(table.shape, table.dtype),
        ),
        in_specs=[spec(SMEM)] * 5 + [spec(VMEM), spec(VMEM), any_],
        out_specs=(any_, spec(SMEM)),
        input_output_aliases={7: 0},
        scratch_shapes=[VMEM((2 * REQUESTS, PAGE, 2 * HEAD), BF16), pltpu.SemaphoreType.DMA((2 * REQUESTS,))],
        compiler_params=params,
        name="write",
    )(where, table, lengths, counts, free_slot, table, attention, pool)
    return projected, updated_pool, new_table


def solution(mesh):
    fine = Mesh(mesh.devices.reshape(4, 8, 2, 8), ("x", "y", "core", "tp"))
    ctx = ("x", "y", "core")
    placed = (
        P(None, ctx, "tp"),
        P(None, ctx, "tp"),
        P(ctx, None, "tp"),
        P("tp", ctx),
        P(),
        P(),
        P(),
        P(),
        P(None, ctx),
        P(None, ctx),
    )
    return jax.shard_map(
        on_device,
        mesh=fine,
        in_specs=placed,
        out_specs=(P(None, "tp", ctx), P(ctx, None, "tp"), P(None, ctx)),
        check_vma=False,
    )
```

time: 695 us -> 118 us (0.17)
  blocking collectives: 532 us -> 65.1 us
  waiting for transfers between devices: 79.3 us -> 7.63 us
  local copies, waits for them, and re-layouts: 38.6 us -> 1.95 us
  starting transfers between devices: 0.12 us -> 24.1 us
  matrix products: 22.3 us -> 0 us
  Pallas kernels: 0 us -> 17.1 us
  between operations: 14 us -> 0.76 us
    psum x1 -> x0, blocking collectives: 246 us -> none  [on_device(): totals = lax.psum((factor * row_sum, factor[..., None] * weighted), 'ctx')]
    pmax x1 -> x0, blocking collectives: 243 us -> none  [on_device(): peak = lax.pmax(row_max, 'ctx')]
    all_gather x1 -> x0, waiting for transfers between devices: 79.2 us -> none  [on_device(): every_query = lax.all_gather(queries, 'ctx', axis=1, tiled=True)]
    all_to_all x0 -> x3, blocking collectives: none -> 65.1 us  [the longest x1 22.8 us: on_device(): attention = lax.all_to_all(mixed, ('x', 'y'), 0, 0, tiled=True)]
    all_gather x1 -> x0, blocking collectives: 42.5 us -> none  [on_device(): every_node = lax.all_gather(node_kv, 'ctx', axis=1, tiled=True)]
    dot_general x31 -> x0, matrix products: 22.3 us -> none  [the longest x8 12.3 us: soft_partial(): jnp.einsum('nkgt,tkd->nkgd', weights, value_rows.astype(jnp.float32), pre...]
    dynamic_slice x32 -> x0, local copies, waits for them, and re-layouts: 17.2 us -> none  [on_device(): lax.map(attend, (query_heads, cache_rows, tree_rows, cache_live, local_ma...]
    pallas_call x0 -> x5, Pallas kernels: none -> 17.1 us  [the longest x1 7.94 us: on_device(): pl.pallas_call(attend_kernel, out_shape=jax.ShapeDtypeStruct((CHIPS, BLOC...]
  transfers between devices with their start and end apart: 3 -> 2, of which waited for: 1 -> 1; matrix products, arithmetic and copies ran while one was open for 3% -> 0% of each run, Pallas kernels for 0% -> 1%
where the time goes in v1:
time: 118 us; the launch traced here: 117 us
  blocking collectives  65.1 us (55%)
  starting transfers between devices  24.1 us (20%)
  Pallas kernels  17.1 us (14%)
  waiting for transfers between devices  7.63 us (6%)
  local copies, waits for them, and re-layouts  1.95 us (2%)
    all_to_all x1, blocking collectives, on_device(): attention = lax.all_to_all(mixed, ('x', 'y'), 0, 0, tiled=True)  22.8 us
    all_to_all x1, blocking collectives, on_device(): every_query = lax.all_to_all(message, ('x', 'y', 'core'), 0, 0, tiled=True)  22 us
    all_to_all x1, blocking collectives, on_device(): parts = lax.all_to_all(partial, ('x', 'y'), 0, 0, tiled=True)  20.2 us
    all_to_all x1, starting transfers between devices, on_device(): shares = lax.all_to_all(sums, ('core', 'tp'), 0, 0, tiled=True)  15.3 us
    ppermute x1, starting transfers between devices, on_device(): peer = lax.ppermute(send, 'core', [(0, 1), (1, 0)])  8.79 us
    pallas_call x1, Pallas kernels, on_device(): pl.pallas_call(attend_kernel, out_shape=jax.ShapeDtypeStruct((CHIPS, BLOC...  7.94 us
    all_to_all x1, waiting for transfers between devices, on_device(): shares = lax.all_to_all(sums, ('core', 'tp'), 0, 0, tiled=True)  7.63 us
    pallas_call x1, Pallas kernels, on_device(): pl.pallas_call(pack_kernel, out_shape=(jax.ShapeDtypeStruct((SEND_ROWS, 2...  4.59 us
  transfers between devices with their start and end apart: 2, of which 1 were waited for; matrix products, arithmetic and copies ran while one was open for 0% of the time, Pallas kernels for 1%

profile of v1, /device:TPU:1, one launch (start us, length us, event | category | flops | bytes accessed | tf_op | source)
XLA Modules:
  0.0 117.3 jit_solution(2222030586640777226)
XLA Ops:
  0.6 0.0 copy-start.3
  0.6 0.0 copy-start.1
  0.7 0.0 copy-start.4
  0.7 0.0 copy-start.2
  0.7 1.7 %copy.17.pool.pool_in = bf16[72,64,256]{2,1,0:T(8,128)(2,1)S(1)} copy(bf16[72,64,256]{2,1,0:T(8,128)(2,1)} %param.12) | data formatting | bytes 4718592
  2.4 0.1 pad_add_fusion.where
  2.5 0.0 copy-done.1
  2.5 4.6 %pack.1 = (bf16[2576,256]{1,0:T(8,128)(2,1)}, f32[4,16,128]{2,1,0:T(8,128)S(1)}) custom-call(s32[2]{0:T(128)S(1)} %pad_add_fusion.where, s32[8,8]{1,0:T(8,128)S(1)} %copy-done.2, bf16[72,64,256]{2,1,0:T(8,128)(2,1)S(1)} %copy.17.pool.pool_in, bf16[1024,128]{1,0:T(8,128)(2,1)S(1)} %copy-done.1, bf16[8,256]{1,0:T(8,128)(2,1)S(1)} %bitcast.9, s32[8,64]{1,0:T(8,128)S(1)} %copy-done.4), custom_call_target="tpu_custom_call" | custom-call | tf_op jit(solution)/shard_map/pack/pallas_call | solution.py:291
  7.1 8.8 %collective-permute-start = (bf16[2576,256]{1,0:T(8,128)(2,1)}, bf16[2576,256]{1,0:T(8,128)(2,1)}, u32[]{:S(2)}, u32[]{:S(2)}) collective-permute-start(bf16[2576,256]{1,0:T(8,128)(2,1)} %get-tuple-element.7), channel_id=1, source_target_pairs={{0,8},{8,0},{1,9},{9,1},{2,10},{10,2},{3,11},{11,3},{4,12},{12,4},... | collective-permute-start | bytes 3956744 | tf_op jit(solution)/shard_map/ppermute | solution.py:303
  15.9 0.1 broadcast_in_dim.8
  16.0 22.0 %all_to_all.20.queries = bf16[64,32,128]{2,1,0:T(8,128)(2,1)S(1)} all-to-all(bf16[64,32,128]{2,1,0:T(8,128)(2,1)S(1)} %bitcast.11), channel_id=1, replica_groups=mesh['x'=4,'y'=8,'core'=2,'tp'=8] {'x','y','core'}, dimensions={0} | all-to-all | bytes 1048576 | tf_op jit(solution)/shard_map/all_to_all | solution.py:307
  38.0 0.0 collective-permute-done.peer
  38.0 7.9 %attend.1 = bf16[32,72,128]{2,1,0:T(8,128)(2,1)S(1)} custom-call(s32[2]{0:T(128)S(1)} %pad_add_fusion.where, s32[8,8]{1,0:T(8,128)S(1)} %copy-done.2, s32[8]{0:T(128)S(1)} %copy-done.6, bf16[72,64,256]{2,1,0:T(8,128)(2,1)S(1)} %copy.17.pool.pool_in, bf16[64,32,128]{2,1,0:T(8,128)(2,1)S(1)} %all_to_all.20.queries, ...), custom_call_target="tpu_custom_call" | custom-call | tf_op jit(solution)/shard_map/attend/pallas_call | solution.py:309
  46.0 20.2 %all_to_all.21.got = bf16[32,72,128]{2,1,0:T(8,128)(2,1)S(1)} all-to-all(bf16[32,72,128]{2,1,0:T(8,128)(2,1)S(1)} %attend.1), channel_id=1, replica_groups=mesh['x'=4,'y'=8,'core'=2,'tp'=8] {'x','y'}, dimensions={0} | all-to-all | bytes 1179648 | tf_op jit(solution)/shard_map/all_to_all | solution.py:319
  66.2 0.8 combine.1
  67.0 0.0 copy-start.9
  67.0 0.0 copy-start.7
  67.0 22.8 %all_to_all.22.got = bf16[32,72,128]{2,1,0:T(8,128)(2,1)S(1)} all-to-all(bf16[32,72,128]{2,1,0:T(8,128)(2,1)S(1)} %combine.1), channel_id=1, replica_groups=mesh['x'=4,'y'=8,'core'=2,'tp'=8] {'x','y'}, dimensions={0} | all-to-all | bytes 1179648 | tf_op jit(solution)/shard_map/all_to_all | solution.py:328
  89.9 2.1 %project.1 = f32[16,4,8,128]{3,2,1,0:T(8,128)} custom-call(s32[2]{0:T(128)S(1)} %pad_add_fusion.where, bf16[32,72,128]{2,1,0:T(8,128)(2,1)S(1)} %all_to_all.22.got, bf16[1024,128]{1,0:T(8,128)(2,1)S(1)} %copy-done.1, bf16[2576,256]{1,0:T(8,128)(2,1)} %collective-permute-done.peer), custom_call_target="tpu_custom_call" | custom-call | tf_op jit(solution)/shard_map/project/pallas_call | solution.py:330
  92.0 15.3 %all-to-all-start.3 = ((f32[16,4,8,128]{3,2,1,0:T(8,128)}), f32[16,4,8,128]{3,2,1,0:T(8,128)S(1)}, u32[]{:S(2)}, u32[]{:S(2)}) async-start(f32[16,4,8,128]{3,2,1,0:T(8,128)} %project.1), calls=%async_computation.3 | async-start | bytes 524288 | tf_op jit(solution)/shard_map/all_to_all | solution.py:344
  107.3 0.1 copy.14.spare
  107.4 1.7 %write.1 = (bf16[72,64,256]{2,1,0:T(8,128)(2,1)}, s32[8,8]{1,0:T(8,128)}) custom-call(s32[2]{0:T(128)S(1)} %pad_add_fusion.where, s32[8,8]{1,0:T(8,128)S(1)} %copy-done.2, s32[8]{0:T(128)S(1)} %copy-done.6, s32[8]{0:T(128)S(1)} %copy-done.7, s32[8,1]{1,0:T(8,128)S(1)} %copy.14.spare, s32[8,8]{1,0:T(8,128)S(1)} %copy-done.2, ...), custom_call_target="tpu_custom_call", output_to_operand_aliasing={{0}: (7, {})} | custom-call | tf_op jit(solution)/shard_map/write/pallas_call | solution.py:347
  109.1 7.6 %all-to-all-done.3 = f32[16,4,8,128]{3,2,1,0:T(8,128)S(1)} async-done(((f32[16,4,8,128]{3,2,1,0:T(8,128)}), f32[16,4,8,128]{3,2,1,0:T(8,128)S(1)}, u32[]{:S(2)}, u32[]{:S(2)}) %all-to-all-start.3) | async-done | bytes 262176 | tf_op jit(solution)/shard_map/all_to_all | solution.py:344
  116.7 0.6 bitcast_reduce_fusion
  (14 shorter events, 0.0 us)
Async XLA Ops:
  0.6 1.8 %copy-start.3 = (bf16[8,1,256]{2,0,1:T(8,128)(2,1)S(1)}, bf16[8,1,256]{2,0,1:T(8,128)(2,1)}, u32[]{:S(2)}) copy-start(bf16[8,1,256]{2,0,1:T(8,128)(2,1)} %param.11) | copy-start | bytes 12292
  0.6 1.8 %copy-start.1 = (bf16[1024,128]{1,0:T(8,128)(2,1)S(1)}, bf16[1024,128]{1,0:T(8,128)(2,1)}, u32[]{:S(2)}) copy-start(bf16[1024,128]{1,0:T(8,128)(2,1)} %weight.3) | copy-start | bytes 786436
  0.7 1.8 %copy-start.4 = (s32[8,64]{1,0:T(8,128)S(1)}, s32[8,64]{1,0:T(8,128)}, u32[]{:S(2)}) copy-start(s32[8,64]{1,0:T(8,128)} %parents.1) | copy-start | bytes 6148
  0.7 1.8 %copy-start.2 = (s32[8,8]{1,0:T(8,128)S(1)}, s32[8,8]{1,0:T(8,128)}, u32[]{:S(2)}) copy-start(s32[8,8]{1,0:T(8,128)} %table_v.1) | copy-start | bytes 772
  2.4 43.6 %copy-start = (bf16[72,64,256]{2,1,0:T(8,128)(2,1)}, bf16[72,64,256]{2,1,0:T(8,128)(2,1)S(1)}, u32[]{:S(2)}) copy-start(bf16[72,64,256]{2,1,0:T(8,128)(2,1)S(1)} %copy.17.pool.pool_in) | copy-start | bytes 7077892
  2.4 13.5 %copy-start.8 = (bf16[8,1,1024]{2,0,1:T(8,128)(2,1)S(1)}, bf16[8,1,1024]{2,0,1:T(8,128)(2,1)}, u32[]{:S(2)}) copy-start(bf16[8,1,1024]{2,0,1:T(8,128)(2,1)} %param.10) | copy-start | bytes 49156
  2.4 35.6 %copy-start.6 = (s32[8]{0:T(128)S(1)}, s32[8]{0:T(128)}, u32[]{:S(2)}) copy-start(s32[8]{0:T(128)} %lengths.3) | copy-start | bytes 100
  7.1 30.9 %collective-permute-start = (bf16[2576,256]{1,0:T(8,128)(2,1)}, bf16[2576,256]{1,0:T(8,128)(2,1)}, u32[]{:S(2)}, u32[]{:S(2)}) collective-permute-start(bf16[2576,256]{1,0:T(8,128)(2,1)} %get-tuple-element.7), channel_id=1, source_target_pairs={{0,8},{8,0},{1,9},{9,1},{2,10},{10,2},{3,11},{11,3},{4,12},{12,4},... | collective-permute-start | bytes 3956744 | tf_op jit(solution)/shard_map/ppermute | solution.py:303
  38.0 28.2 %copy-start.5 = (s32[8,8]{1,0:T(8,128)S(1)}, s32[8,8]{1,0:T(8,128)}, u32[]{:S(2)}) copy-start(s32[8,8]{1,0:T(8,128)} %path.1) | copy-start | bytes 772
  67.0 40.3 %copy-start.9 = (s32[8,1]{0,1:T(1,128)S(1)}, s32[8,1]{0,1:T(1,128)}, u32[]{:S(2)}) copy-start(s32[8,1]{0,1:T(1,128)} %param.19) | copy-start | bytes 100
  67.0 40.4 %copy-start.7 = (s32[8]{0:T(128)S(1)}, s32[8]{0:T(128)}, u32[]{:S(2)}) copy-start(s32[8]{0:T(128)} %counts.1) | copy-start | bytes 100
  92.0 24.7 %all-to-all-start.3 = ((f32[16,4,8,128]{3,2,1,0:T(8,128)}), f32[16,4,8,128]{3,2,1,0:T(8,128)S(1)}, u32[]{:S(2)}, u32[]{:S(2)}) async-start(f32[16,4,8,128]{3,2,1,0:T(8,128)} %project.1), calls=%async_computation.3 | async-start | bytes 524288 | tf_op jit(solution)/shard_map/all_to_all | solution.py:344

commit v2 on v1

v2 whole, which is shorter than its diff:
```python
import jax
import jax.numpy as jnp
from jax import lax
from jax.experimental import pallas as pl
from jax.experimental.pallas import tpu as pltpu
from jax.sharding import Mesh, PartitionSpec as P

F32 = jnp.float32
BF16 = jnp.bfloat16

HEAD = 128
PATH_ROWS = 8
PAGE = 64
REQUESTS = 8
HALF = 4
NODES = 64
PAGES_LOCAL = 8
SPAN = PAGE * PAGES_LOCAL
LANES = 8 * NODES
CHIPS = 32
TAIL = 8
BLOCK = 64 + TAIL
GATHERED = 64 + 2 * PATH_ROWS
NEIGHBOURS = 8
DEAD = -1e30
FLOOR = -1e28
LOG2E = 1.4426950408889634
SCALE2 = HEAD ** (-0.5) * LOG2E

NODE_ROWS0 = HALF * SPAN
SEND_ROWS = NODE_ROWS0 + 16

VMEM = pltpu.VMEM
SMEM = pltpu.SMEM
HBM = pltpu.HBM
LIMIT = 40 * 1024 * 1024


def iota(shape, dim):
    return lax.broadcasted_iota(jnp.int32, shape, dim)


def dot(a, b, ca=1, cb=0):
    return lax.dot_general(a, b, (((ca,), (cb,)), ((), ())), preferred_element_type=F32)


def ctx_index():
    return (lax.axis_index("x") * 8 + lax.axis_index("y")) * 2 + lax.axis_index("core")


def pack_kernel(where, table, pool, node, send, node_pad, sems):
    other = HALF * (1 - where[0])
    copies = []
    for r in range(HALF):
        for p in range(PAGES_LOCAL):
            n = r * PAGES_LOCAL + p
            copies.append(
                pltpu.make_async_copy(
                    pool.at[table[other + r, p]], send.at[pl.ds(n * PAGE, PAGE), :], sems.at[n]
                )
            )
    for c in copies:
        c.start()
    rows = node[...].astype(F32)
    node_pad[...] = jnp.concatenate([rows, jnp.zeros_like(rows)], axis=0).astype(BF16)
    last = pltpu.make_async_copy(node_pad, send.at[pl.ds(NODE_ROWS0, 16), :], sems.at[32])
    last.start()
    for c in copies:
        c.wait()
    last.wait()


def prepare_kernel(where, table, pool, parents, own, pool_copy, mask, sems):
    core = where[0]
    ctx = where[1]
    copies = []
    for r in range(HALF):
        for p in range(PAGES_LOCAL):
            n = r * PAGES_LOCAL + p
            copies.append(
                pltpu.make_async_copy(
                    pool.at[table[HALF * core + r, p]], own.at[pl.ds(n * PAGE, PAGE), :], sems.at[n]
                )
            )
    copies.append(pltpu.make_async_copy(pool, pool_copy, sems.at[32]))
    for c in copies:
        c.start()
    up = iota((NODES, NODES), 0)
    down = iota((NODES, NODES), 1)
    twice = (iota((NODES, 2 * NODES), 0) == iota((NODES, 2 * NODES), 1) % NODES).astype(F32).astype(BF16)
    pick_row = iota((16, NODES), 0)
    pick_node = iota((16, NODES), 1)
    reach = []
    for r in range(HALF):
        link = parents[pl.ds(HALF * core + r, 1), :]
        reach.append(((up == link) | (up == down)).astype(F32).astype(BF16))
    for _ in range(6):
        reach = [jnp.minimum(dot(m, m), 1.0).astype(BF16) for m in reach]
    for r in range(HALF):
        mine = HALF * core + r
        pick = ((pick_row == mine) & (pick_node == ctx)) | (
            (pick_row == REQUESTS + mine) & (pick_node == ctx + 1 - 2 * core)
        )
        seen = dot(pick.astype(F32).astype(BF16), reach[r]).astype(BF16)
        mask[r] = dot(seen, twice)
    for c in copies:
        c.wait()


def attend_kernel(where, lengths, queries, own, peer, node, mask, out):
    core = where[0]
    ctx = where[1]
    lane = iota((LANES, LANES), 1)
    order = (iota((LANES, LANES), 0) == (lane % NODES) * 8 + lane // NODES).astype(F32).astype(BF16)
    peer_node = peer[pl.ds(NODE_ROWS0, 16), :].astype(F32)[:REQUESTS]
    own_node = node[...].astype(F32)
    nodes = jnp.concatenate([own_node, peer_node], axis=0).astype(BF16)
    ones = jnp.ones((16, SPAN), BF16)
    ones_tree = jnp.ones((16, 16), BF16)
    row = iota((SPAN, LANES), 0)
    tail_row = iota((TAIL, HEAD), 0)
    for r in range(HALF):
        part = queries[:, pl.ds((r // 2) * 16, 16), :].astype(F32)[:, (r % 2) * 8 : (r % 2) * 8 + 8, :]
        part = part.reshape(LANES, HEAD).astype(BF16)
        query = dot(part, order, 0, 0).astype(BF16)
        length = lengths[HALF * core + r]
        span_own = own[pl.ds(r * SPAN, SPAN), :]
        span_peer = peer[pl.ds(r * SPAN, SPAN), :]
        live_own = row < length - ctx * SPAN
        live_peer = row < length - (ctx + 1 - 2 * core) * SPAN
        seen = jnp.concatenate([mask[r]] * 4, axis=1)
        s_own = jnp.where(live_own, dot(span_own[:, :HEAD], query), DEAD)
        s_peer = jnp.where(live_peer, dot(span_peer[:, :HEAD], query), DEAD)
        s_tree = jnp.where(seen > 0.5, dot(nodes[:, :HEAD], query), DEAD)
        peak = jnp.maximum(
            jnp.maximum(jnp.max(s_own, axis=0, keepdims=True), jnp.max(s_peer, axis=0, keepdims=True)),
            jnp.max(s_tree, axis=0, keepdims=True),
        )
        peak = jnp.maximum(peak, FLOOR) * SCALE2
        total = None
        for s, v, one in (
            (s_own, span_own[:, HEAD:], ones),
            (s_peer, span_peer[:, HEAD:], ones),
            (s_tree, nodes[:, HEAD:], ones_tree),
        ):
            p = jnp.exp2(s * SCALE2 - peak)
            lhs = jnp.concatenate([v.astype(F32).T.astype(BF16), one], axis=0)
            high = p.astype(BF16)
            low = (p - high.astype(F32)).astype(BF16)
            add = dot(lhs, high) + dot(lhs, low)
            total = add if total is None else total + add
        row_sum = total[HEAD : HEAD + 1]
        some = row_sum > 0.0
        mixed = total[:HEAD] * (1.0 / jnp.where(some, row_sum, 1.0))
        log_sum = jnp.where(some, peak + jnp.log2(jnp.where(some, row_sum, 1.0)), DEAD)
        first = log_sum.astype(BF16).astype(F32)
        rest = log_sum - first
        second = rest.astype(BF16).astype(F32)
        third = rest - second
        for y in range(8):
            lanes = slice((y // 2) * HEAD, (y // 2 + 1) * HEAD)
            half = y % 2
            terms = (
                first[:, lanes],
                second[:, lanes],
                third[:, lanes],
                own_node[y : y + 1, :HEAD],
                own_node[y : y + 1, HEAD:],
                peer_node[y : y + 1, :HEAD],
                peer_node[y : y + 1, HEAD:],
            )
            tail = jnp.zeros((TAIL, HEAD), F32)
            for t, term in enumerate(terms):
                tail = jnp.where(tail_row == t, term, tail)
            block = jnp.concatenate([mixed[half * 64 : half * 64 + 64, lanes], tail], axis=0)
            out[r * 8 + y] = block.astype(BF16)


def combine_kernel(where, path, got, out):
    core = where[0]
    y = (where[1] // 2) % 8
    logs = []
    for s in range(CHIPS):
        tail = got[s].astype(F32)[64:BLOCK]
        logs.append(tail[0:1] + tail[1:2] + tail[2:3])
    peak = logs[0]
    for s in range(1, CHIPS):
        peak = jnp.maximum(peak, logs[s])
    total = jnp.zeros((1, HEAD), F32)
    mixed = jnp.zeros((64, HEAD), F32)
    for s in range(CHIPS):
        share = jnp.exp2(logs[s] - peak)
        total = total + share
        mixed = mixed + share * got[s].astype(F32)[:64]
    mixed = mixed * (1.0 / total)
    tail_row = iota((2 * PATH_ROWS, HEAD), 0)
    tail = jnp.zeros((2 * PATH_ROWS, HEAD), F32)
    for j in range(PATH_ROWS):
        node = path[y, j]
        held = got[node // 2].astype(F32)[64:BLOCK]
        is_own = node % 2 == core
        key = jnp.where(is_own, held[3:4], held[5:6])
        value = jnp.where(is_own, held[4:5], held[6:7])
        tail = jnp.where(tail_row == 2 * j, key, tail)
        tail = jnp.where(tail_row == 2 * j + 1, value, tail)
    block = jnp.concatenate([mixed, tail], axis=0).astype(BF16)
    for s in range(8):
        out[s] = block


def project_kernel(got, weights, out):
    a = got[...][:, :64, :].reshape(LANES, HEAD)
    for pair in range(NEIGHBOURS // 2):
        sums = None
        for h in range(2):
            cols = []
            for n in (2 * pair, 2 * pair + 1):
                rows = [weights[n, (2 * p + h) * HEAD : (2 * p + h + 1) * HEAD, :] for p in range(4)]
                cols.append(jnp.concatenate(rows, axis=0))
            part = dot(a, jnp.concatenate(cols, axis=1), 0, 0)[h * NODES : (h + 1) * NODES]
            sums = part if sums is None else sums + part
        for t in range(8):
            rows = sums[t * 8 : t * 8 + 8]
            out[2 * pair * 8 + t] = rows[:, :HEAD]
            out[(2 * pair + 1) * 8 + t] = rows[:, HEAD:]


def write_kernel(where, table, lengths, counts, spare, table_v, got, pool_in, pool, new_table, pages, sems):
    ctx = where[1]
    for r in range(REQUESTS):
        for p in range(PAGES_LOCAL):
            new_table[r, p] = table[r, p]
    row = iota((PAGE, 2 * HEAD), 0)
    for r in range(REQUESTS):
        length = lengths[r]
        count = counts[r]
        tail_page = length // PAGE
        for step in range(2):
            page = tail_page + step
            local = page - ctx * PAGES_LOCAL
            first = length - page * PAGE
            here = (local >= 0) & (local < PAGES_LOCAL)
            if step == 1:
                here = here & (first + count > 0)

            @pl.when(here)
            def _():
                slot = table[r, local]
                target = slot
                if step == 0:
                    uses = jnp.sum((table_v[...] == slot).astype(jnp.int32))
                    target = jnp.where(uses > 1, spare[r, 0], slot)
                    new_table[r, local] = target
                fetch = pltpu.make_async_copy(pool_in.at[slot], pages.at[2 * r + step], sems.at[2 * r + step])
                fetch.start()
                fetch.wait()
                now = pages[2 * r + step].astype(F32)
                held = got[r].astype(F32)[64:GATHERED]
                for j in range(PATH_ROWS):
                    new = jnp.concatenate([held[2 * j : 2 * j + 1], held[2 * j + 1 : 2 * j + 2]], axis=1)
                    now = jnp.where((row == first + j) & (j < count), new, now)
                pages[2 * r + step] = now.astype(BF16)
                store = pltpu.make_async_copy(pages.at[2 * r + step], pool.at[target], sems.at[2 * r + step])
                store.start()
                store.wait()


def spec(space):
    return pl.BlockSpec(memory_space=space)


def on_device(queries, node_kv, pool, out_weight, parents, path, counts, lengths, table, free_slot):
    params = pltpu.CompilerParams(vmem_limit_bytes=LIMIT)
    shape = jax.ShapeDtypeStruct
    where = jnp.stack([lax.axis_index("core"), ctx_index()]).astype(jnp.int32)
    node = node_kv.reshape(REQUESTS, 2 * HEAD)
    weights = lax.all_gather(out_weight, ("x", "core"), axis=0)

    send = pl.pallas_call(
        pack_kernel,
        out_shape=shape((SEND_ROWS, 2 * HEAD), BF16),
        in_specs=[spec(SMEM), spec(SMEM), spec(HBM), spec(VMEM)],
        out_specs=spec(pl.ANY),
        scratch_shapes=[VMEM((16, 2 * HEAD), BF16), pltpu.SemaphoreType.DMA((33,))],
        compiler_params=params,
        name="pack",
    )(where, table, pool, node)
    peer = lax.ppermute(send, "core", [(0, 1), (1, 0)])

    by_core = queries.reshape(2, HALF * 8, HEAD)
    message = jnp.broadcast_to(by_core[None], (CHIPS, 2, HALF * 8, HEAD)).reshape(2 * CHIPS, HALF * 8, HEAD)
    every_query = lax.all_to_all(message, ("x", "y", "core"), 0, 0, tiled=True)

    own, pool_copy, mask = pl.pallas_call(
        prepare_kernel,
        out_shape=(
            shape((HALF * SPAN, 2 * HEAD), BF16),
            shape(pool.shape, pool.dtype),
            shape((HALF, 16, 2 * NODES), F32),
        ),
        in_specs=[spec(SMEM), spec(SMEM), spec(HBM), spec(VMEM)],
        out_specs=(spec(VMEM), spec(HBM), spec(VMEM)),
        scratch_shapes=[pltpu.SemaphoreType.DMA((33,))],
        compiler_params=params,
        cost_estimate=pl.CostEstimate(flops=50_000_000, bytes_accessed=7_000_000, transcendentals=0),
        name="prepare",
    )(where, table, pool, parents)

    partial = pl.pallas_call(
        attend_kernel,
        out_shape=shape((CHIPS, BLOCK, HEAD), BF16),
        in_specs=[spec(SMEM), spec(SMEM)] + [spec(VMEM)] * 5,
        out_specs=spec(VMEM),
        compiler_params=params,
        name="attend",
    )(where, lengths, every_query, own, peer, node, mask)

    parts = lax.all_to_all(partial, ("x", "y"), 0, 0, tiled=True)
    mixed = pl.pallas_call(
        combine_kernel,
        out_shape=shape((8, GATHERED, HEAD), BF16),
        in_specs=[spec(SMEM), spec(SMEM), spec(VMEM)],
        out_specs=spec(VMEM),
        compiler_params=params,
        name="combine",
    )(where, path, parts)
    attention = lax.all_to_all(mixed, "y", 0, 0, tiled=True)

    sums = pl.pallas_call(
        project_kernel,
        out_shape=shape((64, 8, HEAD), F32),
        in_specs=[spec(VMEM), spec(VMEM)],
        out_specs=spec(VMEM),
        compiler_params=params,
        name="project",
    )(attention, weights)
    shares = lax.all_to_all(sums, ("x", "core", "tp"), 0, 0, tiled=True)
    summed = jnp.sum(shares.reshape(4, 2, 8, 8, HEAD), axis=2)
    projected = jnp.swapaxes(summed, 0, 1).reshape(REQUESTS, 8, HEAD)

    updated_pool, new_table = pl.pallas_call(
        write_kernel,
        out_shape=(shape(pool.shape, pool.dtype), shape(table.shape, table.dtype)),
        in_specs=[spec(SMEM)] * 5 + [spec(VMEM), spec(VMEM), spec(HBM)],
        out_specs=(spec(HBM), spec(SMEM)),
        input_output_aliases={7: 0},
        scratch_shapes=[VMEM((2 * REQUESTS, PAGE, 2 * HEAD), BF16), pltpu.SemaphoreType.DMA((2 * REQUESTS,))],
        compiler_params=params,
        name="write",
    )(where, table, lengths, counts, free_slot, table, attention, pool_copy)
    return projected, updated_pool, new_table


def solution(mesh):
    fine = Mesh(mesh.devices.reshape(4, 8, 2, 8), ("x", "y", "core", "tp"))
    ctx = ("x", "y", "core")
    placed = (
        P(None, ctx, "tp"),
        P(None, ctx, "tp"),
        P(ctx, None, "tp"),
        P("tp", ctx),
        P(),
        P(),
        P(),
        P(),
        P(None, ctx),
        P(None, ctx),
    )
    return jax.shard_map(
        on_device,
        mesh=fine,
        in_specs=placed,
        out_specs=(P(None, "tp", ctx), P(ctx, None, "tp"), P(None, ctx)),
        check_vma=False,
    )
```

time: 118 us -> 127 us (1.076)
  blocking collectives: 65.1 us -> 34.6 us
  waiting for transfers between devices: 7.63 us -> 23.4 us
  between operations: 0.76 us -> 14.2 us
  local copies, waits for them, and re-layouts: 1.95 us -> 8.53 us
  starting transfers between devices: 24.1 us -> 28.6 us
    all_to_all x2 -> x1, blocking collectives: 44.8 us -> 14.3 us  [on_device(): attention = lax.all_to_all(mixed, 'y', 0, 0, tiled=True)]
    all_to_all x1 -> x2, waiting for transfers between devices: 7.63 us -> 22.8 us  [the longest x1 12.5 us: on_device(): every_query = lax.all_to_all(message, ('x', 'y', 'core'), 0, 0, tiled=True)]
    unnamed x22 -> x31, local copies, waits for them, and re-layouts: 1.83 us -> 6.98 us
    all_to_all x1 -> x2, starting transfers between devices: 15.3 us -> 19.8 us  [the longest x1 14.9 us: on_device(): shares = lax.all_to_all(sums, ('x', 'core', 'tp'), 0, 0, tiled=True)]
    pallas_call x5 -> x6, Pallas kernels: 17.1 us -> 16.4 us  [the longest x1 7.1 us: on_device(): pl.pallas_call(attend_kernel, out_shape=shape((CHIPS, BLOCK, HEAD), BF16)...]
  transfers between devices with their start and end apart: 2 -> 4, of which waited for: 1 -> 2; matrix products, arithmetic and copies ran while one was open for 0% -> 1% of each run, Pallas kernels for 1% -> 12%
where the time goes in v2:
time: 127 us; the launch traced here: 126 us
  blocking collectives  34.6 us (27%)
  starting transfers between devices  28.6 us (23%)
  waiting for transfers between devices  23.4 us (18%)
  Pallas kernels  16.4 us (13%)
  between operations  14.2 us (11%)
  local copies, waits for them, and re-layouts  8.53 us (7%)
    all_to_all x1, blocking collectives, on_device(): parts = lax.all_to_all(partial, ('x', 'y'), 0, 0, tiled=True)  20.3 us
    all_to_all x1, starting transfers between devices, on_device(): shares = lax.all_to_all(sums, ('x', 'core', 'tp'), 0, 0, tiled=True)  14.9 us
    all_to_all x1, blocking collectives, on_device(): attention = lax.all_to_all(mixed, 'y', 0, 0, tiled=True)  14.3 us
    all_to_all x1, waiting for transfers between devices, on_device(): every_query = lax.all_to_all(message, ('x', 'y', 'core'), 0, 0, tiled=True)  12.5 us
    all_to_all x1, waiting for transfers between devices, on_device(): shares = lax.all_to_all(sums, ('x', 'core', 'tp'), 0, 0, tiled=True)  10.3 us
    ppermute x1, starting transfers between devices, on_device(): peer = lax.ppermute(send, 'core', [(0, 1), (1, 0)])  8.79 us
    pallas_call x1, Pallas kernels, on_device(): pl.pallas_call(attend_kernel, out_shape=shape((CHIPS, BLOCK, HEAD), BF16)...  7.1 us
    unnamed x31, local copies, waits for them, and re-layouts  6.98 us
  transfers between devices with their start and end apart: 4, of which 2 were waited for; matrix products, arithmetic and copies ran while one was open for 1% of the time, Pallas kernels for 12%

profile of v2, /device:TPU:1, one launch (start us, length us, event | category | flops | bytes accessed | tf_op | source)
XLA Modules:
  0.0 125.9 jit_solution(965880469220473774)
XLA Ops:
  7.2 0.7 all-gather.3.cloned.1.call-update
  7.9 0.1 pad_add_fusion.where
  8.0 1.7 %copy-done = bf16[72,64,256]{2,1,0:T(8,128)(2,1)S(1)} copy-done((bf16[72,64,256]{2,1,0:T(8,128)(2,1)S(1)}, bf16[72,64,256]{2,1,0:T(8,128)(2,1)}, u32[]{:S(2)}) %copy-start) | copy-done | bytes 2359320
  9.7 0.7 copy-done.5
  10.3 0.7 copy-done.7
  11.0 1.9 %pack.1 = bf16[2064,256]{1,0:T(8,128)(2,1)} custom-call(s32[2]{0:T(128)S(1)} %pad_add_fusion.where, s32[8,8]{1,0:T(8,128)S(1)} %copy-done.5, bf16[72,64,256]{2,1,0:T(8,128)(2,1)S(1)} %copy-done, bf16[8,256]{1,0:T(8,128)(2,1)S(1)} %bitcast.12), custom_call_target="tpu_custom_call" | custom-call | tf_op jit(solution)/shard_map/pack/pallas_call | solution.py:279
  12.9 8.8 %collective-permute-start = (bf16[2064,256]{1,0:T(8,128)(2,1)}, bf16[2064,256]{1,0:T(8,128)(2,1)}, u32[]{:S(2)}, u32[]{:S(2)}) collective-permute-start(bf16[2064,256]{1,0:T(8,128)(2,1)} %pack.1), channel_id=1, source_target_pairs={{0,8},{8,0},{1,9},{9,1},{2,10},{10,2},{3,11},{11,3},{4,12},{12,4},... | collective-permute-start | bytes 3170312 | tf_op jit(solution)/shard_map/ppermute | solution.py:288
  21.8 0.9 broadcast_in_dim.8
  22.7 4.9 %all-to-all-start = ((bf16[64,32,128]{2,1,0:T(8,128)(2,1)}), bf16[64,32,128]{2,1,0:T(8,128)(2,1)S(1)}, u32[]{:S(2)}, u32[]{:S(2)}) async-start(bf16[64,32,128]{2,1,0:T(8,128)(2,1)} %bitcast.2), calls=%async_computation | async-start | bytes 1048576 | tf_op jit(solution)/shard_map/all_to_all | solution.py:292
  27.6 3.8 %prepare.1 = (bf16[2048,256]{1,0:T(8,128)(2,1)S(1)}, bf16[72,64,256]{2,1,0:T(8,128)(2,1)}, f32[4,16,128]{2,1,0:T(8,128)S(1)}) custom-call(s32[2]{0:T(128)S(1)} %pad_add_fusion.where, s32[8,8]{1,0:T(8,128)S(1)} %copy-done.6, bf16[72,64,256]{2,1,0:T(8,128)(2,1)S(1)} %copy-done.1, s32[8,64]{1,0:T(8,128)S(1)} %copy-done.9), custom_call_target="tpu_custom_call" | custom-call | flops 50000000 | bytes 7000000 | tf_op jit(solution)/shard_map/prepare/pallas_call | solution.py:294
  31.4 1.0 copy-done.3
  32.4 12.5 %all-to-all-done.queries = bf16[64,32,128]{2,1,0:T(8,128)(2,1)S(1)} async-done(((bf16[64,32,128]{2,1,0:T(8,128)(2,1)}), bf16[64,32,128]{2,1,0:T(8,128)(2,1)S(1)}, u32[]{:S(2)}, u32[]{:S(2)}) %all-to-all-start) | async-done | bytes 524320 | tf_op jit(solution)/shard_map/all_to_all | solution.py:292
  44.9 1.2 copy-done.4
  46.1 7.1 %attend.1 = bf16[32,72,128]{2,1,0:T(8,128)(2,1)S(1)} custom-call(s32[2]{0:T(128)S(1)} %pad_add_fusion.where, s32[8]{0:T(128)S(1)} %copy-done.11, bf16[64,32,128]{2,1,0:T(8,128)(2,1)S(1)} %all-to-all-done.queries, bf16[2048,256]{1,0:T(8,128)(2,1)S(1)} %copy-done.4, bf16[2064,256]{1,0:T(8,128)(2,1)} %collective-permute-done.peer, bf16[8,256]{1,0:T(8,128)(2,1)S(1)} %bitcast.13, ...), custom_call_target="tpu_custom_call" | custom-call | tf_op jit(solution)/shard_map/attend/pallas_call | solution.py:309
  53.2 20.3 %all_to_all.20.got = bf16[32,72,128]{2,1,0:T(8,128)(2,1)S(1)} all-to-all(bf16[32,72,128]{2,1,0:T(8,128)(2,1)S(1)} %attend.1), channel_id=1, replica_groups=mesh['x'=4,'y'=8,'core'=2,'tp'=8] {'x','y'}, dimensions={0} | all-to-all | bytes 1179648 | tf_op jit(solution)/shard_map/all_to_all | solution.py:318
  73.5 0.8 combine.1
  74.3 14.3 %all_to_all.21.got = bf16[8,80,128]{2,1,0:T(8,128)(2,1)S(1)} all-to-all(bf16[8,80,128]{2,1,0:T(8,128)(2,1)S(1)} %combine.1), channel_id=1, replica_groups=mesh['x'=4,'y'=8,'core'=2,'tp'=8] {'y'}, dimensions={0} | all-to-all | bytes 327680 | tf_op jit(solution)/shard_map/all_to_all | solution.py:327
  88.7 1.6 %copy-done.2 = bf16[8192,128]{1,0:T(8,128)(2,1)S(1)} copy-done((bf16[8192,128]{1,0:T(8,128)(2,1)S(1)}, bf16[8192,128]{1,0:T(8,128)(2,1)}, u32[]{:S(2)}) %copy-start.2) | copy-done | bytes 2097176
  90.2 1.2 project.1
  91.4 14.9 %all-to-all-start.3 = ((f32[64,8,128]{2,1,0:T(8,128)}), f32[64,8,128]{2,1,0:T(8,128)S(1)}, u32[]{:S(2)}, u32[]{:S(2)}) async-start(f32[64,8,128]{2,1,0:T(8,128)} %project.1), calls=%async_computation.3 | async-start | bytes 524288 | tf_op jit(solution)/shard_map/all_to_all | solution.py:337
  106.4 0.1 copy.17.spare
  106.4 1.7 %write.1 = (bf16[72,64,256]{2,1,0:T(8,128)(2,1)}, s32[8,8]{1,0:T(8,128)}) custom-call(s32[2]{0:T(128)S(1)} %pad_add_fusion.where, s32[8,8]{1,0:T(8,128)S(1)} %copy-done.6, s32[8]{0:T(128)S(1)} %copy-done.11, s32[8]{0:T(128)S(1)} %copy-done.12, s32[8,1]{1,0:T(8,128)S(1)} %copy.17.spare, s32[8,8]{1,0:T(8,128)S(1)} %copy-done.6, ...), custom_call_target="tpu_custom_call", output_to_operand_aliasing={{0}: (7, {})} | custom-call | tf_op jit(solution)/shard_map/write/pallas_call | solution.py:341
  108.1 10.3 %all-to-all-done.3 = f32[64,8,128]{2,1,0:T(8,128)S(1)} async-done(((f32[64,8,128]{2,1,0:T(8,128)}), f32[64,8,128]{2,1,0:T(8,128)S(1)}, u32[]{:S(2)}, u32[]{:S(2)}) %all-to-all-start.3) | async-done | bytes 262176 | tf_op jit(solution)/shard_map/all_to_all | solution.py:337
  118.4 0.6 copy.16
  (29 shorter events, 0.1 us)
Async XLA Ops:
  7.2 14.6 %copy-start.13 = (bf16[8,1,1024]{2,0,1:T(8,128)(2,1)S(1)}, bf16[8,1,1024]{2,0,1:T(8,128)(2,1)}, u32[]{:S(2)}) copy-start(bf16[8,1,1024]{2,0,1:T(8,128)(2,1)} %param.10) | copy-start | bytes 49156
  7.2 81.5 %all-gather.3.cloned.1.call-start = ((), (), s32[]{:S(2)}) async-start(), calls=%async_computation.4 | async-start | bytes 2359296 | tf_op jit(solution)/shard_map/all_gather | solution.py:277
  8.0 1.7 %copy-start = (bf16[72,64,256]{2,1,0:T(8,128)(2,1)S(1)}, bf16[72,64,256]{2,1,0:T(8,128)(2,1)}, u32[]{:S(2)}) copy-start(bf16[72,64,256]{2,1,0:T(8,128)(2,1)} %pool.3) | copy-start | bytes 7077892
  9.7 0.7 copy-start.5
  10.3 0.7 copy-start.7
  11.0 16.5 %copy-start.1 = (bf16[72,64,256]{2,1,0:T(8,128)(2,1)S(1)}, bf16[72,64,256]{2,1,0:T(8,128)(2,1)}, u32[]{:S(2)}) copy-start(bf16[72,64,256]{2,1,0:T(8,128)(2,1)} %pool.3) | copy-start | bytes 7077892
  11.0 16.5 %copy-start.6 = (s32[8,8]{1,0:T(8,128)S(1)}, s32[8,8]{1,0:T(8,128)}, u32[]{:S(2)}) copy-start(s32[8,8]{1,0:T(8,128)} %table_v.1) | copy-start | bytes 772
  11.0 16.5 %copy-start.9 = (s32[8,64]{1,0:T(8,128)S(1)}, s32[8,64]{1,0:T(8,128)}, u32[]{:S(2)}) copy-start(s32[8,64]{1,0:T(8,128)} %parents.1) | copy-start | bytes 6148
  12.9 32.0 %copy-start.8 = (bf16[8,1,256]{2,0,1:T(8,128)(2,1)S(1)}, bf16[8,1,256]{2,0,1:T(8,128)(2,1)}, u32[]{:S(2)}) copy-start(bf16[8,1,256]{2,0,1:T(8,128)(2,1)} %param.11) | copy-start | bytes 12292
  12.9 32.0 %copy-start.11 = (s32[8]{0:T(128)S(1)}, s32[8]{0:T(128)}, u32[]{:S(2)}) copy-start(s32[8]{0:T(128)} %lengths.3) | copy-start | bytes 100
  12.9 31.9 %collective-permute-start = (bf16[2064,256]{1,0:T(8,128)(2,1)}, bf16[2064,256]{1,0:T(8,128)(2,1)}, u32[]{:S(2)}, u32[]{:S(2)}) collective-permute-start(bf16[2064,256]{1,0:T(8,128)(2,1)} %pack.1), channel_id=1, source_target_pairs={{0,8},{8,0},{1,9},{9,1},{2,10},{10,2},{3,11},{11,3},{4,12},{12,4},... | collective-permute-start | bytes 3170312 | tf_op jit(solution)/shard_map/ppermute | solution.py:288
  22.7 22.2 %all-to-all-start = ((bf16[64,32,128]{2,1,0:T(8,128)(2,1)}), bf16[64,32,128]{2,1,0:T(8,128)(2,1)S(1)}, u32[]{:S(2)}, u32[]{:S(2)}) async-start(bf16[64,32,128]{2,1,0:T(8,128)(2,1)} %bitcast.2), calls=%async_computation | async-start | bytes 1048576 | tf_op jit(solution)/shard_map/all_to_all | solution.py:292
  27.6 45.9 %copy-start.10 = (s32[8,8]{1,0:T(8,128)S(1)}, s32[8,8]{1,0:T(8,128)}, u32[]{:S(2)}) copy-start(s32[8,8]{1,0:T(8,128)} %path.1) | copy-start | bytes 772
  31.4 1.0 copy-start.3
  44.9 1.2 copy-start.4
  73.5 32.9 %copy-start.14 = (s32[8,1]{0,1:T(1,128)S(1)}, s32[8,1]{0,1:T(1,128)}, u32[]{:S(2)}) copy-start(s32[8,1]{0,1:T(1,128)} %param.19) | copy-start | bytes 100
  73.5 32.9 %copy-start.12 = (s32[8]{0:T(128)S(1)}, s32[8]{0:T(128)}, u32[]{:S(2)}) copy-start(s32[8]{0:T(128)} %counts.1) | copy-start | bytes 100
  88.6 1.6 %copy-start.2 = (bf16[8192,128]{1,0:T(8,128)(2,1)S(1)}, bf16[8192,128]{1,0:T(8,128)(2,1)}, u32[]{:S(2)}) copy-start(bf16[8192,128]{1,0:T(8,128)(2,1)} %all-gather.3.cloned.1.call-done) | copy-start | bytes 6291460
  91.4 27.0 %all-to-all-start.3 = ((f32[64,8,128]{2,1,0:T(8,128)}), f32[64,8,128]{2,1,0:T(8,128)S(1)}, u32[]{:S(2)}, u32[]{:S(2)}) async-start(f32[64,8,128]{2,1,0:T(8,128)} %project.1), calls=%async_computation.3 | async-start | bytes 524288 | tf_op jit(solution)/shard_map/all_to_all | solution.py:337
Sparse Core Ops, SparseCore 0:
  10.2 39.7 all-gather.2

commit v3 on v2

--- a/solution.py
+++ b/solution.py
@@ -20,8 +20,7 @@
 CHIPS = 32
 TAIL = 8
 BLOCK = 64 + TAIL
-GATHERED = 64 + 2 * PATH_ROWS
-NEIGHBOURS = 8
+NEIGHBOURS = 4
 DEAD = -1e30
 FLOOR = -1e28
 LOG2E = 1.4426950408889634
@@ -48,7 +47,7 @@
     return (lax.axis_index("x") * 8 + lax.axis_index("y")) * 2 + lax.axis_index("core")
 
 
-def pack_kernel(where, table, pool, node, send, node_pad, sems):
+def pack_kernel(where, table, pool, node, query, send, message, node_pad, sems):
     other = HALF * (1 - where[0])
     copies = []
     for r in range(HALF):
@@ -65,6 +64,10 @@
     node_pad[...] = jnp.concatenate([rows, jnp.zeros_like(rows)], axis=0).astype(BF16)
     last = pltpu.make_async_copy(node_pad, send.at[pl.ds(NODE_ROWS0, 16), :], sems.at[32])
     last.start()
+    for half in range(2):
+        rows = query[half]
+        for chip in range(CHIPS):
+            message[2 * chip + half] = rows
     for c in copies:
         c.wait()
     last.wait()
@@ -193,10 +196,10 @@
         total = total + share
         mixed = mixed + share * got[s].astype(F32)[:64]
     mixed = mixed * (1.0 / total)
-    tail_row = iota((2 * PATH_ROWS, HEAD), 0)
-    tail = jnp.zeros((2 * PATH_ROWS, HEAD), F32)
-    for j in range(PATH_ROWS):
-        node = path[y, j]
+    tail_row = iota((TAIL, HEAD), 0)
+    tail = jnp.zeros((TAIL, HEAD), F32)
+    for j in range(HALF):
+        node = path[y, HALF * core + j]
         held = got[node // 2].astype(F32)[64:BLOCK]
         is_own = node % 2 == core
         key = jnp.where(is_own, held[3:4], held[5:6])
@@ -204,25 +207,38 @@
         tail = jnp.where(tail_row == 2 * j, key, tail)
         tail = jnp.where(tail_row == 2 * j + 1, value, tail)
     block = jnp.concatenate([mixed, tail], axis=0).astype(BF16)
-    for s in range(8):
+    for s in range(16):
         out[s] = block
 
 
-def project_kernel(got, weights, out):
-    a = got[...][:, :64, :].reshape(LANES, HEAD)
+def project_kernel(where, got, w0, w1, w2, w3, out):
+    x = where[1] // 16
+    held = got[...].reshape(8, 2, BLOCK, HEAD)
+    weights = (w0, w1, w2, w3)
     for pair in range(NEIGHBOURS // 2):
-        sums = None
+        wide = []
         for h in range(2):
             cols = []
             for n in (2 * pair, 2 * pair + 1):
-                rows = [weights[n, (2 * p + h) * HEAD : (2 * p + h + 1) * HEAD, :] for p in range(4)]
+                rows = [weights[n][(2 * p + h) * HEAD : (2 * p + h + 1) * HEAD, :] for p in range(4)]
                 cols.append(jnp.concatenate(rows, axis=0))
-            part = dot(a, jnp.concatenate(cols, axis=1), 0, 0)[h * NODES : (h + 1) * NODES]
-            sums = part if sums is None else sums + part
-        for t in range(8):
-            rows = sums[t * 8 : t * 8 + 8]
-            out[2 * pair * 8 + t] = rows[:, :HEAD]
-            out[(2 * pair + 1) * 8 + t] = rows[:, HEAD:]
+            wide.append(jnp.concatenate(cols, axis=1))
+        for k in range(2):
+            a = held[:, k, :64, :].reshape(LANES, HEAD)
+            sums = dot(a, wide[0], 0, 0)[:NODES] + dot(a, wide[1], 0, 0)[NODES:]
+            for n in range(2):
+                to = lax.rem(x + 2 * pair + n, NEIGHBOURS)
+                for t in range(8):
+                    out[to * 8 + t, k] = sums[t * 8 : t * 8 + 8, n * HEAD : (n + 1) * HEAD]
+
+
+def sum_kernel(got, out):
+    for x in range(NEIGHBOURS):
+        total = got[x * 8]
+        for t in range(1, 8):
+            total = total + got[x * 8 + t]
+        out[x] = total[0]
+        out[HALF + x] = total[1]
 
 
 def write_kernel(where, table, lengths, counts, spare, table_v, got, pool_in, pool, new_table, pages, sems):
@@ -255,9 +271,10 @@
                 fetch.start()
                 fetch.wait()
                 now = pages[2 * r + step].astype(F32)
-                held = got[r].astype(F32)[64:GATHERED]
                 for j in range(PATH_ROWS):
-                    new = jnp.concatenate([held[2 * j : 2 * j + 1], held[2 * j + 1 : 2 * j + 2]], axis=1)
+                    held = got[2 * r + j // HALF].astype(F32)[64:BLOCK]
+                    at = 2 * (j % HALF)
+                    new = jnp.concatenate([held[at : at + 1], held[at + 1 : at + 2]], axis=1)
                     now = jnp.where((row == first + j) & (j < count), new, now)
                 pages[2 * r + step] = now.astype(BF16)
                 store = pltpu.make_async_copy(pages.at[2 * r + step], pool.at[target], sems.at[2 * r + step])
@@ -274,21 +291,19 @@
     shape = jax.ShapeDtypeStruct
     where = jnp.stack([lax.axis_index("core"), ctx_index()]).astype(jnp.int32)
     node = node_kv.reshape(REQUESTS, 2 * HEAD)
-    weights = lax.all_gather(out_weight, ("x", "core"), axis=0)
-
-    send = pl.pallas_call(
+    held_pool = pltpu.with_memory_space_constraint(pool, HBM)
+
+    send, message = pl.pallas_call(
         pack_kernel,
-        out_shape=shape((SEND_ROWS, 2 * HEAD), BF16),
-        in_specs=[spec(SMEM), spec(SMEM), spec(HBM), spec(VMEM)],
-        out_specs=spec(pl.ANY),
+        out_shape=(shape((SEND_ROWS, 2 * HEAD), BF16), shape((2 * CHIPS, HALF * 8, HEAD), BF16)),
+        in_specs=[spec(SMEM), spec(SMEM), spec(HBM), spec(VMEM), spec(VMEM)],
+        out_specs=(spec(pl.ANY), spec(VMEM)),
         scratch_shapes=[VMEM((16, 2 * HEAD), BF16), pltpu.SemaphoreType.DMA((33,))],
         compiler_params=params,
         name="pack",
-    )(where, table, pool, node)
+    )(where, table, held_pool, node, queries.reshape(2, HALF * 8, HEAD))
     peer = lax.ppermute(send, "core", [(0, 1), (1, 0)])
 
-    by_core = queries.reshape(2, HALF * 8, HEAD)
-    message = jnp.broadcast_to(by_core[None], (CHIPS, 2, HALF * 8, HEAD)).reshape(2 * CHIPS, HALF * 8, HEAD)
     every_query = lax.all_to_all(message, ("x", "y", "core"), 0, 0, tiled=True)
 
     own, pool_copy, mask = pl.pallas_call(
@@ -304,7 +319,13 @@
         compiler_params=params,
         cost_estimate=pl.CostEstimate(flops=50_000_000, bytes_accessed=7_000_000, transcendentals=0),
         name="prepare",
-    )(where, table, pool, parents)
+    )(where, table, held_pool, parents)
+    mask, weight = lax.optimization_barrier((mask, out_weight))
+    weights = [weight]
+    for step in range(1, NEIGHBOURS):
+        ring = [((i + step) % NEIGHBOURS, i) for i in range(NEIGHBOURS)]
+        weights.append(lax.ppermute(weight, "x", ring))
+    mask, *weights = lax.optimization_barrier((mask, *weights))
 
     partial = pl.pallas_call(
         attend_kernel,
@@ -318,25 +339,31 @@
     parts = lax.all_to_all(partial, ("x", "y"), 0, 0, tiled=True)
     mixed = pl.pallas_call(
         combine_kernel,
-        out_shape=shape((8, GATHERED, HEAD), BF16),
+        out_shape=shape((16, BLOCK, HEAD), BF16),
         in_specs=[spec(SMEM), spec(SMEM), spec(VMEM)],
         out_specs=spec(VMEM),
         compiler_params=params,
         name="combine",
     )(where, path, parts)
-    attention = lax.all_to_all(mixed, "y", 0, 0, tiled=True)
+    attention = lax.all_to_all(mixed, ("y", "core"), 0, 0, tiled=True)
 
     sums = pl.pallas_call(
         project_kernel,
-        out_shape=shape((64, 8, HEAD), F32),
-        in_specs=[spec(VMEM), spec(VMEM)],
+        out_shape=shape((32, 2, 8, HEAD), F32),
+        in_specs=[spec(SMEM)] + [spec(VMEM)] * 5,
         out_specs=spec(VMEM),
         compiler_params=params,
         name="project",
-    )(attention, weights)
-    shares = lax.all_to_all(sums, ("x", "core", "tp"), 0, 0, tiled=True)
-    summed = jnp.sum(shares.reshape(4, 2, 8, 8, HEAD), axis=2)
-    projected = jnp.swapaxes(summed, 0, 1).reshape(REQUESTS, 8, HEAD)
+    )(where, attention, *weights)
+    shares = lax.all_to_all(sums, ("x", "tp"), 0, 0, tiled=True)
+    projected = pl.pallas_call(
+        sum_kernel,
+        out_shape=shape((REQUESTS, 8, HEAD), F32),
+        in_specs=[spec(VMEM)],
+        out_specs=spec(VMEM),
+        compiler_params=params,
+        name="sum",
+    )(shares)
 
     updated_pool, new_table = pl.pallas_call(
         write_kernel,

time: 127 us -> 223 us (1.76)
  Pallas kernels: 16.4 us -> 119 us
  between operations: 14.2 us -> 0.83 us
  blocking collectives: 34.6 us -> 42.5 us
  starting transfers between devices: 28.6 us -> 34.5 us
  local copies, waits for them, and re-layouts: 8.53 us -> 2.93 us
    pallas_call x1, Pallas kernels: 3.78 us -> 73.5 us  [on_device(): pl.pallas_call(prepare_kernel, out_shape=(shape((HALF * SPAN, 2 * HEAD),...]
    pallas_call x3 -> x4, Pallas kernels: 3.85 us -> 37.8 us  [the longest x1 34.6 us: on_device(): pl.pallas_call(pack_kernel, out_shape=(shape((SEND_ROWS, 2 * HEAD), BF16)...]
    all_to_all x1, waiting for transfers between devices: 12.5 us -> 0.01 us  [on_device(): every_query = lax.all_to_all(message, ('x', 'y', 'core'), 0, 0, tiled=True)]
    ppermute x0 -> x3, waiting for transfers between devices: none -> 12.4 us  [on_device(): weights.append(lax.ppermute(weight, 'x', ring))]
    ppermute x0 -> x3, starting transfers between devices: none -> 9.57 us  [on_device(): weights.append(lax.ppermute(weight, 'x', ring))]
    all_to_all x1, blocking collectives: 14.3 us -> 20.5 us  [on_device(): attention = lax.all_to_all(mixed, ('y', 'core'), 0, 0, tiled=True)]
    unnamed x31 -> x25, local copies, waits for them, and re-layouts: 6.98 us -> 2.2 us
    all_to_all x1, starting transfers between devices: 14.9 us -> 11.3 us  [on_device(): shares = lax.all_to_all(sums, ('x', 'tp'), 0, 0, tiled=True)]
  transfers between devices with their start and end apart: 4 -> 6, of which waited for: 2 -> 3; matrix products, arithmetic and copies ran while one was open for 1% -> 0% of each run, Pallas kernels for 12% -> 34%
where the time goes in v3:
time: 223 us; the launch traced here: 222 us
  Pallas kernels  119 us (53%)
  blocking collectives  42.5 us (19%)
  starting transfers between devices  34.5 us (15%)
  waiting for transfers between devices  21.6 us (10%)
  local copies, waits for them, and re-layouts  2.93 us (1%)
    pallas_call x1, Pallas kernels, on_device(): pl.pallas_call(prepare_kernel, out_shape=(shape((HALF * SPAN, 2 * HEAD),...  73.5 us
    pallas_call x1, Pallas kernels, on_device(): pl.pallas_call(pack_kernel, out_shape=(shape((SEND_ROWS, 2 * HEAD), BF16)...  34.6 us
    all_to_all x1, blocking collectives, on_device(): parts = lax.all_to_all(partial, ('x', 'y'), 0, 0, tiled=True)  22 us
    all_to_all x1, blocking collectives, on_device(): attention = lax.all_to_all(mixed, ('y', 'core'), 0, 0, tiled=True)  20.5 us
    ppermute x3, waiting for transfers between devices, on_device(): weights.append(lax.ppermute(weight, 'x', ring))  12.4 us
    all_to_all x1, starting transfers between devices, on_device(): shares = lax.all_to_all(sums, ('x', 'tp'), 0, 0, tiled=True)  11.3 us
    ppermute x3, starting transfers between devices, on_device(): weights.append(lax.ppermute(weight, 'x', ring))  9.57 us
    all_to_all x1, waiting for transfers between devices, on_device(): shares = lax.all_to_all(sums, ('x', 'tp'), 0, 0, tiled=True)  9.26 us
  transfers between devices with their start and end apart: 6, of which 3 were waited for; matrix products, arithmetic and copies ran while one was open for 0% of the time, Pallas kernels for 34%

profile of v3, /device:TPU:1, one launch (start us, length us, event | category | flops | bytes accessed | tf_op | source)
XLA Modules:
  0.0 221.7 jit_solution(4944316929546981272)
XLA Ops:
  0.7 0.7 reshape.13.query
  1.4 0.1 pad_add_fusion.where
  1.5 0.7 copy-done.3
  2.2 0.7 copy-done.5
  2.9 34.6 %pack.1 = (bf16[2064,256]{1,0:T(8,128)(2,1)}, bf16[64,32,128]{2,1,0:T(8,128)(2,1)}) custom-call(s32[2]{0:T(128)S(1)} %pad_add_fusion.where, s32[8,8]{1,0:T(8,128)S(1)} %copy-done.3, bf16[72,64,256]{2,1,0:T(8,128)(2,1)} %pool.3, bf16[8,256]{1,0:T(8,128)(2,1)S(1)} %bitcast.5, bf16[2,32,128]{2,1,0:T(8,128)(2,1)S(1)} %reshape.13.query), custom_call_target="tpu_custom_call" | custom-call | tf_op jit(solution)/shard_map/pack/pallas_call | solution.py:296
  37.5 8.8 %collective-permute-start = (bf16[2064,256]{1,0:T(8,128)(2,1)}, bf16[2064,256]{1,0:T(8,128)(2,1)S(1)}, u32[]{:S(2)}, u32[]{:S(2)}) collective-permute-start(bf16[2064,256]{1,0:T(8,128)(2,1)} %get-tuple-element.19), channel_id=1, source_target_pairs={{0,8},{8,0},{1,9},{9,1},{2,10},{10,2},{3,11},{11,3},{4,12},{12,4},... | collective-permute-start | bytes 3170312 | tf_op jit(solution)/shard_map/ppermute | solution.py:305
  46.3 4.9 %all-to-all-start = ((bf16[64,32,128]{2,1,0:T(8,128)(2,1)}), bf16[64,32,128]{2,1,0:T(8,128)(2,1)S(1)}, u32[]{:S(2)}, u32[]{:S(2)}) async-start(bf16[64,32,128]{2,1,0:T(8,128)(2,1)} %get-tuple-element.17), calls=%async_computation | async-start | bytes 1048576 | tf_op jit(solution)/shard_map/all_to_all | solution.py:307
  51.2 73.5 %prepare.1 = (bf16[2048,256]{1,0:T(8,128)(2,1)S(1)}, bf16[72,64,256]{2,1,0:T(8,128)(2,1)}, f32[4,16,128]{2,1,0:T(8,128)S(1)}) custom-call(s32[2]{0:T(128)S(1)} %pad_add_fusion.where, s32[8,8]{1,0:T(8,128)S(1)} %copy-done.4, bf16[72,64,256]{2,1,0:T(8,128)(2,1)} %pool.3, s32[8,64]{1,0:T(8,128)S(1)} %copy-done.7), custom_call_target="tpu_custom_call" | custom-call | flops 50000000 | bytes 7000000 | tf_op jit(solution)/shard_map/prepare/pallas_call | solution.py:309
  124.7 4.7 %collective-permute-start.1 = (bf16[1024,128]{1,0:T(8,128)(2,1)S(1)}, bf16[1024,128]{1,0:T(8,128)(2,1)S(1)}, u32[]{:S(2)}, u32[]{:S(2)}) collective-permute-start(bf16[1024,128]{1,0:T(8,128)(2,1)S(1)} %copy-done), channel_id=1, source_target_pairs={{128,0},{256,128},{384,256},{0,384},{129,1},{257,129},{385,257},{1... | collective-permute-start | bytes 786440 | tf_op jit(solution)/shard_map/ppermute | solution.py:327
  129.4 2.3 %collective-permute-start.2 = (bf16[1024,128]{1,0:T(8,128)(2,1)S(1)}, bf16[1024,128]{1,0:T(8,128)(2,1)S(1)}, u32[]{:S(2)}, u32[]{:S(2)}) collective-permute-start(bf16[1024,128]{1,0:T(8,128)(2,1)S(1)} %copy-done), channel_id=1, source_target_pairs={{256,0},{384,128},{0,256},{128,384},{257,1},{385,129},{1,257},{129... | collective-permute-start | bytes 786440 | tf_op jit(solution)/shard_map/ppermute | solution.py:327
  131.7 2.6 %collective-permute-start.3 = (bf16[1024,128]{1,0:T(8,128)(2,1)S(1)}, bf16[1024,128]{1,0:T(8,128)(2,1)S(1)}, u32[]{:S(2)}, u32[]{:S(2)}) collective-permute-start(bf16[1024,128]{1,0:T(8,128)(2,1)S(1)} %copy-done), channel_id=1, source_target_pairs={{384,0},{0,128},{128,256},{256,384},{385,1},{1,129},{129,257},{257... | collective-permute-start | bytes 786440 | tf_op jit(solution)/shard_map/ppermute | solution.py:327
  134.3 5.9 %collective-permute-done.1.w1 = bf16[1024,128]{1,0:T(8,128)(2,1)S(1)} collective-permute-done((bf16[1024,128]{1,0:T(8,128)(2,1)S(1)}, bf16[1024,128]{1,0:T(8,128)(2,1)S(1)}, u32[]{:S(2)}, u32[]{:S(2)}) %collective-permute-start.1) | collective-permute-done | bytes 262176 | tf_op jit(solution)/shard_map/ppermute | solution.py:327
  140.2 6.5 %collective-permute-done.3.w3 = bf16[1024,128]{1,0:T(8,128)(2,1)S(1)} collective-permute-done((bf16[1024,128]{1,0:T(8,128)(2,1)S(1)}, bf16[1024,128]{1,0:T(8,128)(2,1)S(1)}, u32[]{:S(2)}, u32[]{:S(2)}) %collective-permute-start.3) | collective-permute-done | bytes 262176 | tf_op jit(solution)/shard_map/ppermute | solution.py:327
  146.7 0.7 copy-done.1
  147.4 6.4 %attend.1 = bf16[32,72,128]{2,1,0:T(8,128)(2,1)S(1)} custom-call(s32[2]{0:T(128)S(1)} %pad_add_fusion.where, s32[8]{0:T(128)S(1)} %copy-done.9, bf16[64,32,128]{2,1,0:T(8,128)(2,1)S(1)} %all-to-all-done.queries, bf16[2048,256]{1,0:T(8,128)(2,1)S(1)} %get-tuple-element.18.own, bf16[2064,256]{1,0:T(8,128)(2,1)S(1)} %collective-permute-done.peer, ...), custom_call_target="tpu_custom_call" | custom-call | tf_op jit(solution)/shard_map/attend/pallas_call | solution.py:330
  153.8 22.0 %all_to_all.20.got = bf16[32,72,128]{2,1,0:T(8,128)(2,1)S(1)} all-to-all(bf16[32,72,128]{2,1,0:T(8,128)(2,1)S(1)} %attend.1), channel_id=1, replica_groups=mesh['x'=4,'y'=8,'core'=2,'tp'=8] {'x','y'}, dimensions={0} | all-to-all | bytes 1179648 | tf_op jit(solution)/shard_map/all_to_all | solution.py:339
  175.8 0.8 combine.1
  176.6 20.5 %all_to_all.21.got = bf16[16,72,128]{2,1,0:T(8,128)(2,1)S(1)} all-to-all(bf16[16,72,128]{2,1,0:T(8,128)(2,1)S(1)} %combine.1), channel_id=1, replica_groups=mesh['x'=4,'y'=8,'core'=2,'tp'=8] {'y','core'}, dimensions={0} | all-to-all | bytes 589824 | tf_op jit(solution)/shard_map/all_to_all | solution.py:348
  197.1 1.7 project.1
  198.8 11.3 %all-to-all-start.3 = ((f32[32,2,8,128]{3,2,1,0:T(8,128)}), f32[32,2,8,128]{3,2,1,0:T(8,128)S(1)}, u32[]{:S(2)}, u32[]{:S(2)}) async-start(f32[32,2,8,128]{3,2,1,0:T(8,128)} %project.1), calls=%async_computation.3 | async-start | bytes 524288 | tf_op jit(solution)/shard_map/all_to_all | solution.py:358
  210.1 0.1 copy.14.spare
  210.2 1.7 write.1
  211.8 9.3 %all-to-all-done.3.got = f32[32,2,8,128]{3,2,1,0:T(8,128)S(1)} async-done(((f32[32,2,8,128]{3,2,1,0:T(8,128)}), f32[32,2,8,128]{3,2,1,0:T(8,128)S(1)}, u32[]{:S(2)}, u32[]{:S(2)}) %all-to-all-start.3) | async-done | bytes 262176 | tf_op jit(solution)/shard_map/all_to_all | solution.py:358
  221.1 0.6 sum.1
  (24 shorter events, 0.1 us)
Async XLA Ops:
  0.6 50.5 %copy-start.4 = (s32[8,8]{1,0:T(8,128)S(1)}, s32[8,8]{1,0:T(8,128)}, u32[]{:S(2)}) copy-start(s32[8,8]{1,0:T(8,128)} %table_v.1) | copy-start | bytes 772
  0.6 50.5 %copy-start.7 = (s32[8,64]{1,0:T(8,128)S(1)}, s32[8,64]{1,0:T(8,128)}, u32[]{:S(2)}) copy-start(s32[8,64]{1,0:T(8,128)} %parents.1) | copy-start | bytes 6148
  1.5 0.7 copy-start.3
  2.2 0.7 copy-start.5
  2.9 121.9 %copy-start = (bf16[1024,128]{1,0:T(8,128)(2,1)S(1)}, bf16[1024,128]{1,0:T(8,128)(2,1)}, u32[]{:S(2)}) copy-start(bf16[1024,128]{1,0:T(8,128)(2,1)} %w0) | copy-start | bytes 786436
  2.9 144.5 %copy-start.6 = (bf16[8,1,256]{2,0,1:T(8,128)(2,1)S(1)}, bf16[8,1,256]{2,0,1:T(8,128)(2,1)}, u32[]{:S(2)}) copy-start(bf16[8,1,256]{2,0,1:T(8,128)(2,1)} %param.11) | copy-start | bytes 12292
  2.9 144.5 %copy-start.9 = (s32[8]{0:T(128)S(1)}, s32[8]{0:T(128)}, u32[]{:S(2)}) copy-start(s32[8]{0:T(128)} %lengths.3) | copy-start | bytes 100
  37.5 109.9 %collective-permute-start = (bf16[2064,256]{1,0:T(8,128)(2,1)}, bf16[2064,256]{1,0:T(8,128)(2,1)S(1)}, u32[]{:S(2)}, u32[]{:S(2)}) collective-permute-start(bf16[2064,256]{1,0:T(8,128)(2,1)} %get-tuple-element.19), channel_id=1, source_target_pairs={{0,8},{8,0},{1,9},{9,1},{2,10},{10,2},{3,11},{11,3},{4,12},{12,4},... | collective-permute-start | bytes 3170312 | tf_op jit(solution)/shard_map/ppermute | solution.py:305
  46.3 101.1 %all-to-all-start = ((bf16[64,32,128]{2,1,0:T(8,128)(2,1)}), bf16[64,32,128]{2,1,0:T(8,128)(2,1)S(1)}, u32[]{:S(2)}, u32[]{:S(2)}) async-start(bf16[64,32,128]{2,1,0:T(8,128)(2,1)} %get-tuple-element.17), calls=%async_computation | async-start | bytes 1048576 | tf_op jit(solution)/shard_map/all_to_all | solution.py:307
  124.7 51.1 %copy-start.8 = (s32[8,8]{1,0:T(8,128)S(1)}, s32[8,8]{1,0:T(8,128)}, u32[]{:S(2)}) copy-start(s32[8,8]{1,0:T(8,128)} %path.1) | copy-start | bytes 772
  124.7 15.5 %collective-permute-start.1 = (bf16[1024,128]{1,0:T(8,128)(2,1)S(1)}, bf16[1024,128]{1,0:T(8,128)(2,1)S(1)}, u32[]{:S(2)}, u32[]{:S(2)}) collective-permute-start(bf16[1024,128]{1,0:T(8,128)(2,1)S(1)} %copy-done), channel_id=1, source_target_pairs={{128,0},{256,128},{384,256},{0,384},{129,1},{257,129},{385,257},{1... | collective-permute-start | bytes 786440 | tf_op jit(solution)/shard_map/ppermute | solution.py:327
  129.4 10.8 %collective-permute-start.2 = (bf16[1024,128]{1,0:T(8,128)(2,1)S(1)}, bf16[1024,128]{1,0:T(8,128)(2,1)S(1)}, u32[]{:S(2)}, u32[]{:S(2)}) collective-permute-start(bf16[1024,128]{1,0:T(8,128)(2,1)S(1)} %copy-done), channel_id=1, source_target_pairs={{256,0},{384,128},{0,256},{128,384},{257,1},{385,129},{1,257},{129... | collective-permute-start | bytes 786440 | tf_op jit(solution)/shard_map/ppermute | solution.py:327
  131.7 15.0 %collective-permute-start.3 = (bf16[1024,128]{1,0:T(8,128)(2,1)S(1)}, bf16[1024,128]{1,0:T(8,128)(2,1)S(1)}, u32[]{:S(2)}, u32[]{:S(2)}) collective-permute-start(bf16[1024,128]{1,0:T(8,128)(2,1)S(1)} %copy-done), channel_id=1, source_target_pairs={{384,0},{0,128},{128,256},{256,384},{385,1},{1,129},{129,257},{257... | collective-permute-start | bytes 786440 | tf_op jit(solution)/shard_map/ppermute | solution.py:327
  146.7 0.7 copy-start.1
  147.4 49.7 %copy-start.2 = (bf16[1024,128]{1,0:T(8,128)(2,1)S(1)}, bf16[1024,128]{1,0:T(8,128)(2,1)}, u32[]{:S(2)}) copy-start(bf16[1024,128]{1,0:T(8,128)(2,1)} %copy-done.1) | copy-start | bytes 786436
  153.8 56.3 %copy-start.11 = (s32[8,1]{0,1:T(1,128)S(1)}, s32[8,1]{0,1:T(1,128)}, u32[]{:S(2)}) copy-start(s32[8,1]{0,1:T(1,128)} %param.19) | copy-start | bytes 100
  153.8 56.4 %copy-start.10 = (s32[8]{0:T(128)S(1)}, s32[8]{0:T(128)}, u32[]{:S(2)}) copy-start(s32[8]{0:T(128)} %counts.1) | copy-start | bytes 100
  198.8 22.3 %all-to-all-start.3 = ((f32[32,2,8,128]{3,2,1,0:T(8,128)}), f32[32,2,8,128]{3,2,1,0:T(8,128)S(1)}, u32[]{:S(2)}, u32[]{:S(2)}) async-start(f32[32,2,8,128]{3,2,1,0:T(8,128)} %project.1), calls=%async_computation.3 | async-start | bytes 524288 | tf_op jit(solution)/shard_map/all_to_all | solution.py:358

commit v4 on v3

--- a/solution.py
+++ b/solution.py
@@ -47,8 +47,12 @@
     return (lax.axis_index("x") * 8 + lax.axis_index("y")) * 2 + lax.axis_index("core")
 
 
-def pack_kernel(where, table, pool, node, query, send, message, node_pad, sems):
-    other = HALF * (1 - where[0])
+def position():
+    return lax.axis_index("core"), ctx_index()
+
+
+def pack_kernel(table, pool, node, query, send, message, sems):
+    other = HALF * (1 - lax.axis_index("core"))
     copies = []
     for r in range(HALF):
         for p in range(PAGES_LOCAL):
@@ -61,21 +65,21 @@
     for c in copies:
         c.start()
     rows = node[...].astype(F32)
-    node_pad[...] = jnp.concatenate([rows, jnp.zeros_like(rows)], axis=0).astype(BF16)
-    last = pltpu.make_async_copy(node_pad, send.at[pl.ds(NODE_ROWS0, 16), :], sems.at[32])
-    last.start()
+    send[pl.ds(NODE_ROWS0, 16), :] = jnp.concatenate([rows, jnp.zeros_like(rows)], axis=0).astype(BF16)
+    flat = query[...].astype(F32)
     for half in range(2):
-        rows = query[half]
+        rows = [
+            flat[r : r + 1, h * HEAD : (h + 1) * HEAD] for r in range(HALF * half, HALF * half + HALF) for h in range(8)
+        ]
+        rows = jnp.concatenate(rows, axis=0).astype(BF16)
         for chip in range(CHIPS):
             message[2 * chip + half] = rows
     for c in copies:
         c.wait()
-    last.wait()
-
-
-def prepare_kernel(where, table, pool, parents, own, pool_copy, mask, sems):
-    core = where[0]
-    ctx = where[1]
+
+
+def prepare_kernel(table, pool, parents, own, pool_copy, mask, held, sems):
+    core, ctx = position()
     copies = []
     for r in range(HALF):
         for p in range(PAGES_LOCAL):
@@ -85,7 +89,8 @@
                     pool.at[table[HALF * core + r, p]], own.at[pl.ds(n * PAGE, PAGE), :], sems.at[n]
                 )
             )
-    copies.append(pltpu.make_async_copy(pool, pool_copy, sems.at[32]))
+    fetch = pltpu.make_async_copy(pool, held, sems.at[32])
+    fetch.start()
     for c in copies:
         c.start()
     up = iota((NODES, NODES), 0)
@@ -106,13 +111,16 @@
         )
         seen = dot(pick.astype(F32).astype(BF16), reach[r]).astype(BF16)
         mask[r] = dot(seen, twice)
+    fetch.wait()
+    store = pltpu.make_async_copy(held, pool_copy, sems.at[33])
+    store.start()
     for c in copies:
         c.wait()
-
-
-def attend_kernel(where, lengths, queries, own, peer, node, mask, out):
-    core = where[0]
-    ctx = where[1]
+    store.wait()
+
+
+def attend_kernel(lengths, queries, own, peer, node, mask, out):
+    core, ctx = position()
     lane = iota((LANES, LANES), 1)
     order = (iota((LANES, LANES), 0) == (lane % NODES) * 8 + lane // NODES).astype(F32).astype(BF16)
     peer_node = peer[pl.ds(NODE_ROWS0, 16), :].astype(F32)[:REQUESTS]
@@ -179,9 +187,9 @@
             out[r * 8 + y] = block.astype(BF16)
 
 
-def combine_kernel(where, path, got, out):
-    core = where[0]
-    y = (where[1] // 2) % 8
+def combine_kernel(path, got, out):
+    core = lax.axis_index("core")
+    y = lax.axis_index("y")
     logs = []
     for s in range(CHIPS):
         tail = got[s].astype(F32)[64:BLOCK]
@@ -211,8 +219,8 @@
         out[s] = block
 
 
-def project_kernel(where, got, w0, w1, w2, w3, out):
-    x = where[1] // 16
+def project_kernel(got, w0, w1, w2, w3, out):
+    x = lax.axis_index("x")
     held = got[...].reshape(8, 2, BLOCK, HEAD)
     weights = (w0, w1, w2, w3)
     for pair in range(NEIGHBOURS // 2):
@@ -241,8 +249,8 @@
         out[HALF + x] = total[1]
 
 
-def write_kernel(where, table, lengths, counts, spare, table_v, got, pool_in, pool, new_table, pages, sems):
-    ctx = where[1]
+def write_kernel(table, lengths, counts, spare, table_v, got, pool_in, pool, new_table, pages, sems):
+    ctx = ctx_index()
     for r in range(REQUESTS):
         for p in range(PAGES_LOCAL):
             new_table[r, p] = table[r, p]
@@ -289,19 +297,21 @@
 def on_device(queries, node_kv, pool, out_weight, parents, path, counts, lengths, table, free_slot):
     params = pltpu.CompilerParams(vmem_limit_bytes=LIMIT)
     shape = jax.ShapeDtypeStruct
-    where = jnp.stack([lax.axis_index("core"), ctx_index()]).astype(jnp.int32)
     node = node_kv.reshape(REQUESTS, 2 * HEAD)
-    held_pool = pltpu.with_memory_space_constraint(pool, HBM)
+    held_pool, held_table, held_node, held_queries = (
+        pltpu.with_memory_space_constraint(a, HBM)
+        for a in (pool, table, node, queries.reshape(REQUESTS, 8 * HEAD))
+    )
 
     send, message = pl.pallas_call(
         pack_kernel,
-        out_shape=(shape((SEND_ROWS, 2 * HEAD), BF16), shape((2 * CHIPS, HALF * 8, HEAD), BF16)),
-        in_specs=[spec(SMEM), spec(SMEM), spec(HBM), spec(VMEM), spec(VMEM)],
-        out_specs=(spec(pl.ANY), spec(VMEM)),
-        scratch_shapes=[VMEM((16, 2 * HEAD), BF16), pltpu.SemaphoreType.DMA((33,))],
+        out_shape=(VMEM((SEND_ROWS, 2 * HEAD), BF16), VMEM((2 * CHIPS, HALF * 8, HEAD), BF16)),
+        in_specs=[spec(SMEM), spec(HBM), spec(VMEM), spec(VMEM)],
+        out_specs=(spec(VMEM), spec(VMEM)),
+        scratch_shapes=[pltpu.SemaphoreType.DMA((32,))],
         compiler_params=params,
         name="pack",
-    )(where, table, held_pool, node, queries.reshape(2, HALF * 8, HEAD))
+    )(held_table, held_pool, held_node, held_queries)
     peer = lax.ppermute(send, "core", [(0, 1), (1, 0)])
 
     every_query = lax.all_to_all(message, ("x", "y", "core"), 0, 0, tiled=True)
@@ -313,48 +323,48 @@
             shape(pool.shape, pool.dtype),
             shape((HALF, 16, 2 * NODES), F32),
         ),
-        in_specs=[spec(SMEM), spec(SMEM), spec(HBM), spec(VMEM)],
+        in_specs=[spec(SMEM), spec(HBM), spec(VMEM)],
         out_specs=(spec(VMEM), spec(HBM), spec(VMEM)),
-        scratch_shapes=[pltpu.SemaphoreType.DMA((33,))],
+        scratch_shapes=[VMEM(pool.shape, BF16), pltpu.SemaphoreType.DMA((34,))],
         compiler_params=params,
         cost_estimate=pl.CostEstimate(flops=50_000_000, bytes_accessed=7_000_000, transcendentals=0),
         name="prepare",
-    )(where, table, held_pool, parents)
-    mask, weight = lax.optimization_barrier((mask, out_weight))
+    )(table, held_pool, parents)
+
+    partial = pl.pallas_call(
+        attend_kernel,
+        out_shape=shape((CHIPS, BLOCK, HEAD), BF16),
+        in_specs=[spec(SMEM)] + [spec(VMEM)] * 5,
+        out_specs=spec(VMEM),
+        compiler_params=params,
+        name="attend",
+    )(lengths, every_query, own, peer, node, mask)
+
+    partial, weight = lax.optimization_barrier((partial, out_weight))
     weights = [weight]
     for step in range(1, NEIGHBOURS):
         ring = [((i + step) % NEIGHBOURS, i) for i in range(NEIGHBOURS)]
         weights.append(lax.ppermute(weight, "x", ring))
-    mask, *weights = lax.optimization_barrier((mask, *weights))
-
-    partial = pl.pallas_call(
-        attend_kernel,
-        out_shape=shape((CHIPS, BLOCK, HEAD), BF16),
-        in_specs=[spec(SMEM), spec(SMEM)] + [spec(VMEM)] * 5,
-        out_specs=spec(VMEM),
-        compiler_params=params,
-        name="attend",
-    )(where, lengths, every_query, own, peer, node, mask)
-
     parts = lax.all_to_all(partial, ("x", "y"), 0, 0, tiled=True)
+    parts, *weights = lax.optimization_barrier((parts, *weights))
     mixed = pl.pallas_call(
         combine_kernel,
         out_shape=shape((16, BLOCK, HEAD), BF16),
-        in_specs=[spec(SMEM), spec(SMEM), spec(VMEM)],
+        in_specs=[spec(SMEM), spec(VMEM)],
         out_specs=spec(VMEM),
         compiler_params=params,
         name="combine",
-    )(where, path, parts)
+    )(path, parts)
     attention = lax.all_to_all(mixed, ("y", "core"), 0, 0, tiled=True)
 
     sums = pl.pallas_call(
         project_kernel,
         out_shape=shape((32, 2, 8, HEAD), F32),
-        in_specs=[spec(SMEM)] + [spec(VMEM)] * 5,
+        in_specs=[spec(VMEM)] * 5,
         out_specs=spec(VMEM),
         compiler_params=params,
         name="project",
-    )(where, attention, *weights)
+    )(attention, *weights)
     shares = lax.all_to_all(sums, ("x", "tp"), 0, 0, tiled=True)
     projected = pl.pallas_call(
         sum_kernel,
@@ -368,13 +378,13 @@
     updated_pool, new_table = pl.pallas_call(
         write_kernel,
         out_shape=(shape(pool.shape, pool.dtype), shape(table.shape, table.dtype)),
-        in_specs=[spec(SMEM)] * 5 + [spec(VMEM), spec(VMEM), spec(HBM)],
+        in_specs=[spec(SMEM)] * 4 + [spec(VMEM), spec(VMEM), spec(HBM)],
         out_specs=(spec(HBM), spec(SMEM)),
-        input_output_aliases={7: 0},
+        input_output_aliases={6: 0},
         scratch_shapes=[VMEM((2 * REQUESTS, PAGE, 2 * HEAD), BF16), pltpu.SemaphoreType.DMA((2 * REQUESTS,))],
         compiler_params=params,
         name="write",
-    )(where, table, lengths, counts, free_slot, table, attention, pool_copy)
+    )(table, lengths, counts, free_slot, table, attention, pool_copy)
     return projected, updated_pool, new_table
 
 

time: 223 us -> 117 us (0.52)
  Pallas kernels: 119 us -> 19 us
  blocking collectives: 42.5 us -> 19.2 us
  waiting for transfers between devices: 21.6 us -> 35.2 us
  starting transfers between devices: 34.5 us -> 42.2 us
  local copies, waits for them, and re-layouts: 2.93 us -> 0.12 us
    pallas_call x1, Pallas kernels: 73.5 us -> 3.99 us  [on_device(): pl.pallas_call(prepare_kernel, out_shape=(shape((HALF * SPAN, 2 * HEAD),...]
    pallas_call x1, Pallas kernels: 34.6 us -> 3.5 us  [on_device(): pl.pallas_call(pack_kernel, out_shape=(VMEM((SEND_ROWS, 2 * HEAD), BF16),...]
    all_to_all x1 -> x0, blocking collectives: 22 us -> none  [on_device(): parts = lax.all_to_all(partial, ('x', 'y'), 0, 0, tiled=True)]
    all_to_all x1, waiting for transfers between devices: 0.01 us -> 13.3 us  [on_device(): every_query = lax.all_to_all(message, ('x', 'y', 'core'), 0, 0, tiled=True)]
    all_to_all x0 -> x1, starting transfers between devices: none -> 5.31 us  [on_device(): parts = lax.all_to_all(partial, ('x', 'y'), 0, 0, tiled=True)]
  transfers between devices with their start and end apart: 6 -> 7, of which waited for: 3 -> 5; matrix products, arithmetic and copies ran while one was open for 0% -> 0% of each run, Pallas kernels for 34% -> 5%
where the time goes in v4:
time: 117 us; the launch traced here: 116 us
  starting transfers between devices  42.2 us (36%)
  waiting for transfers between devices  35.2 us (30%)
  blocking collectives  19.2 us (16%)
  Pallas kernels  19 us (16%)
    all_to_all x1, blocking collectives, on_device(): attention = lax.all_to_all(mixed, ('y', 'core'), 0, 0, tiled=True)  19.2 us
    all_to_all x1, waiting for transfers between devices, on_device(): every_query = lax.all_to_all(message, ('x', 'y', 'core'), 0, 0, tiled=True)  13.3 us
    all_to_all x1, starting transfers between devices, on_device(): shares = lax.all_to_all(sums, ('x', 'tp'), 0, 0, tiled=True)  12.7 us
    ppermute x3, waiting for transfers between devices, on_device(): weights.append(lax.ppermute(weight, 'x', ring))  12.7 us
    ppermute x3, starting transfers between devices, on_device(): weights.append(lax.ppermute(weight, 'x', ring))  10.5 us
    all_to_all x1, waiting for transfers between devices, on_device(): shares = lax.all_to_all(sums, ('x', 'tp'), 0, 0, tiled=True)  9.25 us
    ppermute x1, starting transfers between devices, on_device(): peer = lax.ppermute(send, 'core', [(0, 1), (1, 0)])  8.86 us
    pallas_call x1, Pallas kernels, on_device(): pl.pallas_call(attend_kernel, out_shape=shape((CHIPS, BLOCK, HEAD), BF16)...  7.2 us
  transfers between devices with their start and end apart: 7, of which 5 were waited for; matrix products, arithmetic and copies ran while one was open for 0% of the time, Pallas kernels for 5%

profile of v4, /device:TPU:1, one launch (start us, length us, event | category | flops | bytes accessed | tf_op | source)
XLA Modules:
  0.0 116.5 jit_solution(6789477926191529991)
XLA Ops:
  0.7 3.5 %pack.1 = (bf16[2064,256]{1,0:T(8,128)(2,1)}, bf16[64,32,128]{2,1,0:T(8,128)(2,1)}) custom-call(s32[8,8]{1,0:T(8,128)} %table_v.1, bf16[72,64,256]{2,1,0:T(8,128)(2,1)} %pool.3, bf16[8,256]{1,0:T(8,128)(2,1)} %bitcast.2, bf16[8,1024]{1,0:T(8,128)(2,1)} %bitcast.4), custom_call_target="tpu_custom_call" | custom-call | tf_op jit(solution)/shard_map/pack/pallas_call | solution.py:306
  4.2 8.9 %collective-permute-start = (bf16[2064,256]{1,0:T(8,128)(2,1)}, bf16[2064,256]{1,0:T(8,128)(2,1)S(1)}, u32[]{:S(2)}, u32[]{:S(2)}) collective-permute-start(bf16[2064,256]{1,0:T(8,128)(2,1)} %get-tuple-element.19), channel_id=1, source_target_pairs={{0,8},{8,0},{1,9},{9,1},{2,10},{10,2},{3,11},{11,3},{4,12},{12,4},... | collective-permute-start | bytes 3170312 | tf_op jit(solution)/shard_map/ppermute | solution.py:315
  13.0 4.8 %all-to-all-start = ((bf16[64,32,128]{2,1,0:T(8,128)(2,1)}), bf16[64,32,128]{2,1,0:T(8,128)(2,1)S(1)}, u32[]{:S(2)}, u32[]{:S(2)}) async-start(bf16[64,32,128]{2,1,0:T(8,128)(2,1)} %get-tuple-element.17), calls=%async_computation | async-start | bytes 1048576 | tf_op jit(solution)/shard_map/all_to_all | solution.py:317
  17.9 4.0 %prepare.1 = (bf16[2048,256]{1,0:T(8,128)(2,1)S(1)}, bf16[72,64,256]{2,1,0:T(8,128)(2,1)}, f32[4,16,128]{2,1,0:T(8,128)S(1)}) custom-call(s32[8,8]{1,0:T(8,128)S(1)} %copy-done.1, bf16[72,64,256]{2,1,0:T(8,128)(2,1)} %pool.3, s32[8,64]{1,0:T(8,128)S(1)} %copy-done.3), custom_call_target="tpu_custom_call" | custom-call | flops 50000000 | bytes 7000000 | tf_op jit(solution)/shard_map/prepare/pallas_call | solution.py:319
  21.9 0.0 copy-start
  21.9 0.0 copy-start.4
  21.9 13.3 %all-to-all-done.queries = bf16[64,32,128]{2,1,0:T(8,128)(2,1)S(1)} async-done(((bf16[64,32,128]{2,1,0:T(8,128)(2,1)}), bf16[64,32,128]{2,1,0:T(8,128)(2,1)S(1)}, u32[]{:S(2)}, u32[]{:S(2)}) %all-to-all-start) | async-done | bytes 524320 | tf_op jit(solution)/shard_map/all_to_all | solution.py:317
  35.2 0.0 collective-permute-done.peer
  35.2 7.2 %attend.1 = bf16[32,72,128]{2,1,0:T(8,128)(2,1)} custom-call(s32[8]{0:T(128)S(1)} %copy-done.5, bf16[64,32,128]{2,1,0:T(8,128)(2,1)S(1)} %all-to-all-done.queries, bf16[2048,256]{1,0:T(8,128)(2,1)S(1)} %get-tuple-element.18.own, bf16[2064,256]{1,0:T(8,128)(2,1)S(1)} %collective-permute-done.peer, bf16[8,256]{1,0:T(8,128)(2,1)S(1)} %bitcast.3, ...), custom_call_target="tpu_custom_call" | custom-call | tf_op jit(solution)/shard_map/attend/pallas_call | solution.py:334
  42.4 5.3 %all-to-all-start.1 = ((bf16[32,72,128]{2,1,0:T(8,128)(2,1)}), bf16[32,72,128]{2,1,0:T(8,128)(2,1)S(1)}, u32[]{:S(2)}, u32[]{:S(2)}) async-start(bf16[32,72,128]{2,1,0:T(8,128)(2,1)} %attend.1), calls=%async_computation.1 | async-start | bytes 1179648 | tf_op jit(solution)/shard_map/all_to_all | solution.py:348
  47.7 3.1 %collective-permute-start.3 = (bf16[1024,128]{1,0:T(8,128)(2,1)S(1)}, bf16[1024,128]{1,0:T(8,128)(2,1)S(1)}, u32[]{:S(2)}, u32[]{:S(2)}) collective-permute-start(bf16[1024,128]{1,0:T(8,128)(2,1)S(1)} %copy-done), channel_id=1, source_target_pairs={{384,0},{0,128},{128,256},{256,384},{385,1},{1,129},{129,257},{257... | collective-permute-start | bytes 786440 | tf_op jit(solution)/shard_map/ppermute | solution.py:347
  50.9 4.3 %collective-permute-start.2 = (bf16[1024,128]{1,0:T(8,128)(2,1)S(1)}, bf16[1024,128]{1,0:T(8,128)(2,1)S(1)}, u32[]{:S(2)}, u32[]{:S(2)}) collective-permute-start(bf16[1024,128]{1,0:T(8,128)(2,1)S(1)} %copy-done), channel_id=1, source_target_pairs={{256,0},{384,128},{0,256},{128,384},{257,1},{385,129},{1,257},{129... | collective-permute-start | bytes 786440 | tf_op jit(solution)/shard_map/ppermute | solution.py:347
  55.2 3.1 %collective-permute-start.1 = (bf16[1024,128]{1,0:T(8,128)(2,1)S(1)}, bf16[1024,128]{1,0:T(8,128)(2,1)S(1)}, u32[]{:S(2)}, u32[]{:S(2)}) collective-permute-start(bf16[1024,128]{1,0:T(8,128)(2,1)S(1)} %copy-done), channel_id=1, source_target_pairs={{128,0},{256,128},{384,256},{0,384},{129,1},{257,129},{385,257},{1... | collective-permute-start | bytes 786440 | tf_op jit(solution)/shard_map/ppermute | solution.py:347
  58.3 5.4 %collective-permute-done.3.w3 = bf16[1024,128]{1,0:T(8,128)(2,1)S(1)} collective-permute-done((bf16[1024,128]{1,0:T(8,128)(2,1)S(1)}, bf16[1024,128]{1,0:T(8,128)(2,1)S(1)}, u32[]{:S(2)}, u32[]{:S(2)}) %collective-permute-start.3) | collective-permute-done | bytes 262176 | tf_op jit(solution)/shard_map/ppermute | solution.py:347
  63.6 5.7 %collective-permute-done.2.w2 = bf16[1024,128]{1,0:T(8,128)(2,1)S(1)} collective-permute-done((bf16[1024,128]{1,0:T(8,128)(2,1)S(1)}, bf16[1024,128]{1,0:T(8,128)(2,1)S(1)}, u32[]{:S(2)}, u32[]{:S(2)}) %collective-permute-start.2) | collective-permute-done | bytes 262176 | tf_op jit(solution)/shard_map/ppermute | solution.py:347
  69.4 1.6 %collective-permute-done.1.w1 = bf16[1024,128]{1,0:T(8,128)(2,1)S(1)} collective-permute-done((bf16[1024,128]{1,0:T(8,128)(2,1)S(1)}, bf16[1024,128]{1,0:T(8,128)(2,1)S(1)}, u32[]{:S(2)}, u32[]{:S(2)}) %collective-permute-start.1) | collective-permute-done | bytes 262176 | tf_op jit(solution)/shard_map/ppermute | solution.py:347
  71.0 0.8 combine.1
  71.8 19.2 %all_to_all.20.got = bf16[16,72,128]{2,1,0:T(8,128)(2,1)S(1)} all-to-all(bf16[16,72,128]{2,1,0:T(8,128)(2,1)S(1)} %combine.1), channel_id=1, replica_groups=mesh['x'=4,'y'=8,'core'=2,'tp'=8] {'y','core'}, dimensions={0} | all-to-all | bytes 589824 | tf_op jit(solution)/shard_map/all_to_all | solution.py:358
  90.9 1.2 %project.1 = f32[32,2,8,128]{3,2,1,0:T(8,128)} custom-call(bf16[16,72,128]{2,1,0:T(8,128)(2,1)S(1)} %all_to_all.20.got, bf16[1024,128]{1,0:T(8,128)(2,1)S(1)} %copy-done, bf16[1024,128]{1,0:T(8,128)(2,1)S(1)} %collective-permute-done.1.w1, bf16[1024,128]{1,0:T(8,128)(2,1)S(1)} %collective-permute-done.2.w2, bf16[1024,128]{1,0:T(8,128)(2,1)S(1)} %collective-permute-done.3.w3), custom_call_target="tpu_custom_call" | custom-call | tf_op jit(solution)/shard_map/project/pallas_call | solution.py:360
  92.1 12.7 %all-to-all-start.3 = ((f32[32,2,8,128]{3,2,1,0:T(8,128)}), f32[32,2,8,128]{3,2,1,0:T(8,128)S(1)}, u32[]{:S(2)}, u32[]{:S(2)}) async-start(f32[32,2,8,128]{3,2,1,0:T(8,128)} %project.1), calls=%async_computation.3 | async-start | bytes 524288 | tf_op jit(solution)/shard_map/all_to_all | solution.py:368
  104.8 0.1 copy.14.spare
  104.9 1.7 %write.1 = (bf16[72,64,256]{2,1,0:T(8,128)(2,1)}, s32[8,8]{1,0:T(8,128)}) custom-call(s32[8,8]{1,0:T(8,128)S(1)} %copy-done.1, s32[8]{0:T(128)S(1)} %copy-done.5, s32[8]{0:T(128)S(1)} %copy-done.6, s32[8,1]{1,0:T(8,128)S(1)} %copy.14.spare, s32[8,8]{1,0:T(8,128)S(1)} %copy-done.1, ...), custom_call_target="tpu_custom_call", output_to_operand_aliasing={{0}: (6, {})} | custom-call | tf_op jit(solution)/shard_map/write/pallas_call | solution.py:378
  106.6 9.3 %all-to-all-done.3.got = f32[32,2,8,128]{3,2,1,0:T(8,128)S(1)} async-done(((f32[32,2,8,128]{3,2,1,0:T(8,128)}), f32[32,2,8,128]{3,2,1,0:T(8,128)S(1)}, u32[]{:S(2)}, u32[]{:S(2)}) %all-to-all-start.3) | async-done | bytes 262176 | tf_op jit(solution)/shard_map/all_to_all | solution.py:368
  115.8 0.6 sum.1
  (15 shorter events, 0.0 us)
Async XLA Ops:
  0.6 17.2 %copy-start.1 = (s32[8,8]{1,0:T(8,128)S(1)}, s32[8,8]{1,0:T(8,128)}, u32[]{:S(2)}) copy-start(s32[8,8]{1,0:T(8,128)} %table_v.1) | copy-start | bytes 772
  0.6 17.2 %copy-start.3 = (s32[8,64]{1,0:T(8,128)S(1)}, s32[8,64]{1,0:T(8,128)}, u32[]{:S(2)}) copy-start(s32[8,64]{1,0:T(8,128)} %parents.1) | copy-start | bytes 6148
  0.7 34.5 %copy-start.2 = (bf16[8,1,256]{2,0,1:T(8,128)(2,1)S(1)}, bf16[8,1,256]{2,0,1:T(8,128)(2,1)}, u32[]{:S(2)}) copy-start(bf16[8,1,256]{2,0,1:T(8,128)(2,1)} %param.11) | copy-start | bytes 12292
  0.7 34.5 %copy-start.5 = (s32[8]{0:T(128)S(1)}, s32[8]{0:T(128)}, u32[]{:S(2)}) copy-start(s32[8]{0:T(128)} %lengths.3) | copy-start | bytes 100
  4.2 31.0 %collective-permute-start = (bf16[2064,256]{1,0:T(8,128)(2,1)}, bf16[2064,256]{1,0:T(8,128)(2,1)S(1)}, u32[]{:S(2)}, u32[]{:S(2)}) collective-permute-start(bf16[2064,256]{1,0:T(8,128)(2,1)} %get-tuple-element.19), channel_id=1, source_target_pairs={{0,8},{8,0},{1,9},{9,1},{2,10},{10,2},{3,11},{11,3},{4,12},{12,4},... | collective-permute-start | bytes 3170312 | tf_op jit(solution)/shard_map/ppermute | solution.py:315
  13.0 22.1 %all-to-all-start = ((bf16[64,32,128]{2,1,0:T(8,128)(2,1)}), bf16[64,32,128]{2,1,0:T(8,128)(2,1)S(1)}, u32[]{:S(2)}, u32[]{:S(2)}) async-start(bf16[64,32,128]{2,1,0:T(8,128)(2,1)} %get-tuple-element.17), calls=%async_computation | async-start | bytes 1048576 | tf_op jit(solution)/shard_map/all_to_all | solution.py:317
  21.9 25.8 %copy-start = (bf16[1024,128]{1,0:T(8,128)(2,1)S(1)}, bf16[1024,128]{1,0:T(8,128)(2,1)}, u32[]{:S(2)}) copy-start(bf16[1024,128]{1,0:T(8,128)(2,1)} %w0) | copy-start | bytes 786436
  21.9 49.1 %copy-start.4 = (s32[8,8]{1,0:T(8,128)S(1)}, s32[8,8]{1,0:T(8,128)}, u32[]{:S(2)}) copy-start(s32[8,8]{1,0:T(8,128)} %path.1) | copy-start | bytes 772
  42.4 62.4 %copy-start.7 = (s32[8,1]{0,1:T(1,128)S(1)}, s32[8,1]{0,1:T(1,128)}, u32[]{:S(2)}) copy-start(s32[8,1]{0,1:T(1,128)} %param.19) | copy-start | bytes 100
  42.4 62.5 %copy-start.6 = (s32[8]{0:T(128)S(1)}, s32[8]{0:T(128)}, u32[]{:S(2)}) copy-start(s32[8]{0:T(128)} %counts.1) | copy-start | bytes 100
  42.4 28.6 %all-to-all-start.1 = ((bf16[32,72,128]{2,1,0:T(8,128)(2,1)}), bf16[32,72,128]{2,1,0:T(8,128)(2,1)S(1)}, u32[]{:S(2)}, u32[]{:S(2)}) async-start(bf16[32,72,128]{2,1,0:T(8,128)(2,1)} %attend.1), calls=%async_computation.1 | async-start | bytes 1179648 | tf_op jit(solution)/shard_map/all_to_all | solution.py:348
  47.7 15.9 %collective-permute-start.3 = (bf16[1024,128]{1,0:T(8,128)(2,1)S(1)}, bf16[1024,128]{1,0:T(8,128)(2,1)S(1)}, u32[]{:S(2)}, u32[]{:S(2)}) collective-permute-start(bf16[1024,128]{1,0:T(8,128)(2,1)S(1)} %copy-done), channel_id=1, source_target_pairs={{384,0},{0,128},{128,256},{256,384},{385,1},{1,129},{129,257},{257... | collective-permute-start | bytes 786440 | tf_op jit(solution)/shard_map/ppermute | solution.py:347
  50.9 18.5 %collective-permute-start.2 = (bf16[1024,128]{1,0:T(8,128)(2,1)S(1)}, bf16[1024,128]{1,0:T(8,128)(2,1)S(1)}, u32[]{:S(2)}, u32[]{:S(2)}) collective-permute-start(bf16[1024,128]{1,0:T(8,128)(2,1)S(1)} %copy-done), channel_id=1, source_target_pairs={{256,0},{384,128},{0,256},{128,384},{257,1},{385,129},{1,257},{129... | collective-permute-start | bytes 786440 | tf_op jit(solution)/shard_map/ppermute | solution.py:347
  55.2 15.7 %collective-permute-start.1 = (bf16[1024,128]{1,0:T(8,128)(2,1)S(1)}, bf16[1024,128]{1,0:T(8,128)(2,1)S(1)}, u32[]{:S(2)}, u32[]{:S(2)}) collective-permute-start(bf16[1024,128]{1,0:T(8,128)(2,1)S(1)} %copy-done), channel_id=1, source_target_pairs={{128,0},{256,128},{384,256},{0,384},{129,1},{257,129},{385,257},{1... | collective-permute-start | bytes 786440 | tf_op jit(solution)/shard_map/ppermute | solution.py:347
  92.1 23.7 %all-to-all-start.3 = ((f32[32,2,8,128]{3,2,1,0:T(8,128)}), f32[32,2,8,128]{3,2,1,0:T(8,128)S(1)}, u32[]{:S(2)}, u32[]{:S(2)}) async-start(f32[32,2,8,128]{3,2,1,0:T(8,128)} %project.1), calls=%async_computation.3 | async-start | bytes 524288 | tf_op jit(solution)/shard_map/all_to_all | solution.py:368

commit v5 on v4

--- a/solution.py
+++ b/solution.py
@@ -20,14 +20,15 @@
 CHIPS = 32
 TAIL = 8
 BLOCK = 64 + TAIL
-NEIGHBOURS = 4
 DEAD = -1e30
 FLOOR = -1e28
 LOG2E = 1.4426950408889634
 SCALE2 = HEAD ** (-0.5) * LOG2E
 
-NODE_ROWS0 = HALF * SPAN
-SEND_ROWS = NODE_ROWS0 + 16
+SENDS = 2
+EACH = HALF // SENDS
+NODE_ROWS0 = EACH * SPAN
+W_ROWS = 512
 
 VMEM = pltpu.VMEM
 SMEM = pltpu.SMEM
@@ -51,21 +52,7 @@
     return lax.axis_index("core"), ctx_index()
 
 
-def pack_kernel(table, pool, node, query, send, message, sems):
-    other = HALF * (1 - lax.axis_index("core"))
-    copies = []
-    for r in range(HALF):
-        for p in range(PAGES_LOCAL):
-            n = r * PAGES_LOCAL + p
-            copies.append(
-                pltpu.make_async_copy(
-                    pool.at[table[other + r, p]], send.at[pl.ds(n * PAGE, PAGE), :], sems.at[n]
-                )
-            )
-    for c in copies:
-        c.start()
-    rows = node[...].astype(F32)
-    send[pl.ds(NODE_ROWS0, 16), :] = jnp.concatenate([rows, jnp.zeros_like(rows)], axis=0).astype(BF16)
+def message_kernel(query, message):
     flat = query[...].astype(F32)
     for half in range(2):
         rows = [
@@ -74,25 +61,35 @@
         rows = jnp.concatenate(rows, axis=0).astype(BF16)
         for chip in range(CHIPS):
             message[2 * chip + half] = rows
-    for c in copies:
-        c.wait()
-
-
-def prepare_kernel(table, pool, parents, own, pool_copy, mask, held, sems):
+
+
+def prepare_kernel(table, pool, node, parents, weight, send0, send1, own, pool_copy, mask, held, sems):
     core, ctx = position()
     copies = []
-    for r in range(HALF):
-        for p in range(PAGES_LOCAL):
-            n = r * PAGES_LOCAL + p
-            copies.append(
-                pltpu.make_async_copy(
-                    pool.at[table[HALF * core + r, p]], own.at[pl.ds(n * PAGE, PAGE), :], sems.at[n]
-                )
+    sends = (send0, send1)
+    for mine in range(2):
+        for r in range(HALF):
+            for p in range(PAGES_LOCAL):
+                slot = table[HALF * (core if mine else 1 - core) + r, p]
+                to, n = (own, r * PAGES_LOCAL + p) if mine else (sends[r // EACH], (r % EACH) * PAGES_LOCAL + p)
+                if not mine and r >= EACH:
+                    n += PAGES_LOCAL
+                at = mine * 32 + r * PAGES_LOCAL + p
+                copies.append(pltpu.make_async_copy(pool.at[slot], to.at[pl.ds(n * PAGE, PAGE), :], sems.at[at]))
+    for half in range(2):
+        copies.append(
+            pltpu.make_async_copy(
+                weight.at[pl.ds(half * W_ROWS, W_ROWS), :],
+                send1.at[pl.ds(0, W_ROWS), pl.ds(half * HEAD, HEAD)],
+                sems.at[66 + half],
             )
-    fetch = pltpu.make_async_copy(pool, held, sems.at[32])
-    fetch.start()
+        )
+    fetch = pltpu.make_async_copy(pool, held, sems.at[64])
     for c in copies:
         c.start()
+    fetch.start()
+    rows = node[...].astype(F32)
+    send0[pl.ds(NODE_ROWS0, 16), :] = jnp.concatenate([rows, jnp.zeros_like(rows)], axis=0).astype(BF16)
     up = iota((NODES, NODES), 0)
     down = iota((NODES, NODES), 1)
     twice = (iota((NODES, 2 * NODES), 0) == iota((NODES, 2 * NODES), 1) % NODES).astype(F32).astype(BF16)
@@ -112,18 +109,19 @@
         seen = dot(pick.astype(F32).astype(BF16), reach[r]).astype(BF16)
         mask[r] = dot(seen, twice)
     fetch.wait()
-    store = pltpu.make_async_copy(held, pool_copy, sems.at[33])
+    store = pltpu.make_async_copy(held, pool_copy, sems.at[65])
     store.start()
     for c in copies:
         c.wait()
     store.wait()
 
 
-def attend_kernel(lengths, queries, own, peer, node, mask, out):
+def attend_kernel(lengths, queries, own, node, mask, peer0, peer1, out):
     core, ctx = position()
     lane = iota((LANES, LANES), 1)
     order = (iota((LANES, LANES), 0) == (lane % NODES) * 8 + lane // NODES).astype(F32).astype(BF16)
-    peer_node = peer[pl.ds(NODE_ROWS0, 16), :].astype(F32)[:REQUESTS]
+    peers = (peer0, peer1)
+    peer_node = peer0[pl.ds(NODE_ROWS0, 16), :].astype(F32)[:REQUESTS]
     own_node = node[...].astype(F32)
     nodes = jnp.concatenate([own_node, peer_node], axis=0).astype(BF16)
     ones = jnp.ones((16, SPAN), BF16)
@@ -136,7 +134,7 @@
         query = dot(part, order, 0, 0).astype(BF16)
         length = lengths[HALF * core + r]
         span_own = own[pl.ds(r * SPAN, SPAN), :]
-        span_peer = peer[pl.ds(r * SPAN, SPAN), :]
+        span_peer = peers[r // EACH][pl.ds((r // EACH + r % EACH) * SPAN, SPAN), :]
         live_own = row < length - ctx * SPAN
         live_peer = row < length - (ctx + 1 - 2 * core) * SPAN
         seen = jnp.concatenate([mask[r]] * 4, axis=1)
@@ -189,6 +187,7 @@
 
 def combine_kernel(path, got, out):
     core = lax.axis_index("core")
+    x = lax.axis_index("x")
     y = lax.axis_index("y")
     logs = []
     for s in range(CHIPS):
@@ -206,8 +205,8 @@
     mixed = mixed * (1.0 / total)
     tail_row = iota((TAIL, HEAD), 0)
     tail = jnp.zeros((TAIL, HEAD), F32)
-    for j in range(HALF):
-        node = path[y, HALF * core + j]
+    for j in range(2):
+        node = path[y, 2 * x + j]
         held = got[node // 2].astype(F32)[64:BLOCK]
         is_own = node % 2 == core
         key = jnp.where(is_own, held[3:4], held[5:6])
@@ -215,38 +214,36 @@
         tail = jnp.where(tail_row == 2 * j, key, tail)
         tail = jnp.where(tail_row == 2 * j + 1, value, tail)
     block = jnp.concatenate([mixed, tail], axis=0).astype(BF16)
-    for s in range(16):
+    for s in range(CHIPS):
         out[s] = block
 
 
-def project_kernel(got, w0, w1, w2, w3, out):
-    x = lax.axis_index("x")
-    held = got[...].reshape(8, 2, BLOCK, HEAD)
-    weights = (w0, w1, w2, w3)
-    for pair in range(NEIGHBOURS // 2):
-        wide = []
-        for h in range(2):
-            cols = []
-            for n in (2 * pair, 2 * pair + 1):
-                rows = [weights[n][(2 * p + h) * HEAD : (2 * p + h + 1) * HEAD, :] for p in range(4)]
-                cols.append(jnp.concatenate(rows, axis=0))
-            wide.append(jnp.concatenate(cols, axis=1))
-        for k in range(2):
-            a = held[:, k, :64, :].reshape(LANES, HEAD)
-            sums = dot(a, wide[0], 0, 0)[:NODES] + dot(a, wide[1], 0, 0)[NODES:]
-            for n in range(2):
-                to = lax.rem(x + 2 * pair + n, NEIGHBOURS)
-                for t in range(8):
-                    out[to * 8 + t, k] = sums[t * 8 : t * 8 + 8, n * HEAD : (n + 1) * HEAD]
+def project_kernel(got, weight, peer, out):
+    core = lax.axis_index("core")
+    sides = []
+    for h in range(2):
+        own_h = [weight[(2 * p + h) * HEAD : (2 * p + h + 1) * HEAD, :] for p in range(4)]
+        peer_h = []
+        for p in range(4):
+            at = (2 * p + h) * HEAD
+            side = at // W_ROWS * HEAD
+            peer_h.append(peer[at % W_ROWS : at % W_ROWS + HEAD, side : side + HEAD])
+        sides.append(jnp.concatenate([jnp.concatenate(own_h, axis=0), jnp.concatenate(peer_h, axis=0)], axis=1))
+    for r in range(HALF):
+        a = got[pl.ds(r * 8, 8)][:, :64, :].reshape(LANES, HEAD)
+        sums = dot(a, sides[0], 0, 0)[:NODES] + dot(a, sides[1], 0, 0)[NODES:]
+        for t in range(8):
+            rows = sums[t * 8 : t * 8 + 8]
+            out[core * 8 + t, r] = rows[:, :HEAD]
+            out[(1 - core) * 8 + t, r] = rows[:, HEAD:]
 
 
 def sum_kernel(got, out):
-    for x in range(NEIGHBOURS):
-        total = got[x * 8]
+    for core in range(2):
+        total = got[core * 8]
         for t in range(1, 8):
-            total = total + got[x * 8 + t]
-        out[x] = total[0]
-        out[HALF + x] = total[1]
+            total = total + got[core * 8 + t]
+        out[HALF * core : HALF * core + HALF] = total
 
 
 def write_kernel(table, lengths, counts, spare, table_v, got, pool_in, pool, new_table, pages, sems):
@@ -280,8 +277,8 @@
                 fetch.wait()
                 now = pages[2 * r + step].astype(F32)
                 for j in range(PATH_ROWS):
-                    held = got[2 * r + j // HALF].astype(F32)[64:BLOCK]
-                    at = 2 * (j % HALF)
+                    held = got[(j // 2) * 8 + r].astype(F32)[64:BLOCK]
+                    at = 2 * (j % 2)
                     new = jnp.concatenate([held[at : at + 1], held[at + 1 : at + 2]], axis=1)
                     now = jnp.where((row == first + j) & (j < count), new, now)
                 pages[2 * r + step] = now.astype(BF16)
@@ -298,74 +295,73 @@
     params = pltpu.CompilerParams(vmem_limit_bytes=LIMIT)
     shape = jax.ShapeDtypeStruct
     node = node_kv.reshape(REQUESTS, 2 * HEAD)
-    held_pool, held_table, held_node, held_queries = (
+    held_pool, held_table, held_node, held_parents, held_weight, held_queries = (
         pltpu.with_memory_space_constraint(a, HBM)
-        for a in (pool, table, node, queries.reshape(REQUESTS, 8 * HEAD))
+        for a in (pool, table, node, parents, out_weight, queries.reshape(REQUESTS, 8 * HEAD))
     )
 
-    send, message = pl.pallas_call(
-        pack_kernel,
-        out_shape=(VMEM((SEND_ROWS, 2 * HEAD), BF16), VMEM((2 * CHIPS, HALF * 8, HEAD), BF16)),
-        in_specs=[spec(SMEM), spec(HBM), spec(VMEM), spec(VMEM)],
-        out_specs=(spec(VMEM), spec(VMEM)),
-        scratch_shapes=[pltpu.SemaphoreType.DMA((32,))],
-        compiler_params=params,
-        name="pack",
-    )(held_table, held_pool, held_node, held_queries)
-    peer = lax.ppermute(send, "core", [(0, 1), (1, 0)])
-
+    message = pl.pallas_call(
+        message_kernel,
+        out_shape=shape((2 * CHIPS, HALF * 8, HEAD), BF16),
+        in_specs=[spec(VMEM)],
+        out_specs=spec(VMEM),
+        compiler_params=params,
+        name="message",
+    )(held_queries)
     every_query = lax.all_to_all(message, ("x", "y", "core"), 0, 0, tiled=True)
 
-    own, pool_copy, mask = pl.pallas_call(
+    *sends, own, pool_copy, mask = pl.pallas_call(
         prepare_kernel,
         out_shape=(
+            *(shape((NODE_ROWS0 + extra, 2 * HEAD), BF16) for extra in (16, W_ROWS)),
             shape((HALF * SPAN, 2 * HEAD), BF16),
             shape(pool.shape, pool.dtype),
             shape((HALF, 16, 2 * NODES), F32),
         ),
-        in_specs=[spec(SMEM), spec(HBM), spec(VMEM)],
-        out_specs=(spec(VMEM), spec(HBM), spec(VMEM)),
-        scratch_shapes=[VMEM(pool.shape, BF16), pltpu.SemaphoreType.DMA((34,))],
+        in_specs=[spec(SMEM), spec(HBM), spec(VMEM), spec(VMEM), spec(HBM)],
+        out_specs=(*([spec(VMEM)] * (SENDS + 1)), spec(HBM), spec(VMEM)),
+        scratch_shapes=[VMEM(pool.shape, BF16), pltpu.SemaphoreType.DMA((68,))],
         compiler_params=params,
         cost_estimate=pl.CostEstimate(flops=50_000_000, bytes_accessed=7_000_000, transcendentals=0),
         name="prepare",
-    )(table, held_pool, parents)
+    )(held_table, held_pool, held_node, held_parents, held_weight)
+    peers = [lax.ppermute(a, "core", [(0, 1), (1, 0)]) for a in sends]
+    mask, *peers = lax.optimization_barrier((mask, *peers))
 
     partial = pl.pallas_call(
         attend_kernel,
         out_shape=shape((CHIPS, BLOCK, HEAD), BF16),
-        in_specs=[spec(SMEM)] + [spec(VMEM)] * 5,
+        in_specs=[spec(SMEM)] + [spec(VMEM)] * (4 + SENDS),
         out_specs=spec(VMEM),
         compiler_params=params,
         name="attend",
-    )(lengths, every_query, own, peer, node, mask)
-
-    partial, weight = lax.optimization_barrier((partial, out_weight))
-    weights = [weight]
-    for step in range(1, NEIGHBOURS):
-        ring = [((i + step) % NEIGHBOURS, i) for i in range(NEIGHBOURS)]
-        weights.append(lax.ppermute(weight, "x", ring))
+    )(lengths, every_query, own, node, mask, *peers)
+
     parts = lax.all_to_all(partial, ("x", "y"), 0, 0, tiled=True)
-    parts, *weights = lax.optimization_barrier((parts, *weights))
     mixed = pl.pallas_call(
         combine_kernel,
-        out_shape=shape((16, BLOCK, HEAD), BF16),
+        out_shape=shape((CHIPS, BLOCK, HEAD), BF16),
         in_specs=[spec(SMEM), spec(VMEM)],
         out_specs=spec(VMEM),
         compiler_params=params,
         name="combine",
     )(path, parts)
-    attention = lax.all_to_all(mixed, ("y", "core"), 0, 0, tiled=True)
+    attention = lax.all_to_all(mixed, ("x", "y"), 0, 0, tiled=True)
 
     sums = pl.pallas_call(
         project_kernel,
-        out_shape=shape((32, 2, 8, HEAD), F32),
-        in_specs=[spec(VMEM)] * 5,
-        out_specs=spec(VMEM),
+        grid=(1,),
+        out_shape=shape((16, HALF, 8, HEAD), F32),
+        in_specs=[
+            pl.BlockSpec((CHIPS, BLOCK, HEAD), lambda i: (0, 0, 0)),
+            pl.BlockSpec((8 * HEAD, HEAD), lambda i: (0, 0)),
+            pl.BlockSpec((W_ROWS, 2 * HEAD), lambda i: (0, 0)),
+        ],
+        out_specs=pl.BlockSpec((16, HALF, 8, HEAD), lambda i: (0, 0, 0, 0)),
         compiler_params=params,
         name="project",
-    )(attention, *weights)
-    shares = lax.all_to_all(sums, ("x", "tp"), 0, 0, tiled=True)
+    )(attention, out_weight, peers[1])
+    shares = lax.all_to_all(sums, ("core", "tp"), 0, 0, tiled=True)
     projected = pl.pallas_call(
         sum_kernel,
         out_shape=shape((REQUESTS, 8, HEAD), F32),

time: 117 us -> 109 us (0.932)
  blocking collectives: 19.2 us -> 43.2 us
  waiting for transfers between devices: 35.2 us -> 14.5 us
  starting transfers between devices: 42.2 us -> 31.3 us
    all_to_all x1 -> x2, blocking collectives: 19.2 us -> 43.2 us  [the longest x1 22.8 us: on_device(): attention = lax.all_to_all(mixed, ('x', 'y'), 0, 0, tiled=True)]
    ppermute x4 -> x2, starting transfers between devices: 19.4 us -> 4.33 us  [on_device(): peers = [lax.ppermute(a, 'core', [(0, 1), (1, 0)]) for a in sends]]
    ppermute x4 -> x2, waiting for transfers between devices: 12.7 us -> 1.86 us  [on_device(): peers = [lax.ppermute(a, 'core', [(0, 1), (1, 0)]) for a in sends]]
    all_to_all x1, waiting for transfers between devices: 13.3 us -> 5.02 us  [on_device(): every_query = lax.all_to_all(message, ('x', 'y', 'core'), 0, 0, tiled=True)]
    all_to_all x1, starting transfers between devices: 4.8 us -> 11.6 us  [on_device(): every_query = lax.all_to_all(message, ('x', 'y', 'core'), 0, 0, tiled=True)]
    all_to_all x2 -> x1, starting transfers between devices: 18 us -> 15.3 us  [on_device(): shares = lax.all_to_all(sums, ('core', 'tp'), 0, 0, tiled=True)]
    all_to_all x2 -> x1, waiting for transfers between devices: 9.26 us -> 7.63 us  [on_device(): shares = lax.all_to_all(sums, ('core', 'tp'), 0, 0, tiled=True)]
  transfers between devices with their start and end apart: 7 -> 4, of which waited for: 5 -> 3; matrix products, arithmetic and copies ran while one was open for 0% -> 0% of each run, Pallas kernels for 5% -> 7%
where the time goes in v5:
time: 109 us; the launch traced here: 108 us
  blocking collectives  43.2 us (40%)
  starting transfers between devices  31.3 us (29%)
  Pallas kernels  18.3 us (17%)
  waiting for transfers between devices  14.5 us (13%)
    all_to_all x1, blocking collectives, on_device(): attention = lax.all_to_all(mixed, ('x', 'y'), 0, 0, tiled=True)  22.8 us
    all_to_all x1, blocking collectives, on_device(): parts = lax.all_to_all(partial, ('x', 'y'), 0, 0, tiled=True)  20.4 us
    all_to_all x1, starting transfers between devices, on_device(): shares = lax.all_to_all(sums, ('core', 'tp'), 0, 0, tiled=True)  15.3 us
    all_to_all x1, starting transfers between devices, on_device(): every_query = lax.all_to_all(message, ('x', 'y', 'core'), 0, 0, tiled=True)  11.6 us
    all_to_all x1, waiting for transfers between devices, on_device(): shares = lax.all_to_all(sums, ('core', 'tp'), 0, 0, tiled=True)  7.63 us
    pallas_call x1, Pallas kernels, on_device(): pl.pallas_call(attend_kernel, out_shape=shape((CHIPS, BLOCK, HEAD), BF16)...  6.34 us
    pallas_call x1, Pallas kernels, on_device(): pl.pallas_call(prepare_kernel, out_shape=(*(shape((NODE_ROWS0 + extra, 2...  6.07 us
    all_to_all x1, waiting for transfers between devices, on_device(): every_query = lax.all_to_all(message, ('x', 'y', 'core'), 0, 0, tiled=True)  5.02 us
  transfers between devices with their start and end apart: 4, of which 3 were waited for; matrix products, arithmetic and copies ran while one was open for 0% of the time, Pallas kernels for 7%

profile of v5, /device:TPU:1, one launch (start us, length us, event | category | flops | bytes accessed | tf_op | source)
XLA Modules:
  0.0 108.1 jit_solution(10997348390994259267)
XLA Ops:
  0.6 0.0 copy-start.2
  0.7 1.6 %message.1 = bf16[64,32,128]{2,1,0:T(8,128)(2,1)} custom-call(bf16[8,1024]{1,0:T(8,128)(2,1)} %bitcast.4), custom_call_target="tpu_custom_call" | custom-call | tf_op jit(solution)/shard_map/message/pallas_call | solution.py:303
  2.2 11.6 %all-to-all-start = ((bf16[64,32,128]{2,1,0:T(8,128)(2,1)}), bf16[64,32,128]{2,1,0:T(8,128)(2,1)S(1)}, u32[]{:S(2)}, u32[]{:S(2)}) async-start(bf16[64,32,128]{2,1,0:T(8,128)(2,1)} %message.1), calls=%async_computation | async-start | bytes 1048576 | tf_op jit(solution)/shard_map/all_to_all | solution.py:311
  13.9 6.1 %prepare.1 = (bf16[1040,256]{1,0:T(8,128)(2,1)S(1)}, bf16[1536,256]{1,0:T(8,128)(2,1)S(1)}, bf16[2048,256]{1,0:T(8,128)(2,1)S(1)}, bf16[72,64,256]{2,1,0:T(8,128)(2,1)}, f32[4,16,128]{2,1,0:T(8,128)S(1)}) custom-call(s32[8,8]{1,0:T(8,128)} %table_v.1, bf16[72,64,256]{2,1,0:T(8,128)(2,1)} %pool.1, bf16[8,256]{1,0:T(8,128)(2,1)} %bitcast.2, s32[8,64]{1,0:T(8,128)} %parents.1, ...), custom_call_target="tpu_custom_call" | custom-call | flops 50000000 | bytes 7000000 | tf_op jit(solution)/shard_map/prepare/pallas_call | solution.py:313
  19.9 0.0 copy-start.3
  20.0 2.4 %collective-permute-start.1 = (bf16[1536,256]{1,0:T(8,128)(2,1)S(1)}, bf16[1536,256]{1,0:T(8,128)(2,1)S(1)}, u32[]{:S(2)}, u32[]{:S(2)}) collective-permute-start(bf16[1536,256]{1,0:T(8,128)(2,1)S(1)} %get-tuple-element.16), channel_id=1, source_target_pairs={{0,8},{8,0},{1,9},{9,1},{2,10},{10,2},{3,11},{11,3},{4,12},{12,4},... | collective-permute-start | bytes 2359304 | tf_op jit(solution)/shard_map/ppermute | solution.py:328
  22.3 1.9 %collective-permute-start = (bf16[1040,256]{1,0:T(8,128)(2,1)S(1)}, bf16[1040,256]{1,0:T(8,128)(2,1)S(1)}, u32[]{:S(2)}, u32[]{:S(2)}) collective-permute-start(bf16[1040,256]{1,0:T(8,128)(2,1)S(1)} %get-tuple-element.15), channel_id=1, source_target_pairs={{0,8},{8,0},{1,9},{9,1},{2,10},{10,2},{3,11},{11,3},{4,12},{12,4},... | collective-permute-start | bytes 1597448 | tf_op jit(solution)/shard_map/ppermute | solution.py:328
  24.3 1.9 %collective-permute-done.peer0 = bf16[1040,256]{1,0:T(8,128)(2,1)S(1)} collective-permute-done((bf16[1040,256]{1,0:T(8,128)(2,1)S(1)}, bf16[1040,256]{1,0:T(8,128)(2,1)S(1)}, u32[]{:S(2)}, u32[]{:S(2)}) %collective-permute-start) | collective-permute-done | bytes 532512 | tf_op jit(solution)/shard_map/ppermute | solution.py:328
  26.2 0.0 collective-permute-done.1.peer1.peer
  26.2 5.0 %all-to-all-done.queries = bf16[64,32,128]{2,1,0:T(8,128)(2,1)S(1)} async-done(((bf16[64,32,128]{2,1,0:T(8,128)(2,1)}), bf16[64,32,128]{2,1,0:T(8,128)(2,1)S(1)}, u32[]{:S(2)}, u32[]{:S(2)}) %all-to-all-start) | async-done | bytes 524320 | tf_op jit(solution)/shard_map/all_to_all | solution.py:311
  31.2 0.0 copy-done.4
  31.2 6.3 %attend.1 = bf16[32,72,128]{2,1,0:T(8,128)(2,1)S(1)} custom-call(s32[8]{0:T(128)S(1)} %copy-done.4, bf16[64,32,128]{2,1,0:T(8,128)(2,1)S(1)} %all-to-all-done.queries, bf16[2048,256]{1,0:T(8,128)(2,1)S(1)} %get-tuple-element.13.own, bf16[8,256]{1,0:T(8,128)(2,1)S(1)} %bitcast.3, f32[4,16,128]{2,1,0:T(8,128)S(1)} %get-tuple-element.17.mask, ...), custom_call_target="tpu_custom_call" | custom-call | tf_op jit(solution)/shard_map/attend/pallas_call | solution.py:331
  37.5 0.0 copy-start
  37.6 20.4 %all_to_all.20.got = bf16[32,72,128]{2,1,0:T(8,128)(2,1)S(1)} all-to-all(bf16[32,72,128]{2,1,0:T(8,128)(2,1)S(1)} %attend.1), channel_id=1, replica_groups=mesh['x'=4,'y'=8,'core'=2,'tp'=8] {'x','y'}, dimensions={0} | all-to-all | bytes 1179648 | tf_op jit(solution)/shard_map/all_to_all | solution.py:340
  57.9 0.0 copy-done.3
  57.9 0.8 combine.1
  58.7 22.8 %all_to_all.21.got = bf16[32,72,128]{2,1,0:T(8,128)(2,1)S(1)} all-to-all(bf16[32,72,128]{2,1,0:T(8,128)(2,1)S(1)} %combine.1), channel_id=1, replica_groups=mesh['x'=4,'y'=8,'core'=2,'tp'=8] {'x','y'}, dimensions={0} | all-to-all | bytes 1179648 | tf_op jit(solution)/shard_map/all_to_all | solution.py:349
  81.6 1.2 %project.1 = f32[16,4,8,128]{3,2,1,0:T(8,128)} custom-call(bf16[32,72,128]{2,1,0:T(8,128)(2,1)S(1)} %all_to_all.21.got, bf16[1024,128]{1,0:T(8,128)(2,1)S(1)} %copy-done, bf16[1536,256]{1,0:T(8,128)(2,1)S(1)} %collective-permute-done.1.peer1.peer), custom_call_target="tpu_custom_call" | custom-call | tf_op jit(solution)/shard_map/project/pallas_call | solution.py:351
  82.8 15.3 %all-to-all-start.3 = ((f32[16,4,8,128]{3,2,1,0:T(8,128)}), f32[16,4,8,128]{3,2,1,0:T(8,128)S(1)}, u32[]{:S(2)}, u32[]{:S(2)}) async-start(f32[16,4,8,128]{3,2,1,0:T(8,128)} %project.1), calls=%async_computation.3 | async-start | bytes 524288 | tf_op jit(solution)/shard_map/all_to_all | solution.py:364
  98.1 0.1 copy.14.spare
  98.2 0.0 copy-done.1
  98.2 1.7 %write.1 = (bf16[72,64,256]{2,1,0:T(8,128)(2,1)}, s32[8,8]{1,0:T(8,128)}) custom-call(s32[8,8]{1,0:T(8,128)S(1)} %copy-done.1, s32[8]{0:T(128)S(1)} %copy-done.4, s32[8]{0:T(128)S(1)} %copy-done.5, s32[8,1]{1,0:T(8,128)S(1)} %copy.14.spare, s32[8,8]{1,0:T(8,128)S(1)} %copy-done.1, ...), custom_call_target="tpu_custom_call", output_to_operand_aliasing={{0}: (6, {})} | custom-call | tf_op jit(solution)/shard_map/write/pallas_call | solution.py:374
  99.9 7.6 %all-to-all-done.3.got = f32[16,4,8,128]{3,2,1,0:T(8,128)S(1)} async-done(((f32[16,4,8,128]{3,2,1,0:T(8,128)}), f32[16,4,8,128]{3,2,1,0:T(8,128)S(1)}, u32[]{:S(2)}, u32[]{:S(2)}) %all-to-all-start.3) | async-done | bytes 262176 | tf_op jit(solution)/shard_map/all_to_all | solution.py:364
  107.5 0.6 sum.1
  (8 shorter events, 0.0 us)
Async XLA Ops:
  0.6 30.6 %copy-start.2 = (bf16[8,1,256]{2,0,1:T(8,128)(2,1)S(1)}, bf16[8,1,256]{2,0,1:T(8,128)(2,1)}, u32[]{:S(2)}) copy-start(bf16[8,1,256]{2,0,1:T(8,128)(2,1)} %param.11) | copy-start | bytes 12292
  0.6 30.6 %copy-start.4 = (s32[8]{0:T(128)S(1)}, s32[8]{0:T(128)}, u32[]{:S(2)}) copy-start(s32[8]{0:T(128)} %lengths.3) | copy-start | bytes 100
  2.2 29.0 %all-to-all-start = ((bf16[64,32,128]{2,1,0:T(8,128)(2,1)}), bf16[64,32,128]{2,1,0:T(8,128)(2,1)S(1)}, u32[]{:S(2)}, u32[]{:S(2)}) async-start(bf16[64,32,128]{2,1,0:T(8,128)(2,1)} %message.1), calls=%async_computation | async-start | bytes 1048576 | tf_op jit(solution)/shard_map/all_to_all | solution.py:311
  19.9 38.0 %copy-start.3 = (s32[8,8]{1,0:T(8,128)S(1)}, s32[8,8]{1,0:T(8,128)}, u32[]{:S(2)}) copy-start(s32[8,8]{1,0:T(8,128)} %path.1) | copy-start | bytes 772
  20.0 6.2 %collective-permute-start.1 = (bf16[1536,256]{1,0:T(8,128)(2,1)S(1)}, bf16[1536,256]{1,0:T(8,128)(2,1)S(1)}, u32[]{:S(2)}, u32[]{:S(2)}) collective-permute-start(bf16[1536,256]{1,0:T(8,128)(2,1)S(1)} %get-tuple-element.16), channel_id=1, source_target_pairs={{0,8},{8,0},{1,9},{9,1},{2,10},{10,2},{3,11},{11,3},{4,12},{12,4},... | collective-permute-start | bytes 2359304 | tf_op jit(solution)/shard_map/ppermute | solution.py:328
  22.3 3.8 %collective-permute-start = (bf16[1040,256]{1,0:T(8,128)(2,1)S(1)}, bf16[1040,256]{1,0:T(8,128)(2,1)S(1)}, u32[]{:S(2)}, u32[]{:S(2)}) collective-permute-start(bf16[1040,256]{1,0:T(8,128)(2,1)S(1)} %get-tuple-element.15), channel_id=1, source_target_pairs={{0,8},{8,0},{1,9},{9,1},{2,10},{10,2},{3,11},{11,3},{4,12},{12,4},... | collective-permute-start | bytes 1597448 | tf_op jit(solution)/shard_map/ppermute | solution.py:328
  37.5 44.0 %copy-start = (bf16[1024,128]{1,0:T(8,128)(2,1)S(1)}, bf16[1024,128]{1,0:T(8,128)(2,1)}, u32[]{:S(2)}) copy-start(bf16[1024,128]{1,0:T(8,128)(2,1)} %weight.3) | copy-start | bytes 786436
  57.9 40.2 %copy-start.6 = (s32[8,1]{0,1:T(1,128)S(1)}, s32[8,1]{0,1:T(1,128)}, u32[]{:S(2)}) copy-start(s32[8,1]{0,1:T(1,128)} %param.19) | copy-start | bytes 100
  57.9 40.3 %copy-start.1 = (s32[8,8]{1,0:T(8,128)S(1)}, s32[8,8]{1,0:T(8,128)}, u32[]{:S(2)}) copy-start(s32[8,8]{1,0:T(8,128)} %table_v.1) | copy-start | bytes 772
  57.9 40.3 %copy-start.5 = (s32[8]{0:T(128)S(1)}, s32[8]{0:T(128)}, u32[]{:S(2)}) copy-start(s32[8]{0:T(128)} %counts.1) | copy-start | bytes 100
  82.8 24.7 %all-to-all-start.3 = ((f32[16,4,8,128]{3,2,1,0:T(8,128)}), f32[16,4,8,128]{3,2,1,0:T(8,128)S(1)}, u32[]{:S(2)}, u32[]{:S(2)}) async-start(f32[16,4,8,128]{3,2,1,0:T(8,128)} %project.1), calls=%async_computation.3 | async-start | bytes 524288 | tf_op jit(solution)/shard_map/all_to_all | solution.py:364

commit v6 on v5

--- a/solution.py
+++ b/solution.py
@@ -99,8 +99,12 @@
     for r in range(HALF):
         link = parents[pl.ds(HALF * core + r, 1), :]
         reach.append(((up == link) | (up == down)).astype(F32).astype(BF16))
-    for _ in range(6):
+    for step in range(6):
         reach = [jnp.minimum(dot(m, m), 1.0).astype(BF16) for m in reach]
+        if step == 2:
+            fetch.wait()
+            store = pltpu.make_async_copy(held, pool_copy, sems.at[65])
+            store.start()
     for r in range(HALF):
         mine = HALF * core + r
         pick = ((pick_row == mine) & (pick_node == ctx)) | (
@@ -108,9 +112,6 @@
         )
         seen = dot(pick.astype(F32).astype(BF16), reach[r]).astype(BF16)
         mask[r] = dot(seen, twice)
-    fetch.wait()
-    store = pltpu.make_async_copy(held, pool_copy, sems.at[65])
-    store.start()
     for c in copies:
         c.wait()
     store.wait()
@@ -128,7 +129,7 @@
     ones_tree = jnp.ones((16, 16), BF16)
     row = iota((SPAN, LANES), 0)
     tail_row = iota((TAIL, HEAD), 0)
-    for r in range(HALF):
+    def scores(r):
         part = queries[:, pl.ds((r // 2) * 16, 16), :].astype(F32)[:, (r % 2) * 8 : (r % 2) * 8 + 8, :]
         part = part.reshape(LANES, HEAD).astype(BF16)
         query = dot(part, order, 0, 0).astype(BF16)
@@ -146,6 +147,13 @@
             jnp.max(s_tree, axis=0, keepdims=True),
         )
         peak = jnp.maximum(peak, FLOOR) * SCALE2
+        return s_own, s_peer, s_tree, span_own, span_peer, peak
+
+    ahead = scores(0)
+    for r in range(HALF):
+        s_own, s_peer, s_tree, span_own, span_peer, peak = ahead
+        if r + 1 < HALF:
+            ahead = scores(r + 1)
         total = None
         for s, v, one in (
             (s_own, span_own[:, HEAD:], ones),

time: 109 us -> 108 us (level)
  Pallas kernels: 18.3 us -> 16.9 us
  transfers between devices with their start and end apart: 4 -> 4, of which waited for: 3 -> 3; matrix products, arithmetic and copies ran while one was open for 0% -> 0% of each run, Pallas kernels for 7% -> 6%
where the time goes in v6:
time: 108 us; the launch traced here: 107 us
  blocking collectives  43.2 us (40%)
  starting transfers between devices  31.3 us (29%)
  Pallas kernels  16.9 us (16%)
  waiting for transfers between devices  15.3 us (14%)
    all_to_all x1, blocking collectives, on_device(): attention = lax.all_to_all(mixed, ('x', 'y'), 0, 0, tiled=True)  22.8 us
    all_to_all x1, blocking collectives, on_device(): parts = lax.all_to_all(partial, ('x', 'y'), 0, 0, tiled=True)  20.4 us
    all_to_all x1, starting transfers between devices, on_device(): shares = lax.all_to_all(sums, ('core', 'tp'), 0, 0, tiled=True)  15.3 us
    all_to_all x1, starting transfers between devices, on_device(): every_query = lax.all_to_all(message, ('x', 'y', 'core'), 0, 0, tiled=True)  11.6 us
    all_to_all x1, waiting for transfers between devices, on_device(): shares = lax.all_to_all(sums, ('core', 'tp'), 0, 0, tiled=True)  7.63 us
    all_to_all x1, waiting for transfers between devices, on_device(): every_query = lax.all_to_all(message, ('x', 'y', 'core'), 0, 0, tiled=True)  5.81 us
    pallas_call x1, Pallas kernels, on_device(): pl.pallas_call(attend_kernel, out_shape=shape((CHIPS, BLOCK, HEAD), BF16)...  5.72 us
    pallas_call x1, Pallas kernels, on_device(): pl.pallas_call(prepare_kernel, out_shape=(*(shape((NODE_ROWS0 + extra, 2...  5.28 us
  transfers between devices with their start and end apart: 4, of which 3 were waited for; matrix products, arithmetic and copies ran while one was open for 0% of the time, Pallas kernels for 6%

profile of v6, /device:TPU:1, one launch (start us, length us, event | category | flops | bytes accessed | tf_op | source)
XLA Modules:
  0.0 107.5 jit_solution(891590539212237938)
XLA Ops:
  0.6 0.0 copy-start.2
  0.7 1.6 %message.1 = bf16[64,32,128]{2,1,0:T(8,128)(2,1)} custom-call(bf16[8,1024]{1,0:T(8,128)(2,1)} %bitcast.4), custom_call_target="tpu_custom_call" | custom-call | tf_op jit(solution)/shard_map/message/pallas_call | solution.py:311
  2.2 11.6 %all-to-all-start = ((bf16[64,32,128]{2,1,0:T(8,128)(2,1)}), bf16[64,32,128]{2,1,0:T(8,128)(2,1)S(1)}, u32[]{:S(2)}, u32[]{:S(2)}) async-start(bf16[64,32,128]{2,1,0:T(8,128)(2,1)} %message.1), calls=%async_computation | async-start | bytes 1048576 | tf_op jit(solution)/shard_map/all_to_all | solution.py:319
  13.9 5.3 %prepare.1 = (bf16[1040,256]{1,0:T(8,128)(2,1)S(1)}, bf16[1536,256]{1,0:T(8,128)(2,1)S(1)}, bf16[2048,256]{1,0:T(8,128)(2,1)S(1)}, bf16[72,64,256]{2,1,0:T(8,128)(2,1)}, f32[4,16,128]{2,1,0:T(8,128)S(1)}) custom-call(s32[8,8]{1,0:T(8,128)} %table_v.1, bf16[72,64,256]{2,1,0:T(8,128)(2,1)} %pool.1, bf16[8,256]{1,0:T(8,128)(2,1)} %bitcast.2, s32[8,64]{1,0:T(8,128)} %parents.1, ...), custom_call_target="tpu_custom_call" | custom-call | flops 50000000 | bytes 7000000 | tf_op jit(solution)/shard_map/prepare/pallas_call | solution.py:321
  19.2 0.0 copy-start.3
  19.2 2.4 %collective-permute-start.1 = (bf16[1536,256]{1,0:T(8,128)(2,1)S(1)}, bf16[1536,256]{1,0:T(8,128)(2,1)S(1)}, u32[]{:S(2)}, u32[]{:S(2)}) collective-permute-start(bf16[1536,256]{1,0:T(8,128)(2,1)S(1)} %get-tuple-element.16), channel_id=1, source_target_pairs={{0,8},{8,0},{1,9},{9,1},{2,10},{10,2},{3,11},{11,3},{4,12},{12,4},... | collective-permute-start | bytes 2359304 | tf_op jit(solution)/shard_map/ppermute | solution.py:336
  21.6 1.9 %collective-permute-start = (bf16[1040,256]{1,0:T(8,128)(2,1)S(1)}, bf16[1040,256]{1,0:T(8,128)(2,1)S(1)}, u32[]{:S(2)}, u32[]{:S(2)}) collective-permute-start(bf16[1040,256]{1,0:T(8,128)(2,1)S(1)} %get-tuple-element.15), channel_id=1, source_target_pairs={{0,8},{8,0},{1,9},{9,1},{2,10},{10,2},{3,11},{11,3},{4,12},{12,4},... | collective-permute-start | bytes 1597448 | tf_op jit(solution)/shard_map/ppermute | solution.py:336
  23.5 1.9 %collective-permute-done.peer0 = bf16[1040,256]{1,0:T(8,128)(2,1)S(1)} collective-permute-done((bf16[1040,256]{1,0:T(8,128)(2,1)S(1)}, bf16[1040,256]{1,0:T(8,128)(2,1)S(1)}, u32[]{:S(2)}, u32[]{:S(2)}) %collective-permute-start) | collective-permute-done | bytes 532512 | tf_op jit(solution)/shard_map/ppermute | solution.py:336
  25.4 0.0 collective-permute-done.1.peer1.peer
  25.4 5.8 %all-to-all-done.queries = bf16[64,32,128]{2,1,0:T(8,128)(2,1)S(1)} async-done(((bf16[64,32,128]{2,1,0:T(8,128)(2,1)}), bf16[64,32,128]{2,1,0:T(8,128)(2,1)S(1)}, u32[]{:S(2)}, u32[]{:S(2)}) %all-to-all-start) | async-done | bytes 524320 | tf_op jit(solution)/shard_map/all_to_all | solution.py:319
  31.2 0.0 copy-done.2
  31.2 5.7 %attend.1 = bf16[32,72,128]{2,1,0:T(8,128)(2,1)S(1)} custom-call(s32[8]{0:T(128)S(1)} %copy-done.4, bf16[64,32,128]{2,1,0:T(8,128)(2,1)S(1)} %all-to-all-done.queries, bf16[2048,256]{1,0:T(8,128)(2,1)S(1)} %get-tuple-element.13.own, bf16[8,256]{1,0:T(8,128)(2,1)S(1)} %bitcast.3, f32[4,16,128]{2,1,0:T(8,128)S(1)} %get-tuple-element.17.mask, ...), custom_call_target="tpu_custom_call" | custom-call | tf_op jit(solution)/shard_map/attend/pallas_call | solution.py:339
  36.9 0.0 copy-start
  36.9 20.4 %all_to_all.20.got = bf16[32,72,128]{2,1,0:T(8,128)(2,1)S(1)} all-to-all(bf16[32,72,128]{2,1,0:T(8,128)(2,1)S(1)} %attend.1), channel_id=1, replica_groups=mesh['x'=4,'y'=8,'core'=2,'tp'=8] {'x','y'}, dimensions={0} | all-to-all | bytes 1179648 | tf_op jit(solution)/shard_map/all_to_all | solution.py:348
  57.3 0.0 copy-done.3
  57.3 0.8 combine.1
  58.1 22.8 %all_to_all.21.got = bf16[32,72,128]{2,1,0:T(8,128)(2,1)S(1)} all-to-all(bf16[32,72,128]{2,1,0:T(8,128)(2,1)S(1)} %combine.1), channel_id=1, replica_groups=mesh['x'=4,'y'=8,'core'=2,'tp'=8] {'x','y'}, dimensions={0} | all-to-all | bytes 1179648 | tf_op jit(solution)/shard_map/all_to_all | solution.py:357
  81.0 1.2 %project.1 = f32[16,4,8,128]{3,2,1,0:T(8,128)} custom-call(bf16[32,72,128]{2,1,0:T(8,128)(2,1)S(1)} %all_to_all.21.got, bf16[1024,128]{1,0:T(8,128)(2,1)S(1)} %copy-done, bf16[1536,256]{1,0:T(8,128)(2,1)S(1)} %collective-permute-done.1.peer1.peer), custom_call_target="tpu_custom_call" | custom-call | tf_op jit(solution)/shard_map/project/pallas_call | solution.py:359
  82.2 15.3 %all-to-all-start.3 = ((f32[16,4,8,128]{3,2,1,0:T(8,128)}), f32[16,4,8,128]{3,2,1,0:T(8,128)S(1)}, u32[]{:S(2)}, u32[]{:S(2)}) async-start(f32[16,4,8,128]{3,2,1,0:T(8,128)} %project.1), calls=%async_computation.3 | async-start | bytes 524288 | tf_op jit(solution)/shard_map/all_to_all | solution.py:372
  97.5 0.0 copy-done.6
  97.5 0.1 copy.14.spare
  97.6 1.7 %write.1 = (bf16[72,64,256]{2,1,0:T(8,128)(2,1)}, s32[8,8]{1,0:T(8,128)}) custom-call(s32[8,8]{1,0:T(8,128)S(1)} %copy-done.1, s32[8]{0:T(128)S(1)} %copy-done.4, s32[8]{0:T(128)S(1)} %copy-done.5, s32[8,1]{1,0:T(8,128)S(1)} %copy.14.spare, s32[8,8]{1,0:T(8,128)S(1)} %copy-done.1, ...), custom_call_target="tpu_custom_call", output_to_operand_aliasing={{0}: (6, {})} | custom-call | tf_op jit(solution)/shard_map/write/pallas_call | solution.py:382
  99.2 7.6 %all-to-all-done.3.got = f32[16,4,8,128]{3,2,1,0:T(8,128)S(1)} async-done(((f32[16,4,8,128]{3,2,1,0:T(8,128)}), f32[16,4,8,128]{3,2,1,0:T(8,128)S(1)}, u32[]{:S(2)}, u32[]{:S(2)}) %all-to-all-start.3) | async-done | bytes 262176 | tf_op jit(solution)/shard_map/all_to_all | solution.py:372
  106.9 0.6 sum.1
  (8 shorter events, 0.0 us)
Async XLA Ops:
  0.6 30.6 %copy-start.2 = (bf16[8,1,256]{2,0,1:T(8,128)(2,1)S(1)}, bf16[8,1,256]{2,0,1:T(8,128)(2,1)}, u32[]{:S(2)}) copy-start(bf16[8,1,256]{2,0,1:T(8,128)(2,1)} %param.11) | copy-start | bytes 12292
  0.6 30.6 %copy-start.4 = (s32[8]{0:T(128)S(1)}, s32[8]{0:T(128)}, u32[]{:S(2)}) copy-start(s32[8]{0:T(128)} %lengths.3) | copy-start | bytes 100
  2.2 29.0 %all-to-all-start = ((bf16[64,32,128]{2,1,0:T(8,128)(2,1)}), bf16[64,32,128]{2,1,0:T(8,128)(2,1)S(1)}, u32[]{:S(2)}, u32[]{:S(2)}) async-start(bf16[64,32,128]{2,1,0:T(8,128)(2,1)} %message.1), calls=%async_computation | async-start | bytes 1048576 | tf_op jit(solution)/shard_map/all_to_all | solution.py:319
  19.2 38.2 %copy-start.3 = (s32[8,8]{1,0:T(8,128)S(1)}, s32[8,8]{1,0:T(8,128)}, u32[]{:S(2)}) copy-start(s32[8,8]{1,0:T(8,128)} %path.1) | copy-start | bytes 772
  19.2 6.2 %collective-permute-start.1 = (bf16[1536,256]{1,0:T(8,128)(2,1)S(1)}, bf16[1536,256]{1,0:T(8,128)(2,1)S(1)}, u32[]{:S(2)}, u32[]{:S(2)}) collective-permute-start(bf16[1536,256]{1,0:T(8,128)(2,1)S(1)} %get-tuple-element.16), channel_id=1, source_target_pairs={{0,8},{8,0},{1,9},{9,1},{2,10},{10,2},{3,11},{11,3},{4,12},{12,4},... | collective-permute-start | bytes 2359304 | tf_op jit(solution)/shard_map/ppermute | solution.py:336
  21.6 3.8 %collective-permute-start = (bf16[1040,256]{1,0:T(8,128)(2,1)S(1)}, bf16[1040,256]{1,0:T(8,128)(2,1)S(1)}, u32[]{:S(2)}, u32[]{:S(2)}) collective-permute-start(bf16[1040,256]{1,0:T(8,128)(2,1)S(1)} %get-tuple-element.15), channel_id=1, source_target_pairs={{0,8},{8,0},{1,9},{9,1},{2,10},{10,2},{3,11},{11,3},{4,12},{12,4},... | collective-permute-start | bytes 1597448 | tf_op jit(solution)/shard_map/ppermute | solution.py:336
  36.9 44.0 %copy-start = (bf16[1024,128]{1,0:T(8,128)(2,1)S(1)}, bf16[1024,128]{1,0:T(8,128)(2,1)}, u32[]{:S(2)}) copy-start(bf16[1024,128]{1,0:T(8,128)(2,1)} %weight.3) | copy-start | bytes 786436
  57.3 40.2 %copy-start.6 = (s32[8,1]{0,1:T(1,128)S(1)}, s32[8,1]{0,1:T(1,128)}, u32[]{:S(2)}) copy-start(s32[8,1]{0,1:T(1,128)} %param.19) | copy-start | bytes 100
  57.3 40.2 %copy-start.1 = (s32[8,8]{1,0:T(8,128)S(1)}, s32[8,8]{1,0:T(8,128)}, u32[]{:S(2)}) copy-start(s32[8,8]{1,0:T(8,128)} %table_v.1) | copy-start | bytes 772
  57.3 40.2 %copy-start.5 = (s32[8]{0:T(128)S(1)}, s32[8]{0:T(128)}, u32[]{:S(2)}) copy-start(s32[8]{0:T(128)} %counts.1) | copy-start | bytes 100
  82.2 24.7 %all-to-all-start.3 = ((f32[16,4,8,128]{3,2,1,0:T(8,128)}), f32[16,4,8,128]{3,2,1,0:T(8,128)S(1)}, u32[]{:S(2)}, u32[]{:S(2)}) async-start(f32[16,4,8,128]{3,2,1,0:T(8,128)} %project.1), calls=%async_computation.3 | async-start | bytes 524288 | tf_op jit(solution)/shard_map/all_to_all | solution.py:372

commit v7 on v6

--- a/solution.py
+++ b/solution.py
@@ -60,7 +60,7 @@
         ]
         rows = jnp.concatenate(rows, axis=0).astype(BF16)
         for chip in range(CHIPS):
-            message[2 * chip + half] = rows
+            message[CHIPS * half + chip] = rows
 
 
 def prepare_kernel(table, pool, node, parents, weight, send0, send1, own, pool_copy, mask, held, sems):
@@ -120,7 +120,9 @@
 def attend_kernel(lengths, queries, own, node, mask, peer0, peer1, out):
     core, ctx = position()
     lane = iota((LANES, LANES), 1)
-    order = (iota((LANES, LANES), 0) == (lane % NODES) * 8 + lane // NODES).astype(F32).astype(BF16)
+    asker = lane % NODES
+    came = (asker % 2) * CHIPS + (asker // 2 % 8) * 4 + asker // 16
+    order = (iota((LANES, LANES), 0) == came * 8 + lane // NODES).astype(F32).astype(BF16)
     peers = (peer0, peer1)
     peer_node = peer0[pl.ds(NODE_ROWS0, 16), :].astype(F32)[:REQUESTS]
     own_node = node[...].astype(F32)
@@ -316,7 +318,7 @@
         compiler_params=params,
         name="message",
     )(held_queries)
-    every_query = lax.all_to_all(message, ("x", "y", "core"), 0, 0, tiled=True)
+    every_query = lax.all_to_all(message, ("core", "y", "x"), 0, 0, tiled=True)
 
     *sends, own, pool_copy, mask = pl.pallas_call(
         prepare_kernel,

time: 108 us -> 108 us (level)
  no operation moved by 1% of the time
where the time goes in v7:
time: 108 us; the launch traced here: 107 us
  blocking collectives  44 us (41%)
  starting transfers between devices  30.4 us (28%)
  Pallas kernels  16.9 us (16%)
  waiting for transfers between devices  15.3 us (14%)
    all_to_all x1, blocking collectives, on_device(): attention = lax.all_to_all(mixed, ('x', 'y'), 0, 0, tiled=True)  23.8 us
    all_to_all x1, blocking collectives, on_device(): parts = lax.all_to_all(partial, ('x', 'y'), 0, 0, tiled=True)  20.2 us
    all_to_all x1, starting transfers between devices, on_device(): shares = lax.all_to_all(sums, ('core', 'tp'), 0, 0, tiled=True)  14.3 us
    all_to_all x1, starting transfers between devices, on_device(): every_query = lax.all_to_all(message, ('core', 'y', 'x'), 0, 0, tiled=True)  11.7 us
    all_to_all x1, waiting for transfers between devices, on_device(): shares = lax.all_to_all(sums, ('core', 'tp'), 0, 0, tiled=True)  7.63 us
    all_to_all x1, waiting for transfers between devices, on_device(): every_query = lax.all_to_all(message, ('core', 'y', 'x'), 0, 0, tiled=True)  5.98 us
    pallas_call x1, Pallas kernels, on_device(): pl.pallas_call(attend_kernel, out_shape=shape((CHIPS, BLOCK, HEAD), BF16)...  5.72 us
    pallas_call x1, Pallas kernels, on_device(): pl.pallas_call(prepare_kernel, out_shape=(*(shape((NODE_ROWS0 + extra, 2...  5.31 us
  transfers between devices with their start and end apart: 4, of which 3 were waited for; matrix products, arithmetic and copies ran while one was open for 0% of the time, Pallas kernels for 6%

profile of v7, /device:TPU:1, one launch (start us, length us, event | category | flops | bytes accessed | tf_op | source)
XLA Modules:
  0.0 107.4 jit_solution(8785327968553553487)
XLA Ops:
  0.6 0.0 copy-start.2
  0.6 0.0 copy-start.4
  0.7 1.6 %message.1 = bf16[64,32,128]{2,1,0:T(8,128)(2,1)} custom-call(bf16[8,1024]{1,0:T(8,128)(2,1)} %bitcast.4), custom_call_target="tpu_custom_call" | custom-call | tf_op jit(solution)/shard_map/message/pallas_call | solution.py:313
  2.2 11.7 %all-to-all-start = ((bf16[64,32,128]{2,1,0:T(8,128)(2,1)}), bf16[64,32,128]{2,1,0:T(8,128)(2,1)S(1)}, u32[]{:S(2)}, u32[]{:S(2)}) async-start(bf16[64,32,128]{2,1,0:T(8,128)(2,1)} %message.1), calls=%async_computation | async-start | bytes 1048576 | tf_op jit(solution)/shard_map/all_to_all | solution.py:321
  13.9 5.3 %prepare.1 = (bf16[1040,256]{1,0:T(8,128)(2,1)S(1)}, bf16[1536,256]{1,0:T(8,128)(2,1)S(1)}, bf16[2048,256]{1,0:T(8,128)(2,1)S(1)}, bf16[72,64,256]{2,1,0:T(8,128)(2,1)}, f32[4,16,128]{2,1,0:T(8,128)S(1)}) custom-call(s32[8,8]{1,0:T(8,128)} %table_v.1, bf16[72,64,256]{2,1,0:T(8,128)(2,1)} %pool.1, bf16[8,256]{1,0:T(8,128)(2,1)} %bitcast.2, s32[8,64]{1,0:T(8,128)} %parents.1, ...), custom_call_target="tpu_custom_call" | custom-call | flops 50000000 | bytes 7000000 | tf_op jit(solution)/shard_map/prepare/pallas_call | solution.py:323
  19.3 0.0 copy-start.3
  19.3 2.2 %collective-permute-start.1 = (bf16[1536,256]{1,0:T(8,128)(2,1)S(1)}, bf16[1536,256]{1,0:T(8,128)(2,1)S(1)}, u32[]{:S(2)}, u32[]{:S(2)}) collective-permute-start(bf16[1536,256]{1,0:T(8,128)(2,1)S(1)} %get-tuple-element.16), channel_id=1, source_target_pairs={{0,8},{8,0},{1,9},{9,1},{2,10},{10,2},{3,11},{11,3},{4,12},{12,4},... | collective-permute-start | bytes 2359304 | tf_op jit(solution)/shard_map/ppermute | solution.py:338
  21.5 2.1 %collective-permute-start = (bf16[1040,256]{1,0:T(8,128)(2,1)S(1)}, bf16[1040,256]{1,0:T(8,128)(2,1)S(1)}, u32[]{:S(2)}, u32[]{:S(2)}) collective-permute-start(bf16[1040,256]{1,0:T(8,128)(2,1)S(1)} %get-tuple-element.15), channel_id=1, source_target_pairs={{0,8},{8,0},{1,9},{9,1},{2,10},{10,2},{3,11},{11,3},{4,12},{12,4},... | collective-permute-start | bytes 1597448 | tf_op jit(solution)/shard_map/ppermute | solution.py:338
  23.6 1.7 %collective-permute-done.peer0 = bf16[1040,256]{1,0:T(8,128)(2,1)S(1)} collective-permute-done((bf16[1040,256]{1,0:T(8,128)(2,1)S(1)}, bf16[1040,256]{1,0:T(8,128)(2,1)S(1)}, u32[]{:S(2)}, u32[]{:S(2)}) %collective-permute-start) | collective-permute-done | bytes 532512 | tf_op jit(solution)/shard_map/ppermute | solution.py:338
  25.3 0.0 collective-permute-done.1.peer1.peer
  25.3 6.0 %all-to-all-done.queries = bf16[64,32,128]{2,1,0:T(8,128)(2,1)S(1)} async-done(((bf16[64,32,128]{2,1,0:T(8,128)(2,1)}), bf16[64,32,128]{2,1,0:T(8,128)(2,1)S(1)}, u32[]{:S(2)}, u32[]{:S(2)}) %all-to-all-start) | async-done | bytes 524320 | tf_op jit(solution)/shard_map/all_to_all | solution.py:321
  31.3 5.7 %attend.1 = bf16[32,72,128]{2,1,0:T(8,128)(2,1)S(1)} custom-call(s32[8]{0:T(128)S(1)} %copy-done.4, bf16[64,32,128]{2,1,0:T(8,128)(2,1)S(1)} %all-to-all-done.queries, bf16[2048,256]{1,0:T(8,128)(2,1)S(1)} %get-tuple-element.13.own, bf16[8,256]{1,0:T(8,128)(2,1)S(1)} %bitcast.3, f32[4,16,128]{2,1,0:T(8,128)S(1)} %get-tuple-element.17.mask, ...), custom_call_target="tpu_custom_call" | custom-call | tf_op jit(solution)/shard_map/attend/pallas_call | solution.py:341
  37.1 0.0 copy-start
  37.1 20.2 %all_to_all.20.got = bf16[32,72,128]{2,1,0:T(8,128)(2,1)S(1)} all-to-all(bf16[32,72,128]{2,1,0:T(8,128)(2,1)S(1)} %attend.1), channel_id=1, replica_groups=mesh['x'=4,'y'=8,'core'=2,'tp'=8] {'x','y'}, dimensions={0} | all-to-all | bytes 1179648 | tf_op jit(solution)/shard_map/all_to_all | solution.py:350
  57.2 0.8 combine.1
  58.0 23.8 %all_to_all.21.got = bf16[32,72,128]{2,1,0:T(8,128)(2,1)S(1)} all-to-all(bf16[32,72,128]{2,1,0:T(8,128)(2,1)S(1)} %combine.1), channel_id=1, replica_groups=mesh['x'=4,'y'=8,'core'=2,'tp'=8] {'x','y'}, dimensions={0} | all-to-all | bytes 1179648 | tf_op jit(solution)/shard_map/all_to_all | solution.py:359
  81.9 0.0 copy-done
  81.9 1.2 %project.1 = f32[16,4,8,128]{3,2,1,0:T(8,128)} custom-call(bf16[32,72,128]{2,1,0:T(8,128)(2,1)S(1)} %all_to_all.21.got, bf16[1024,128]{1,0:T(8,128)(2,1)S(1)} %copy-done, bf16[1536,256]{1,0:T(8,128)(2,1)S(1)} %collective-permute-done.1.peer1.peer), custom_call_target="tpu_custom_call" | custom-call | tf_op jit(solution)/shard_map/project/pallas_call | solution.py:361
  83.1 14.3 %all-to-all-start.3 = ((f32[16,4,8,128]{3,2,1,0:T(8,128)}), f32[16,4,8,128]{3,2,1,0:T(8,128)S(1)}, u32[]{:S(2)}, u32[]{:S(2)}) async-start(f32[16,4,8,128]{3,2,1,0:T(8,128)} %project.1), calls=%async_computation.3 | async-start | bytes 524288 | tf_op jit(solution)/shard_map/all_to_all | solution.py:374
  97.4 0.1 copy.14.spare
  97.5 0.0 copy-done.1
  97.5 1.7 %write.1 = (bf16[72,64,256]{2,1,0:T(8,128)(2,1)}, s32[8,8]{1,0:T(8,128)}) custom-call(s32[8,8]{1,0:T(8,128)S(1)} %copy-done.1, s32[8]{0:T(128)S(1)} %copy-done.4, s32[8]{0:T(128)S(1)} %copy-done.5, s32[8,1]{1,0:T(8,128)S(1)} %copy.14.spare, s32[8,8]{1,0:T(8,128)S(1)} %copy-done.1, ...), custom_call_target="tpu_custom_call", output_to_operand_aliasing={{0}: (6, {})} | custom-call | tf_op jit(solution)/shard_map/write/pallas_call | solution.py:384
  99.2 7.6 %all-to-all-done.3.got = f32[16,4,8,128]{3,2,1,0:T(8,128)S(1)} async-done(((f32[16,4,8,128]{3,2,1,0:T(8,128)}), f32[16,4,8,128]{3,2,1,0:T(8,128)S(1)}, u32[]{:S(2)}, u32[]{:S(2)}) %all-to-all-start.3) | async-done | bytes 262176 | tf_op jit(solution)/shard_map/all_to_all | solution.py:374
  106.8 0.6 sum.1
  (8 shorter events, 0.0 us)
Async XLA Ops:
  0.6 30.7 %copy-start.2 = (bf16[8,1,256]{2,0,1:T(8,128)(2,1)S(1)}, bf16[8,1,256]{2,0,1:T(8,128)(2,1)}, u32[]{:S(2)}) copy-start(bf16[8,1,256]{2,0,1:T(8,128)(2,1)} %param.11) | copy-start | bytes 12292
  0.6 30.7 %copy-start.4 = (s32[8]{0:T(128)S(1)}, s32[8]{0:T(128)}, u32[]{:S(2)}) copy-start(s32[8]{0:T(128)} %lengths.3) | copy-start | bytes 100
  2.2 29.1 %all-to-all-start = ((bf16[64,32,128]{2,1,0:T(8,128)(2,1)}), bf16[64,32,128]{2,1,0:T(8,128)(2,1)S(1)}, u32[]{:S(2)}, u32[]{:S(2)}) async-start(bf16[64,32,128]{2,1,0:T(8,128)(2,1)} %message.1), calls=%async_computation | async-start | bytes 1048576 | tf_op jit(solution)/shard_map/all_to_all | solution.py:321
  19.3 38.0 %copy-start.3 = (s32[8,8]{1,0:T(8,128)S(1)}, s32[8,8]{1,0:T(8,128)}, u32[]{:S(2)}) copy-start(s32[8,8]{1,0:T(8,128)} %path.1) | copy-start | bytes 772
  19.3 6.1 %collective-permute-start.1 = (bf16[1536,256]{1,0:T(8,128)(2,1)S(1)}, bf16[1536,256]{1,0:T(8,128)(2,1)S(1)}, u32[]{:S(2)}, u32[]{:S(2)}) collective-permute-start(bf16[1536,256]{1,0:T(8,128)(2,1)S(1)} %get-tuple-element.16), channel_id=1, source_target_pairs={{0,8},{8,0},{1,9},{9,1},{2,10},{10,2},{3,11},{11,3},{4,12},{12,4},... | collective-permute-start | bytes 2359304 | tf_op jit(solution)/shard_map/ppermute | solution.py:338
  21.5 3.8 %collective-permute-start = (bf16[1040,256]{1,0:T(8,128)(2,1)S(1)}, bf16[1040,256]{1,0:T(8,128)(2,1)S(1)}, u32[]{:S(2)}, u32[]{:S(2)}) collective-permute-start(bf16[1040,256]{1,0:T(8,128)(2,1)S(1)} %get-tuple-element.15), channel_id=1, source_target_pairs={{0,8},{8,0},{1,9},{9,1},{2,10},{10,2},{3,11},{11,3},{4,12},{12,4},... | collective-permute-start | bytes 1597448 | tf_op jit(solution)/shard_map/ppermute | solution.py:338
  37.1 44.8 %copy-start = (bf16[1024,128]{1,0:T(8,128)(2,1)S(1)}, bf16[1024,128]{1,0:T(8,128)(2,1)}, u32[]{:S(2)}) copy-start(bf16[1024,128]{1,0:T(8,128)(2,1)} %weight.3) | copy-start | bytes 786436
  57.2 40.2 %copy-start.6 = (s32[8,1]{0,1:T(1,128)S(1)}, s32[8,1]{0,1:T(1,128)}, u32[]{:S(2)}) copy-start(s32[8,1]{0,1:T(1,128)} %param.19) | copy-start | bytes 100
  57.2 40.3 %copy-start.1 = (s32[8,8]{1,0:T(8,128)S(1)}, s32[8,8]{1,0:T(8,128)}, u32[]{:S(2)}) copy-start(s32[8,8]{1,0:T(8,128)} %table_v.1) | copy-start | bytes 772
  57.2 40.3 %copy-start.5 = (s32[8]{0:T(128)S(1)}, s32[8]{0:T(128)}, u32[]{:S(2)}) copy-start(s32[8]{0:T(128)} %counts.1) | copy-start | bytes 100
  83.1 23.7 %all-to-all-start.3 = ((f32[16,4,8,128]{3,2,1,0:T(8,128)}), f32[16,4,8,128]{3,2,1,0:T(8,128)S(1)}, u32[]{:S(2)}, u32[]{:S(2)}) async-start(f32[16,4,8,128]{3,2,1,0:T(8,128)} %project.1), calls=%async_computation.3 | async-start | bytes 524288 | tf_op jit(solution)/shard_map/all_to_all | solution.py:374

commit v8 on v6

--- a/solution.py
+++ b/solution.py
@@ -63,7 +63,7 @@
             message[2 * chip + half] = rows
 
 
-def prepare_kernel(table, pool, node, parents, weight, send0, send1, own, pool_copy, mask, held, sems):
+def prepare_kernel(table, pool, node, parents, weight, send0, send1, own, pool_copy, mask, order, turned, held, sems):
     core, ctx = position()
     copies = []
     sends = (send0, send1)
@@ -112,15 +112,20 @@
         )
         seen = dot(pick.astype(F32).astype(BF16), reach[r]).astype(BF16)
         mask[r] = dot(seen, twice)
+    lane = iota((LANES, LANES), 1)
+    order[...] = (iota((LANES, LANES), 0) == (lane % NODES) * 8 + lane // NODES).astype(F32).astype(BF16)
     for c in copies:
         c.wait()
+    ones = jnp.ones((16, SPAN), BF16)
+    for r in range(HALF):
+        values = own[pl.ds(r * SPAN, SPAN), :][:, HEAD:].astype(F32).T.astype(BF16)
+        turned[r] = jnp.concatenate([values, ones], axis=0)
     store.wait()
 
 
-def attend_kernel(lengths, queries, own, node, mask, peer0, peer1, out):
+def attend_kernel(lengths, queries, own, node, mask, order_in, turned, peer0, peer1, out):
     core, ctx = position()
-    lane = iota((LANES, LANES), 1)
-    order = (iota((LANES, LANES), 0) == (lane % NODES) * 8 + lane // NODES).astype(F32).astype(BF16)
+    order = order_in[...]
     peers = (peer0, peer1)
     peer_node = peer0[pl.ds(NODE_ROWS0, 16), :].astype(F32)[:REQUESTS]
     own_node = node[...].astype(F32)
@@ -156,12 +161,12 @@
             ahead = scores(r + 1)
         total = None
         for s, v, one in (
-            (s_own, span_own[:, HEAD:], ones),
+            (s_own, None, turned[r]),
             (s_peer, span_peer[:, HEAD:], ones),
             (s_tree, nodes[:, HEAD:], ones_tree),
         ):
             p = jnp.exp2(s * SCALE2 - peak)
-            lhs = jnp.concatenate([v.astype(F32).T.astype(BF16), one], axis=0)
+            lhs = one if v is None else jnp.concatenate([v.astype(F32).T.astype(BF16), one], axis=0)
             high = p.astype(BF16)
             low = (p - high.astype(F32)).astype(BF16)
             add = dot(lhs, high) + dot(lhs, low)
@@ -318,16 +323,18 @@
     )(held_queries)
     every_query = lax.all_to_all(message, ("x", "y", "core"), 0, 0, tiled=True)
 
-    *sends, own, pool_copy, mask = pl.pallas_call(
+    *sends, own, pool_copy, mask, order, turned = pl.pallas_call(
         prepare_kernel,
         out_shape=(
             *(shape((NODE_ROWS0 + extra, 2 * HEAD), BF16) for extra in (16, W_ROWS)),
             shape((HALF * SPAN, 2 * HEAD), BF16),
             shape(pool.shape, pool.dtype),
             shape((HALF, 16, 2 * NODES), F32),
+            shape((LANES, LANES), BF16),
+            shape((HALF, HEAD + 16, SPAN), BF16),
         ),
         in_specs=[spec(SMEM), spec(HBM), spec(VMEM), spec(VMEM), spec(HBM)],
-        out_specs=(*([spec(VMEM)] * (SENDS + 1)), spec(HBM), spec(VMEM)),
+        out_specs=(*([spec(VMEM)] * (SENDS + 1)), spec(HBM), spec(VMEM), spec(VMEM), spec(VMEM)),
         scratch_shapes=[VMEM(pool.shape, BF16), pltpu.SemaphoreType.DMA((68,))],
         compiler_params=params,
         cost_estimate=pl.CostEstimate(flops=50_000_000, bytes_accessed=7_000_000, transcendentals=0),
@@ -339,11 +346,11 @@
     partial = pl.pallas_call(
         attend_kernel,
         out_shape=shape((CHIPS, BLOCK, HEAD), BF16),
-        in_specs=[spec(SMEM)] + [spec(VMEM)] * (4 + SENDS),
+        in_specs=[spec(SMEM)] + [spec(VMEM)] * (6 + SENDS),
         out_specs=spec(VMEM),
         compiler_params=params,
         name="attend",
-    )(lengths, every_query, own, node, mask, *peers)
+    )(lengths, every_query, own, node, mask, order, turned, *peers)
 
     parts = lax.all_to_all(partial, ("x", "y"), 0, 0, tiled=True)
     mixed = pl.pallas_call(

time: 108 us -> 110 us (1.019)
  local copies, waits for them, and re-layouts: 0.12 us -> 3.32 us
  waiting for transfers between devices: 15.3 us -> 13.9 us
    unnamed x15 -> x23, local copies, waits for them, and re-layouts: 0.12 us -> 3.32 us
    all_to_all x1, waiting for transfers between devices: 5.81 us -> 4.42 us  [on_device(): every_query = lax.all_to_all(message, ('x', 'y', 'core'), 0, 0, tiled=True)]
where the time goes in v8:
time: 110 us; the launch traced here: 109 us
  blocking collectives  43.2 us (39%)
  starting transfers between devices  31.2 us (28%)
  Pallas kernels  16.6 us (15%)
  waiting for transfers between devices  13.9 us (13%)
  local copies, waits for them, and re-layouts  3.32 us (3%)
    all_to_all x1, blocking collectives, on_device(): attention = lax.all_to_all(mixed, ('x', 'y'), 0, 0, tiled=True)  22.9 us
    all_to_all x1, blocking collectives, on_device(): parts = lax.all_to_all(partial, ('x', 'y'), 0, 0, tiled=True)  20.4 us
    all_to_all x1, starting transfers between devices, on_device(): shares = lax.all_to_all(sums, ('core', 'tp'), 0, 0, tiled=True)  15.3 us
    all_to_all x1, starting transfers between devices, on_device(): every_query = lax.all_to_all(message, ('x', 'y', 'core'), 0, 0, tiled=True)  11.6 us
    all_to_all x1, waiting for transfers between devices, on_device(): shares = lax.all_to_all(sums, ('core', 'tp'), 0, 0, tiled=True)  7.63 us
    pallas_call x1, Pallas kernels, on_device(): pl.pallas_call(attend_kernel, out_shape=shape((CHIPS, BLOCK, HEAD), BF16)...  5.38 us
    pallas_call x1, Pallas kernels, on_device(): pl.pallas_call(prepare_kernel, out_shape=(*(shape((NODE_ROWS0 + extra, 2...  5.31 us
    all_to_all x1, waiting for transfers between devices, on_device(): every_query = lax.all_to_all(message, ('x', 'y', 'core'), 0, 0, tiled=True)  4.42 us
  transfers between devices with their start and end apart: 4, of which 3 were waited for; matrix products, arithmetic and copies ran while one was open for 0% of the time, Pallas kernels for 6%

profile of v8, /device:TPU:1, one launch (start us, length us, event | category | flops | bytes accessed | tf_op | source)
XLA Modules:
  0.0 109.0 jit_solution(13297556107919504834)
XLA Ops:
  0.6 0.0 copy-start.6
  0.7 1.6 %message.1 = bf16[64,32,128]{2,1,0:T(8,128)(2,1)} custom-call(bf16[8,1024]{1,0:T(8,128)(2,1)} %bitcast.4), custom_call_target="tpu_custom_call" | custom-call | tf_op jit(solution)/shard_map/message/pallas_call | solution.py:316
  2.3 11.6 %all-to-all-start = ((bf16[64,32,128]{2,1,0:T(8,128)(2,1)}), bf16[64,32,128]{2,1,0:T(8,128)(2,1)S(1)}, u32[]{:S(2)}, u32[]{:S(2)}) async-start(bf16[64,32,128]{2,1,0:T(8,128)(2,1)} %message.1), calls=%async_computation | async-start | bytes 1048576 | tf_op jit(solution)/shard_map/all_to_all | solution.py:324
  13.9 5.3 %prepare.1 = (bf16[1040,256]{1,0:T(8,128)(2,1)S(1)}, bf16[1536,256]{1,0:T(8,128)(2,1)S(1)}, bf16[2048,256]{1,0:T(8,128)(2,1)S(1)}, bf16[72,64,256]{2,1,0:T(8,128...) custom-call(s32[8,8]{1,0:T(8,128)} %table_v.1, ...), custom_call_target="tpu_custom_call" | custom-call | flops 50000000 | bytes 7000000 | tf_op jit(solution)/shard_map/prepare/pallas_call | solution.py:326
  19.2 0.8 copy-done.1
  20.0 0.6 copy-done.4
  20.6 2.3 %collective-permute-start.1 = (bf16[1536,256]{1,0:T(8,128)(2,1)S(1)}, bf16[1536,256]{1,0:T(8,128)(2,1)S(1)}, u32[]{:S(2)}, u32[]{:S(2)}) collective-permute-start(bf16[1536,256]{1,0:T(8,128)(2,1)S(1)} %get-tuple-element.18), channel_id=1, source_target_pairs={{0,8},{8,0},{1,9},{9,1},{2,10},{10,2},{3,11},{11,3},{4,12},{12,4},... | collective-permute-start | bytes 2359304 | tf_op jit(solution)/shard_map/ppermute | solution.py:343
  23.0 2.0 %collective-permute-start = (bf16[1040,256]{1,0:T(8,128)(2,1)S(1)}, bf16[1040,256]{1,0:T(8,128)(2,1)S(1)}, u32[]{:S(2)}, u32[]{:S(2)}) collective-permute-start(bf16[1040,256]{1,0:T(8,128)(2,1)S(1)} %get-tuple-element.17), channel_id=1, source_target_pairs={{0,8},{8,0},{1,9},{9,1},{2,10},{10,2},{3,11},{11,3},{4,12},{12,4},... | collective-permute-start | bytes 1597448 | tf_op jit(solution)/shard_map/ppermute | solution.py:343
  25.0 1.8 %collective-permute-done.peer0 = bf16[1040,256]{1,0:T(8,128)(2,1)S(1)} collective-permute-done((bf16[1040,256]{1,0:T(8,128)(2,1)S(1)}, bf16[1040,256]{1,0:T(8,128)(2,1)S(1)}, u32[]{:S(2)}, u32[]{:S(2)}) %collective-permute-start) | collective-permute-done | bytes 532512 | tf_op jit(solution)/shard_map/ppermute | solution.py:343
  26.8 0.0 collective-permute-done.1.peer1.peer
  26.8 4.4 %all-to-all-done.queries = bf16[64,32,128]{2,1,0:T(8,128)(2,1)S(1)} async-done(((bf16[64,32,128]{2,1,0:T(8,128)(2,1)}), bf16[64,32,128]{2,1,0:T(8,128)(2,1)S(1)}, u32[]{:S(2)}, u32[]{:S(2)}) %all-to-all-start) | async-done | bytes 524320 | tf_op jit(solution)/shard_map/all_to_all | solution.py:324
  31.2 1.0 copy-done.2
  32.3 0.8 copy-done.5
  33.0 5.4 %attend.1 = bf16[32,72,128]{2,1,0:T(8,128)(2,1)S(1)} custom-call(s32[8]{0:T(128)S(1)} %copy-done.8, bf16[64,32,128]{2,1,0:T(8,128)(2,1)S(1)} %all-to-all-done.queries, bf16[2048,256]{1,0:T(8,128)(2,1)S(1)} %get-tuple-element.15.own, bf16[8,256]{1,0:T(8,128)(2,1)S(1)} %bitcast.3, f32[4,16,128]{2,1,0:T(8,128)S(1)} %copy-done.5, ...), custom_call_target="tpu_custom_call" | custom-call | tf_op jit(solution)/shard_map/attend/pallas_call | solution.py:346
  38.4 0.0 copy-start
  38.4 20.4 %all_to_all.20.got = bf16[32,72,128]{2,1,0:T(8,128)(2,1)S(1)} all-to-all(bf16[32,72,128]{2,1,0:T(8,128)(2,1)S(1)} %attend.1), channel_id=1, replica_groups=mesh['x'=4,'y'=8,'core'=2,'tp'=8] {'x','y'}, dimensions={0} | all-to-all | bytes 1179648 | tf_op jit(solution)/shard_map/all_to_all | solution.py:355
  58.8 0.8 combine.1
  59.6 22.9 %all_to_all.21.got = bf16[32,72,128]{2,1,0:T(8,128)(2,1)S(1)} all-to-all(bf16[32,72,128]{2,1,0:T(8,128)(2,1)S(1)} %combine.1), channel_id=1, replica_groups=mesh['x'=4,'y'=8,'core'=2,'tp'=8] {'x','y'}, dimensions={0} | all-to-all | bytes 1179648 | tf_op jit(solution)/shard_map/all_to_all | solution.py:364
  82.5 1.2 %project.1 = f32[16,4,8,128]{3,2,1,0:T(8,128)} custom-call(bf16[32,72,128]{2,1,0:T(8,128)(2,1)S(1)} %all_to_all.21.got, bf16[1024,128]{1,0:T(8,128)(2,1)S(1)} %copy-done, bf16[1536,256]{1,0:T(8,128)(2,1)S(1)} %collective-permute-done.1.peer1.peer), custom_call_target="tpu_custom_call" | custom-call | tf_op jit(solution)/shard_map/project/pallas_call | solution.py:366
  83.7 15.3 %all-to-all-start.3 = ((f32[16,4,8,128]{3,2,1,0:T(8,128)}), f32[16,4,8,128]{3,2,1,0:T(8,128)S(1)}, u32[]{:S(2)}, u32[]{:S(2)}) async-start(f32[16,4,8,128]{3,2,1,0:T(8,128)} %project.1), calls=%async_computation.3 | async-start | bytes 524288 | tf_op jit(solution)/shard_map/all_to_all | solution.py:379
  99.0 0.1 copy.14.spare
  99.0 1.7 %write.1 = (bf16[72,64,256]{2,1,0:T(8,128)(2,1)}, s32[8,8]{1,0:T(8,128)}) custom-call(s32[8,8]{1,0:T(8,128)S(1)} %copy-done.3, s32[8]{0:T(128)S(1)} %copy-done.8, s32[8]{0:T(128)S(1)} %copy-done.9, s32[8,1]{1,0:T(8,128)S(1)} %copy.14.spare, s32[8,8]{1,0:T(8,128)S(1)} %copy-done.3, ...), custom_call_target="tpu_custom_call", output_to_operand_aliasing={{0}: (6, {})} | custom-call | tf_op jit(solution)/shard_map/write/pallas_call | solution.py:389
  100.7 7.6 %all-to-all-done.3.got = f32[16,4,8,128]{3,2,1,0:T(8,128)S(1)} async-done(((f32[16,4,8,128]{3,2,1,0:T(8,128)}), f32[16,4,8,128]{3,2,1,0:T(8,128)S(1)}, u32[]{:S(2)}, u32[]{:S(2)}) %all-to-all-start.3) | async-done | bytes 262176 | tf_op jit(solution)/shard_map/all_to_all | solution.py:379
  108.3 0.6 sum.1
  (16 shorter events, 0.0 us)
Async XLA Ops:
  0.6 30.6 %copy-start.6 = (bf16[8,1,256]{2,0,1:T(8,128)(2,1)S(1)}, bf16[8,1,256]{2,0,1:T(8,128)(2,1)}, u32[]{:S(2)}) copy-start(bf16[8,1,256]{2,0,1:T(8,128)(2,1)} %param.11) | copy-start | bytes 12292
  0.6 30.6 %copy-start.8 = (s32[8]{0:T(128)S(1)}, s32[8]{0:T(128)}, u32[]{:S(2)}) copy-start(s32[8]{0:T(128)} %lengths.3) | copy-start | bytes 100
  2.3 29.0 %all-to-all-start = ((bf16[64,32,128]{2,1,0:T(8,128)(2,1)}), bf16[64,32,128]{2,1,0:T(8,128)(2,1)S(1)}, u32[]{:S(2)}, u32[]{:S(2)}) async-start(bf16[64,32,128]{2,1,0:T(8,128)(2,1)} %message.1), calls=%async_computation | async-start | bytes 1048576 | tf_op jit(solution)/shard_map/all_to_all | solution.py:324
  19.2 0.8 copy-start.1
  20.0 0.6 copy-start.4
  20.6 6.2 %collective-permute-start.1 = (bf16[1536,256]{1,0:T(8,128)(2,1)S(1)}, bf16[1536,256]{1,0:T(8,128)(2,1)S(1)}, u32[]{:S(2)}, u32[]{:S(2)}) collective-permute-start(bf16[1536,256]{1,0:T(8,128)(2,1)S(1)} %get-tuple-element.18), channel_id=1, source_target_pairs={{0,8},{8,0},{1,9},{9,1},{2,10},{10,2},{3,11},{11,3},{4,12},{12,4},... | collective-permute-start | bytes 2359304 | tf_op jit(solution)/shard_map/ppermute | solution.py:343
  23.0 3.8 %collective-permute-start = (bf16[1040,256]{1,0:T(8,128)(2,1)S(1)}, bf16[1040,256]{1,0:T(8,128)(2,1)S(1)}, u32[]{:S(2)}, u32[]{:S(2)}) collective-permute-start(bf16[1040,256]{1,0:T(8,128)(2,1)S(1)} %get-tuple-element.17), channel_id=1, source_target_pairs={{0,8},{8,0},{1,9},{9,1},{2,10},{10,2},{3,11},{11,3},{4,12},{12,4},... | collective-permute-start | bytes 1597448 | tf_op jit(solution)/shard_map/ppermute | solution.py:343
  31.2 1.0 copy-start.2
  32.3 0.8 copy-start.5
  33.0 25.8 %copy-start.7 = (s32[8,8]{1,0:T(8,128)S(1)}, s32[8,8]{1,0:T(8,128)}, u32[]{:S(2)}) copy-start(s32[8,8]{1,0:T(8,128)} %path.1) | copy-start | bytes 772
  38.4 44.1 %copy-start = (bf16[1024,128]{1,0:T(8,128)(2,1)S(1)}, bf16[1024,128]{1,0:T(8,128)(2,1)}, u32[]{:S(2)}) copy-start(bf16[1024,128]{1,0:T(8,128)(2,1)} %weight.3) | copy-start | bytes 786436
  58.8 40.2 %copy-start.10 = (s32[8,1]{0,1:T(1,128)S(1)}, s32[8,1]{0,1:T(1,128)}, u32[]{:S(2)}) copy-start(s32[8,1]{0,1:T(1,128)} %param.19) | copy-start | bytes 100
  58.8 40.3 %copy-start.3 = (s32[8,8]{1,0:T(8,128)S(1)}, s32[8,8]{1,0:T(8,128)}, u32[]{:S(2)}) copy-start(s32[8,8]{1,0:T(8,128)} %table_v.1) | copy-start | bytes 772
  58.8 40.3 %copy-start.9 = (s32[8]{0:T(128)S(1)}, s32[8]{0:T(128)}, u32[]{:S(2)}) copy-start(s32[8]{0:T(128)} %counts.1) | copy-start | bytes 100
  83.7 24.7 %all-to-all-start.3 = ((f32[16,4,8,128]{3,2,1,0:T(8,128)}), f32[16,4,8,128]{3,2,1,0:T(8,128)S(1)}, u32[]{:S(2)}, u32[]{:S(2)}) async-start(f32[16,4,8,128]{3,2,1,0:T(8,128)} %project.1), calls=%async_computation.3 | async-start | bytes 524288 | tf_op jit(solution)/shard_map/all_to_all | solution.py:379
